TPU v7x, 32 devices: a whole 2x2x4 slice. The times are simulated.
32 devices in a mesh: dp: 8 (over z, x), tensor: 4 (over y, core).
Axes of the slice: x: 2, y: 2, z: 4, core: 2. Of those that a mesh axis runs over, the one named last changes fastest.
Arguments:
- tokens: bfloat16 [5120, 2048], P('dp'), may hold values from -6 to 6
- cotangent: bfloat16 [5120, 2048], P('dp'), may hold values from -6 to 6
- gain_attn: bfloat16 [2048], replicated, may hold values from 0.099609375 to 1.8984375
- gain_mlp: bfloat16 [2048], replicated, may hold values from 0.099609375 to 1.8984375
- w_query: bfloat16 [2048, 2048], P(None, 'tensor'), may hold values from -0.125 to 0.125
- w_kv: bfloat16 [2048, 2, 512], P(None, None, 'tensor'), may hold values from -0.125 to 0.125
- w_out: bfloat16 [2048, 2048], P('tensor'), may hold values from -1 to 1
- w_gate_up: bfloat16 [2048, 2, 8192], P(None, None, 'tensor'), may hold values from -0.125 to 0.125
- w_down: bfloat16 [8192, 2048], P('tensor'), may hold values from -0.0625 to 0.0625
- a_attn: bfloat16 [2048, 3, 4, 16], replicated, may hold values from -0.125 to 0.125
- b_query: bfloat16 [4, 16, 2048], P(None, None, 'tensor'), may hold values from -0.75 to 0.75
- b_kv: bfloat16 [4, 16, 2, 512], P(None, None, None, 'tensor'), may hold values from -0.75 to 0.75
- a_out: bfloat16 [2048, 4, 16], P('tensor'), may hold values from -1 to 1
- b_out: bfloat16 [4, 16, 2048], replicated, may hold values from -0.75 to 0.75
- a_mlp: bfloat16 [2048, 2, 4, 16], replicated, may hold values from -0.125 to 0.125
- b_mlp: bfloat16 [4, 16, 2, 8192], P(None, None, None, 'tensor'), may hold values from -0.75 to 0.75
- a_down: bfloat16 [8192, 4, 16], P('tensor'), may hold values from -0.125 to 0.125
- b_down: bfloat16 [4, 16, 2048], replicated, may hold values from -0.75 to 0.75
- prompt_adapter: int32 [8], P('dp'), may hold values from 0 to 3
- cont_adapter: int32 [16], P('dp'), may hold values from 0 to 3
- group_map: int32 [16], replicated, may hold values from 0 to 7, as said below
Outputs:
- output: bfloat16 [5120, 2048], P('dp')
- tokens_grad: bfloat16 [5120, 2048], P('dp')
- grad_a_attn: float32 [2048, 3, 4, 16], replicated
- grad_b_query: float32 [4, 16, 2048], P(None, None, 'tensor')
- grad_b_kv: float32 [4, 16, 2, 512], P(None, None, None, 'tensor')
- grad_a_out: float32 [2048, 4, 16], P('tensor')
- grad_b_out: float32 [4, 16, 2048], replicated
- grad_a_mlp: float32 [2048, 2, 4, 16], replicated
- grad_b_mlp: float32 [4, 16, 2, 8192], P(None, None, None, 'tensor')
- grad_a_down: float32 [8192, 4, 16], P('tensor')
- grad_b_down: float32 [4, 16, 2048], replicated
Inputs may be any that keep to these rules, and one draw needn't show every extreme that they name: `group_map`: every prompt is named by exactly 2 continuations.
All inputs are finite; a program needn't handle non-finite values.
Results may differ from a plain program's by a relative error of at most 0.02.
Values may be sent and summed in bfloat16 or wider, within the bound.
A program may use at most 256 MiB of HBM per device.

v0:
```python
import math

import jax
import jax.numpy as jnp
from jax import lax
from jax.sharding import PartitionSpec as P

HD = 64
R = 16
NA = 4
PLEN = 384
CLEN = 128
CONT_DEV = 2


PRECISE = lax.Precision.HIGHEST
EPSILON = 1e-05
ROPE_BASE = 500000.0
MASKED_SCORE = -1e30


def plain_dot(left, right, precision=None):
    return jnp.dot(left, right, precision=precision, preferred_element_type=jnp.float32)


def rows_dot(left, right, precision=None):
    return lax.dot_general(
        left,
        right,
        (((0,), (0,)), ((), ())),
        precision=precision,
        preferred_element_type=jnp.float32,
    )


def cols_dot(left, right, precision=None):
    return lax.dot_general(
        left,
        right,
        (((1,), (1,)), ((), ())),
        precision=precision,
        preferred_element_type=jnp.float32,
    )


def rotate(value, cosine, sine):
    half = value.shape[-1] // 2
    first = value[..., :half]
    second = value[..., half:]
    return jnp.concatenate(
        [first * cosine - second * sine, second * cosine + first * sine], axis=-1
    )


def layout_rows():
    segment = jnp.concatenate(
        [jnp.zeros((PLEN,), jnp.int32), 1 + jnp.arange(CONT_DEV * CLEN, dtype=jnp.int32) // CLEN]
    )
    position = jnp.concatenate(
        [
            jnp.arange(PLEN, dtype=jnp.int32),
            PLEN + jnp.arange(CONT_DEV * CLEN, dtype=jnp.int32) % CLEN,
        ]
    )
    return (segment, position)


def rope_tables(position):
    exponent = jnp.arange(HD // 2, dtype=jnp.float32) * (2.0 / HD)
    frequency = jnp.exp(-math.log(ROPE_BASE) * exponent)
    angle = position.astype(jnp.float32)[:, None] * frequency[None, :]
    return (jnp.cos(angle)[:, None, :], jnp.sin(angle)[:, None, :])


def allowed_keys(segment):
    row_index = jnp.arange(segment.shape[0], dtype=jnp.int32)
    inside = (segment[:, None] == segment[None, :]) & (row_index[None, :] <= row_index[:, None])
    remote = segment[:, None] == (1 + jnp.arange(CONT_DEV, dtype=jnp.int32))[None, :]
    return jnp.concatenate([inside, jnp.repeat(remote, PLEN, axis=1)], axis=1)


def selection(prompt_ids, cont_ids, segment):
    table = jnp.concatenate([prompt_ids, cont_ids])
    member = (segment[:, None] == jnp.arange(1 + CONT_DEV, dtype=jnp.int32)[None, :]).astype(
        jnp.int32
    )
    adapter_ids = jnp.sum(member * table[None, :], axis=1)
    onehot = (adapter_ids[:, None] == jnp.arange(NA, dtype=jnp.int32)[None, :]).astype(jnp.float32)
    return jnp.repeat(onehot, R, axis=1)


def norm_forward(value, gain):
    inverse = lax.rsqrt(jnp.mean(value * value, axis=-1, keepdims=True) + EPSILON)
    return (value * inverse * gain, inverse)


def norm_backward(value, inverse, gain, upstream):
    scaled = value * inverse
    weighted = upstream * gain
    return inverse * (weighted - scaled * jnp.mean(weighted * scaled, axis=-1, keepdims=True))


def shards(
    tokens,
    cotangent,
    gain_attn,
    gain_mlp,
    w_query,
    w_kv,
    w_out,
    w_gate_up,
    w_down,
    a_attn,
    b_query,
    b_kv,
    a_out,
    b_out,
    a_mlp,
    b_mlp,
    a_down,
    b_down,
    prompt_adapter,
    cont_adapter,
    group_map,
):
    rows_here = tokens.shape[0]
    width = tokens.shape[1]
    ranked = NA * R
    heads_here = w_query.shape[1] // HD
    groups_here = w_kv.shape[2] // HD
    per_group = heads_here // groups_here
    kv_width = groups_here * HD
    hidden_here = w_down.shape[0]
    scale = 1.0 / math.sqrt(HD)
    prompts = lax.axis_size("dp")
    device_index = lax.axis_index("dp")
    partners = lax.dynamic_slice_in_dim(group_map, device_index * CONT_DEV, CONT_DEV)
    segment, position = layout_rows()
    cosine, sine = rope_tables(position)
    allowed = allowed_keys(segment)
    select = selection(prompt_adapter, cont_adapter, segment)
    select_two = jnp.tile(select, (1, 2))
    select_three = jnp.tile(select, (1, 3))
    gain_one = gain_attn.astype(jnp.float32)
    gain_two = gain_mlp.astype(jnp.float32)
    a_attn_flat = a_attn.reshape(width, 3 * ranked)
    b_query_flat = b_query.reshape(ranked, heads_here * HD)
    b_kv_flat = b_kv.reshape(ranked, 2 * kv_width)
    w_kv_flat = w_kv.reshape(width, 2 * kv_width)
    a_out_flat = a_out.reshape(heads_here * HD, ranked)
    b_out_flat = b_out.reshape(ranked, width)
    a_mlp_flat = a_mlp.reshape(width, 2 * ranked)
    b_mlp_flat = b_mlp.reshape(ranked, 2 * hidden_here)
    w_gate_flat = w_gate_up.reshape(width, 2 * hidden_here)
    a_down_flat = a_down.reshape(hidden_here, ranked)
    b_down_flat = b_down.reshape(ranked, width)
    inputs = tokens.astype(jnp.float32)
    normed_wide, inverse_one = norm_forward(inputs, gain_one)
    normed_one = normed_wide.astype(jnp.bfloat16)
    adapter_qkv = (plain_dot(normed_one, a_attn_flat) * select_three).astype(jnp.bfloat16)
    query_pre = plain_dot(normed_one, w_query) + plain_dot(adapter_qkv[:, :ranked], b_query_flat)
    kv_pre = plain_dot(normed_one, w_kv_flat)
    key_pre = kv_pre[:, :kv_width] + plain_dot(
        adapter_qkv[:, ranked : 2 * ranked], b_kv_flat[:, :kv_width]
    )
    values = (
        kv_pre[:, kv_width:] + plain_dot(adapter_qkv[:, 2 * ranked :], b_kv_flat[:, kv_width:])
    ).astype(jnp.bfloat16)
    queries = rotate(query_pre.reshape(rows_here, heads_here, HD), cosine, sine).astype(
        jnp.bfloat16
    )
    keys = (
        rotate(key_pre.reshape(rows_here, groups_here, HD), cosine, sine)
        .astype(jnp.bfloat16)
        .reshape(rows_here, kv_width)
    )
    every_key, every_value = (
        lax.all_gather(keys[:PLEN], "dp", axis=0, tiled=True),
        lax.all_gather(values[:PLEN], "dp", axis=0, tiled=True),
    )
    far_keys = []
    far_values = []
    for column in range(CONT_DEV):
        start = partners[column] * PLEN
        far_keys.append(lax.dynamic_slice_in_dim(every_key, start, PLEN, 0))
        far_values.append(lax.dynamic_slice_in_dim(every_value, start, PLEN, 0))
    key_block = jnp.concatenate([keys] + far_keys, axis=0).reshape(-1, groups_here, HD)
    value_block = jnp.concatenate([values] + far_values, axis=0).reshape(-1, groups_here, HD)
    grouped_query = queries.reshape(rows_here, groups_here, per_group, HD)

    def masked_scores():
        raw = (
            jnp.einsum(
                "tkgd,skd->kgts", grouped_query, key_block, preferred_element_type=jnp.float32
            )
            * scale
        )
        return jnp.where(allowed[None, None], raw, MASKED_SCORE)

    scores = masked_scores()
    top = jnp.max(scores, axis=-1, keepdims=True)
    weight = jnp.exp(scores - top)
    total = jnp.sum(weight, axis=-1, keepdims=True)
    log_total = top + jnp.log(total)
    prob_low = (weight / total).astype(jnp.bfloat16)
    attended = jnp.einsum(
        "kgts,skd->tkgd", prob_low, value_block, preferred_element_type=jnp.float32
    )
    attended_low = attended.reshape(rows_here, heads_here * HD).astype(jnp.bfloat16)
    adapter_out = plain_dot(attended_low, a_out_flat) * select
    attn_part = plain_dot(attended_low, w_out) + plain_dot(
        adapter_out, b_out_flat.astype(jnp.float32), PRECISE
    )
    attn_total = lax.psum(attn_part, "tensor")
    resid = inputs + attn_total
    normed_wide_two, inverse_two = norm_forward(resid, gain_two)
    normed_two = normed_wide_two.astype(jnp.bfloat16)
    adapter_mlp = (plain_dot(normed_two, a_mlp_flat) * select_two).astype(jnp.bfloat16)
    gate_up = plain_dot(normed_two, w_gate_flat)
    gate = gate_up[:, :hidden_here] + plain_dot(
        adapter_mlp[:, :ranked], b_mlp_flat[:, :hidden_here]
    )
    upper = gate_up[:, hidden_here:] + plain_dot(
        adapter_mlp[:, ranked:], b_mlp_flat[:, hidden_here:]
    )
    sigma = jax.nn.sigmoid(gate)
    silu_gate = gate * sigma
    activ_low = (silu_gate * upper).astype(jnp.bfloat16)
    adapter_down = plain_dot(activ_low, a_down_flat) * select
    mlp_part = plain_dot(activ_low, w_down) + plain_dot(
        adapter_down, b_down_flat.astype(jnp.float32), PRECISE
    )
    mlp_total = lax.psum(mlp_part.astype(jnp.bfloat16), "tensor").astype(jnp.float32)
    output = (resid + mlp_total).astype(jnp.bfloat16)
    upstream = cotangent.astype(jnp.float32)
    grad_b_down = rows_dot(adapter_down, upstream, PRECISE)
    down_grad_low = (cols_dot(cotangent, b_down_flat) * select).astype(jnp.bfloat16)
    grad_a_down = rows_dot(activ_low, down_grad_low)
    activ_grad = cols_dot(cotangent, w_down) + cols_dot(down_grad_low, a_down_flat)
    gate_grad = activ_grad * upper * sigma * (1.0 + gate * (1.0 - sigma))
    upper_grad = activ_grad * silu_gate
    gate_up_low = jnp.concatenate([gate_grad, upper_grad], axis=1).astype(jnp.bfloat16)
    grad_b_mlp = jnp.concatenate(
        [
            rows_dot(adapter_mlp[:, :ranked], gate_up_low[:, :hidden_here]),
            rows_dot(adapter_mlp[:, ranked:], gate_up_low[:, hidden_here:]),
        ],
        axis=1,
    )
    mlp_adapter_grad = (
        jnp.concatenate(
            [
                cols_dot(gate_up_low[:, :hidden_here], b_mlp_flat[:, :hidden_here]),
                cols_dot(gate_up_low[:, hidden_here:], b_mlp_flat[:, hidden_here:]),
            ],
            axis=1,
        )
        * select_two
    )
    grad_a_mlp = rows_dot(normed_two.astype(jnp.float32), mlp_adapter_grad, PRECISE)
    normed_two_part = cols_dot(gate_up_low, w_gate_flat) + cols_dot(
        mlp_adapter_grad, a_mlp_flat.astype(jnp.float32), PRECISE
    )
    normed_two_grad = lax.psum(normed_two_part.astype(jnp.bfloat16), "tensor").astype(jnp.float32)
    resid_grad = upstream + norm_backward(resid, inverse_two, gain_two, normed_two_grad)
    attn_grad_low = resid_grad.astype(jnp.bfloat16)
    grad_b_out = rows_dot(adapter_out, attn_grad_low.astype(jnp.float32), PRECISE)
    out_grad_low = (cols_dot(attn_grad_low, b_out_flat) * select).astype(jnp.bfloat16)
    grad_a_out = rows_dot(attended_low, out_grad_low)
    attended_grad = (cols_dot(attn_grad_low, w_out) + cols_dot(out_grad_low, a_out_flat)).astype(
        jnp.bfloat16
    )
    grouped_grad = attended_grad.reshape(rows_here, groups_here, per_group, HD)
    probs = jnp.exp(masked_scores() - log_total)
    prob_grad = jnp.einsum(
        "tkgd,skd->kgts", grouped_grad, value_block, preferred_element_type=jnp.float32
    )
    inner = jnp.sum(probs * prob_grad, axis=-1, keepdims=True)
    score_grad = (probs * (prob_grad - inner)).astype(jnp.bfloat16)
    query_grad = (
        jnp.einsum("kgts,skd->tkgd", score_grad, key_block, preferred_element_type=jnp.float32)
        * scale
    )
    key_grad_all = (
        jnp.einsum("kgts,tkgd->skd", score_grad, grouped_query, preferred_element_type=jnp.float32)
        * scale
    ).reshape(-1, kv_width)
    value_grad_all = jnp.einsum(
        "kgts,tkgd->skd",
        probs.astype(jnp.bfloat16),
        grouped_grad,
        preferred_element_type=jnp.float32,
    ).reshape(-1, kv_width)
    far_key_grad = key_grad_all[rows_here:]
    far_value_grad = value_grad_all[rows_here:]
    buffer_key = jnp.zeros((prompts * PLEN, kv_width), jnp.float32)
    buffer_value = jnp.zeros((prompts * PLEN, kv_width), jnp.float32)
    for column in range(CONT_DEV):
        start = partners[column] * PLEN
        piece_key = far_key_grad[column * PLEN : (column + 1) * PLEN]
        piece_value = far_value_grad[column * PLEN : (column + 1) * PLEN]
        buffer_key = lax.dynamic_update_slice_in_dim(
            buffer_key, lax.dynamic_slice_in_dim(buffer_key, start, PLEN, 0) + piece_key, start, 0
        )
        buffer_value = lax.dynamic_update_slice_in_dim(
            buffer_value,
            lax.dynamic_slice_in_dim(buffer_value, start, PLEN, 0) + piece_value,
            start,
            0,
        )
    own_key, own_value = (
        lax.psum_scatter(
            buffer_key.astype(jnp.bfloat16), "dp", scatter_dimension=0, tiled=True
        ).astype(jnp.float32),
        lax.psum_scatter(
            buffer_value.astype(jnp.bfloat16), "dp", scatter_dimension=0, tiled=True
        ).astype(jnp.float32),
    )
    local_key = key_grad_all[:rows_here]
    local_value = value_grad_all[:rows_here]
    key_total = jnp.concatenate([local_key[:PLEN] + own_key, local_key[PLEN:]], axis=0)
    value_total = jnp.concatenate([local_value[:PLEN] + own_value, local_value[PLEN:]], axis=0)
    value_grad_low = value_total.astype(jnp.bfloat16)
    key_rot_low = key_total.astype(jnp.bfloat16).astype(jnp.float32)
    query_rot_low = (
        query_grad.reshape(rows_here, heads_here, HD).astype(jnp.bfloat16).astype(jnp.float32)
    )
    query_pre_grad = (
        rotate(query_rot_low, cosine, -sine)
        .reshape(rows_here, heads_here * HD)
        .astype(jnp.bfloat16)
    )
    key_pre_grad = (
        rotate(key_rot_low.reshape(rows_here, groups_here, HD), cosine, -sine)
        .reshape(rows_here, kv_width)
        .astype(jnp.bfloat16)
    )
    grad_b_query = rows_dot(adapter_qkv[:, :ranked], query_pre_grad)
    grad_b_kv = jnp.concatenate(
        [
            rows_dot(adapter_qkv[:, ranked : 2 * ranked], key_pre_grad),
            rows_dot(adapter_qkv[:, 2 * ranked :], value_grad_low),
        ],
        axis=1,
    )
    kv_grad_low = jnp.concatenate([key_pre_grad, value_grad_low], axis=1)
    qkv_adapter_grad = (
        jnp.concatenate(
            [
                cols_dot(query_pre_grad, b_query_flat),
                cols_dot(key_pre_grad, b_kv_flat[:, :kv_width]),
                cols_dot(value_grad_low, b_kv_flat[:, kv_width:]),
            ],
            axis=1,
        )
        * select_three
    )
    grad_a_attn = rows_dot(normed_one.astype(jnp.float32), qkv_adapter_grad, PRECISE)
    normed_one_part = (
        cols_dot(query_pre_grad, w_query)
        + cols_dot(kv_grad_low, w_kv_flat)
        + cols_dot(qkv_adapter_grad, a_attn_flat.astype(jnp.float32), PRECISE)
    )
    normed_one_grad = lax.psum(normed_one_part.astype(jnp.bfloat16), "tensor").astype(jnp.float32)
    tokens_grad = (
        resid_grad + norm_backward(inputs, inverse_one, gain_one, normed_one_grad)
    ).astype(jnp.bfloat16)
    grad_b_query, grad_b_kv, grad_a_out, grad_b_mlp, grad_a_down = (
        lax.psum(grad_b_query.astype(jnp.bfloat16), "dp").astype(jnp.float32),
        lax.psum(grad_b_kv.astype(jnp.bfloat16), "dp").astype(jnp.float32),
        lax.psum(grad_a_out.astype(jnp.bfloat16), "dp").astype(jnp.float32),
        lax.psum(grad_b_mlp.astype(jnp.bfloat16), "dp").astype(jnp.float32),
        lax.psum(grad_a_down.astype(jnp.bfloat16), "dp").astype(jnp.float32),
    )
    grad_a_attn, grad_b_out, grad_a_mlp, grad_b_down = lax.psum(
        (grad_a_attn, grad_b_out, grad_a_mlp, grad_b_down), ("dp", "tensor")
    )
    return (
        output,
        tokens_grad,
        grad_a_attn.reshape(a_attn.shape),
        grad_b_query.reshape(b_query.shape),
        grad_b_kv.reshape(b_kv.shape),
        grad_a_out.reshape(a_out.shape),
        grad_b_out.reshape(b_out.shape),
        grad_a_mlp.reshape(a_mlp.shape),
        grad_b_mlp.reshape(b_mlp.shape),
        grad_a_down.reshape(a_down.shape),
        grad_b_down.reshape(b_down.shape),
    )


def solution(mesh):
    in_specs = (
        P("dp", None),
        P("dp", None),
        P(),
        P(),
        P(None, "tensor"),
        P(None, None, "tensor"),
        P("tensor", None),
        P(None, None, "tensor"),
        P("tensor", None),
        P(),
        P(None, None, "tensor"),
        P(None, None, None, "tensor"),
        P("tensor", None, None),
        P(),
        P(),
        P(None, None, None, "tensor"),
        P("tensor", None, None),
        P(),
        P("dp"),
        P("dp"),
        P(),
    )
    out_specs = (
        P("dp", None),
        P("dp", None),
        P(),
        P(None, None, "tensor"),
        P(None, None, None, "tensor"),
        P("tensor", None, None),
        P(),
        P(),
        P(None, None, None, "tensor"),
        P("tensor", None, None),
        P(),
    )
    return jax.shard_map(shards, mesh=mesh, in_specs=in_specs, out_specs=out_specs, check_vma=False)
```

profile of v0, /device:TPU:0, one launch (start us, length us, event | category | flops | bytes accessed | tf_op | source)
XLA Modules:
  0.0 926.6 jit_solution(14628238637599683854)
XLA Ops:
  12.2 2.5 fusion.18
  16.2 3.2 fusion.43
  21.2 33.9 %all_gather.6 = bf16[3072,128]{0,1:T(8,128)(2,1)S(1)} all-gather(bf16[384,128]{0,1:T(8,128)(2,1)S(1)} %slice.207), channel_id=1, replica_groups=mesh['dp'=8,'tensor'=4] {'dp'}, dimensions={0}, use_global_device_ids=true | all-gather | bytes 884736 | tf_op jit(solution)/shard_map/all_gather | solution.py:179
  57.5 34.0 %all_gather.7 = bf16[3072,128]{0,1:T(8,128)(2,1)} all-gather(bf16[384,128]{0,1:T(8,128)(2,1)S(1)} %bitcast.259), channel_id=1, replica_groups=mesh['dp'=8,'tensor'=4] {'dp'}, dimensions={0}, use_global_device_ids=true | all-gather | bytes 884736 | tf_op jit(solution)/shard_map/all_gather | solution.py:178
  92.6 4.4 fusion.96
  97.1 1.3 convolution_add_fusion.3
  99.2 12.5 %fusion.103 = (f32[2,4,640]{2,1,0:T(4,128)S(1)}, f32[2,4,640,1408]{2,3,1,0:T(8,128)}) fusion(bf16[640,2,4,32]{0,3,2,1:T(8,128)(2,1)S(1)} %bitcast.235, bf16[640,2,4,32]{0,3,2,1:T(8,128)(2,1)S(1)} %bitcast.233, bf16[384,2,64]{0,2,1:T(8,128)(2,1)S(1)} %bitcast.257, bf16[384,2,64]{0,2,1:T(8,128)(2,1)S(1)} %bitcast.255, ...), kind=kOutput, calls=%fused_computation.199 | convolution fusion | flops 947121152 | bytes 30773248 | tf_op jit(solution)/shard_map/tkgd,skd->kgts/dot_general | solution.py:193
  111.7 11.7 %fusion.3 = f32[2,4,640]{2,1,0:T(4,128)S(1)} fusion(f32[2,4,640,1408]{2,3,1,0:T(8,128)} %get-tuple-element.50, f32[2,4,640]{2,1,0:T(4,128)S(1)} %get-tuple-element.49), kind=kLoop, calls=%fused_computation.9 | loop fusion | flops 14412800 | bytes 28876800 | tf_op jit(solution)/shard_map/reduce_sum | solution.py:203
  123.4 11.9 %fusion.35 = bf16[2,64,4,640]{3,1,2,0:T(8,128)(2,1)S(1)} fusion(bf16[1408,2,64,1]{0,2,3,1:T(8,128)(2,1)S(1)} %bitcast.229, f32[2,4,640,1408]{2,3,1,0:T(8,128)} %get-tuple-element.50, f32[2,4,640]{2,1,0:T(4,128)S(1)} %fusion.3, f32[2,4,640]{2,1,0:T(4,128)S(1)} %get-tuple-element.49), kind=kOutput, calls=%fused_computation.66 | convolution fusion | flops 944701440 | bytes 29892608 | tf_op jit(solution)/shard_map/kgts,skd->tkgd/dot_general | solution.py:206
  136.1 1.6 fusion.104
  137.7 4.6 convolution_add_fusion
  143.3 2.8 fusion.39
  146.4 18.5 %copy.62 = bf16[256,8,2,2048]{3,1,2,0:T(8,128)(2,1)} copy(bf16[256,8,2,2048]{3,2,1,0:T(2,128)(2,1)} %bitcast.193) | data formatting | bytes 33554432
  165.5 5.6 fusion.107
  171.2 3.2 convolution_add_fusion.1
  174.3 72.6 %all-reduce.10.cloned.1.call-done = f32[640,2048]{1,0:T(8,128)} async-done(((f32[640,2048]{1,0:T(8,128)}), f32[640,2048]{1,0:T(8,128)}) %all-reduce.10.cloned.1.call-update) | async-done | bytes 5242896 | tf_op jit(solution)/shard_map/psum | solution.py:214
  246.9 4.2 multiply_reduce_fusion.1
  253.3 18.1 %fusion.105 = f32[640,4096]{1,0:T(8,128)} fusion(bf16[640,2048]{1,0:T(8,128)(2,1)S(1)} %multiply_convert_fusion.3, bf16[2048,4096]{1,0:T(8,128)(2,1)} %bitcast.194), kind=kOutput, calls=%fused_computation.201 | convolution fusion | flops 10737418240 | bytes 29884416 | tf_op jit(solution)/shard_map/dot_general | solution.py:23
  272.5 3.5 slice_add_fusion
  276.3 5.3 multiply_convert_fusion.1
  282.5 1.3 convolution_convert_fusion.2
  284.8 1.3 convolution_convert_fusion.1
  288.0 7.3 fusion.106
  295.3 4.6 fusion.108
  299.9 18.4 %add_convert_fusion.1 = bf16[640,2048]{1,0:T(8,128)(2,1)} fusion(f32[640,2048]{1,0:T(8,128)} %fusion.108, bf16[2048,4096]{1,0:T(8,128)(2,1)} %bitcast.195, bf16[640,2048]{1,0:T(8,128)(2,1)} %copy-done.13, bf16[640,2048]{1,0:T(8,128)(2,1)} %copy-done.12), kind=kOutput, calls=%fused_computation.38 | convolution fusion | flops 10750525440 | bytes 29884416 | tf_op jit(solution)/shard_map/dot_general | solution.py:37
  320.6 3.0 convolution_convert_fusion
  323.6 2.8 convolution_multiply_fusion.6
  326.5 6.4 add_convert_fusion.3
  332.9 45.6 %all-reduce.12.cloned.1.call-done = bf16[640,2048]{1,0:T(8,128)(2,1)} async-done(((bf16[640,2048]{1,0:T(8,128)(2,1)}), bf16[640,2048]{1,0:T(8,128)(2,1)}) %all-reduce.12.cloned.1.call-update) | async-done | bytes 2621456 | tf_op jit(solution)/shard_map/psum | solution.py:264
  378.6 5.5 multiply_reduce_fusion
  384.9 4.6 multiply_add_fusion
  390.5 1.8 fusion.92
  392.8 18.2 %fusion = (f32[2,4,640]{2,1,0:T(4,128)S(1)}, f32[2,1408,640,4]{2,1,3,0:T(8,128)}) fusion(f32[2,4,640,1408]{2,3,1,0:T(8,128)} %get-tuple-element.50, f32[2,4,640]{2,1,0:T(4,128)S(1)} %bitcast.261, bf16[1408,2,64,1]{0,2,3,1:T(8,128)(2,1)} %bitcast.230, bf16[640,2,4,64]{0,3,2,1:T(8,128)(2,1)S(1)} %bitcast.202), kind=kOutput, calls=%fused_computation.2 | convolution fusion | flops 944368640 | bytes 58728448 | tf_op jit(solution)/shard_map/tkgd,skd->kgts/dot_general | solution.py:275
  411.0 24.2 %fusion.2 = bf16[2,4,640,1408]{2,3,1,0:T(8,128)(2,1)} fusion(f32[2,1408,640,4]{2,1,3,0:T(8,128)} %get-tuple-element.52, f32[2,4,640,1408]{2,3,1,0:T(8,128)} %get-tuple-element.50, f32[2,4,640]{2,1,0:T(4,128)S(1)} %get-tuple-element.51, f32[2,4,640]{2,1,0:T(4,128)S(1)} %bitcast.262), kind=kLoop, calls=%fused_computation.4 | loop fusion | flops 28835840 | bytes 72130560 | tf_op jit(solution)/shard_map/convert_element_type | solution.py:279
  435.2 9.6 %fusion.30 = f32[1408,2,64]{0,2,1:T(8,128)S(1)} fusion(bf16[2,4,640,1408]{2,3,1,0:T(8,128)(2,1)} %fusion.2, bf16[640,2,4,32]{0,3,2,1:T(8,128)(2,1)S(1)} %bitcast.236, bf16[640,2,4,32]{0,3,2,1:T(8,128)(2,1)S(1)} %bitcast.234), kind=kOutput, calls=%fused_computation.54 | convolution fusion | flops 924237824 | bytes 15794176 | tf_op jit(solution)/shard_map/kgts,tkgd->skd/dot_general | solution.py:285
  446.8 2.3 copy.56
  449.2 12.6 %fusion.26 = f32[1408,2,64]{0,2,1:T(8,128)} fusion(bf16[640,2,4,64]{0,3,2,1:T(8,128)(2,1)S(1)} %bitcast.203, f32[2,4,640,1408]{2,3,1,0:T(8,128)} %get-tuple-element.50, f32[2,4,640]{2,1,0:T(4,128)S(1)} %bitcast.263), kind=kOutput, calls=%fused_computation.51 | convolution fusion | flops 937164800 | bytes 30232576 | tf_op jit(solution)/shard_map/kgts,tkgd->skd/dot_general | solution.py:288
  461.8 1.8 fusion.101
  465.2 8.1 fusion.33
  473.4 1.7 slice.294
  475.1 1.5 slice.295
  477.8 1.8 convolution_convert_fusion.4
  480.6 3.9 fusion.109
  484.6 27.3 %reduce-scatter.7.cloned.1.call-done = bf16[384,128]{1,0:T(8,128)(2,1)} async-done(((bf16[3072,128]{1,0:T(8,128)(2,1)}), bf16[384,128]{1,0:T(8,128)(2,1)}) %reduce-scatter.7.cloned.1.call-update) | async-done | bytes 98320
  514.7 62.6 %reduce-scatter.9.cloned.1.call-done = bf16[384,128]{1,0:T(8,128)(2,1)} async-done(((bf16[3072,128]{1,0:T(8,128)(2,1)}), bf16[384,128]{1,0:T(8,128)(2,1)}) %reduce-scatter.9.cloned.1.call-update) | async-done | bytes 98320
  581.3 2.6 fusion.41
  583.9 4.5 add_convert_fusion
  588.8 4.2 fusion.111
  593.0 2.4 fusion.110
  595.4 4.9 fusion.89
  600.3 57.7 %all-reduce.16.cloned.1.call-done = (bf16[4,16,512]{2,1,0:T(8,128)(2,1)}, bf16[512,4,16]{0,2,1:T(8,128)(2,1)}, bf16[4,16,2,2048]{3,2,1,0:T(2,128)(2,1)}, bf16[2048,4,16]{0,2,1:T(8,128)(2,1)}) async-done(((bf16[4,16,512]{2,1,0:T(8,128)(2,1)}, bf16[512,4,16]{0,2,1:T(8,128)(2,1)}, bf16[4,16,2,2048]{3,2,1,0:T(2,128)(2,1)}, bf16[2048,4,16]{0,2,1:T(8,128)(2,1)}), (bf16[4,16,512]{2,1,0:T(8,128)(2,1)}, ...) | async-done | bytes 917520 | tf_op jit(solution)/shard_map/psum | solution.py:369
  658.0 1.5 reshape.356
  659.5 1.5 reshape.360
  661.0 1.8 reshape.366
  662.8 2.6 reshape.364
  665.9 5.4 fusion.94
  671.4 35.7 %psum.97 = bf16[4,16,2,128]{3,2,1,0:T(2,128)(2,1)S(1)} all-reduce(bf16[4,16,2,128]{3,2,1,0:T(2,128)(2,1)S(1)} %reshape.357), channel_id=1, replica_groups=mesh['dp'=8,'tensor'=4] {'dp'}, use_global_device_ids=true, to_apply=%region_16.17 | all-reduce | flops 16384 | bytes 65536 | tf_op jit(solution)/shard_map/psum | solution.py:370
  707.7 55.6 %all-reduce.18.cloned.1.call-done = (bf16[640,2048]{1,0:T(8,128)(2,1)}, bf16[640,2048]{1,0:T(8,128)(2,1)}) async-done(((bf16[640,2048]{1,0:T(8,128)(2,1)}, bf16[640,2048]{1,0:T(8,128)(2,1)}), (bf16[640,2048]{1,0:T(8,128)(2,1)}, bf16[640,2048]{1,0:T(8,128)(2,1)})) %all-reduce.18.cloned.1.call-update) | async-done | bytes 5242896 | tf_op jit(solution)/shard_map/psum | solution.py:233
  763.3 3.8 fusion.13
  767.3 8.0 fusion.17
  775.3 136.3 %all-reduce.14.cloned.1.call-done = (f32[2048,3,4,16]{0,3,2,1:T(8,128)}, f32[4,16,2048]{2,1,0:T(8,128)}, f32[2048,2,4,16]{0,3,2,1:T(8,128)}, f32[4,16,2048]{2,1,0:T(8,128)}) async-done(((f32[2048,3,4,16]{0,3,2,1:T(8,128)}, f32[4,16,2048]{2,1,0:T(8,128)}, f32[2048,2,4,16]{0,3,2,1:T(8,128)}, f32[4,16,2048]{2,1,0:T(8,128)}), (f32[2048,3,4,16]{0,3,2,1:T(8,128)}, f32[4,16,2048]{2,1,0:T(8,128)}, ...) | async-done | bytes 3670032 | tf_op jit(solution)/shard_map/psum | solution.py:375
  911.6 2.8 copy.91
  914.4 1.9 copy.92
  916.3 2.3 copy.93
  (266 shorter events, 39.6 us)
Async XLA Ops:
  7.2 129.0 %copy-start = (bf16[512,2048]{1,0:T(8,128)(2,1)S(1)}, bf16[512,2048]{1,0:T(8,128)(2,1)}, u32[]{:S(2)}) copy-start(bf16[512,2048]{1,0:T(8,128)(2,1)} %param.27) | copy-start | bytes 6291460
  7.2 239.7 %all-reduce.10.cloned.1.call-start = ((), (), s32[]{:S(2)}) async-start(), calls=%async_computation.2 | async-start | bytes 10485760 | tf_op jit(solution)/shard_map/psum | solution.py:214
  12.2 7.2 copy-start.2
  12.2 7.2 copy-start.40
  14.7 77.8 %copy-start.72 = (f32[640]{0:T(1024)}, f32[640]{0:T(1024)S(1)}, u32[]{:S(2)}) copy-start(f32[640]{0:T(1024)S(1)} %add_rsqrt_fusion.1) | copy-start | bytes 7684
  15.4 77.1 %copy-start.70 = (f32[2048]{0:T(1024)}, f32[2048]{0:T(1024)S(1)}, u32[]{:S(2)}) copy-start(f32[2048]{0:T(1024)S(1)} %convert_element_type.177) | copy-start | bytes 24580
  16.2 4.7 copy-start.62
  19.4 35.8 %copy-start.75 = (f32[32]{0:T(128)S(1)}, f32[32]{0:T(128)}, u32[]{:S(2)}) copy-start(f32[32]{0:T(128)} %multiply_exponential_fusion) | copy-start | bytes 388
  20.6 36.9 %copy-start.54 = (bf16[640,192]{0,1:T(8,128)(2,1)}, bf16[640,192]{0,1:T(8,128)(2,1)S(1)}, u32[]{:S(2)}) copy-start(bf16[640,192]{0,1:T(8,128)(2,1)S(1)} %fusion.36) | copy-start | bytes 737284
  20.9 34.3 %copy-start.34 = (bf16[640,128]{0,1:T(8,128)(2,1)}, bf16[640,128]{0,1:T(8,128)(2,1)S(1)}, u32[]{:S(2)}) copy-start(bf16[640,128]{0,1:T(8,128)(2,1)S(1)} %fusion.37) | copy-start | bytes 491524
  56.2 42.2 %copy-start.21 = (f32[640,32]{0,1:T(8,128)}, f32[640,32]{0,1:T(8,128)S(1)}, u32[]{:S(2)}) copy-start(f32[640,32]{0,1:T(8,128)S(1)} %get-tuple-element.46) | copy-start | bytes 245764
  92.6 6.6 copy-start.59
  92.6 6.6 copy-start.60
  92.6 4.5 copy-start.66
  92.6 5.8 copy-start.47
  98.6 13.1 %copy-start.30 = (bf16[640,8,32]{0,2,1:T(8,128)(2,1)}, bf16[640,8,32]{0,2,1:T(8,128)(2,1)S(1)}, u32[]{:S(2)}) copy-start(bf16[640,8,32]{0,2,1:T(8,128)(2,1)S(1)} %get-tuple-element.28) | copy-start | bytes 983044
  98.6 13.0 %copy-start.32 = (bf16[640,8,32]{0,2,1:T(8,128)(2,1)}, bf16[640,8,32]{0,2,1:T(8,128)(2,1)S(1)}, u32[]{:S(2)}) copy-start(bf16[640,8,32]{0,2,1:T(8,128)(2,1)S(1)} %get-tuple-element.29) | copy-start | bytes 983044
  99.2 24.2 %copy-start.29 = (bf16[1408,128]{0,1:T(8,128)(2,1)}, bf16[1408,128]{0,1:T(8,128)(2,1)S(1)}, u32[]{:S(2)}) copy-start(bf16[1408,128]{0,1:T(8,128)(2,1)S(1)} %pad_maximum_fusion.4) | copy-start | bytes 1081348
  123.4 11.9 %copy-start.64 = (bf16[512,4,16]{0,2,1:T(8,128)(2,1)S(1)}, bf16[512,4,16]{0,2,1:T(8,128)(2,1)}, u32[]{:S(2)}) copy-start(bf16[512,4,16]{0,2,1:T(8,128)(2,1)} %param.33) | copy-start | bytes 196612
  142.4 236.2 %all-reduce.12.cloned.1.call-start = ((), (), s32[]{:S(2)}) async-start(), calls=%async_computation.3 | async-start | bytes 5242880 | tf_op jit(solution)/shard_map/psum | solution.py:264
  143.3 22.2 %slice-start.4 = ((s8[8388608]{0:T(1024)(128)(4,1)}), s8[4194304]{0:T(1024)(128)(4,1)S(1)}, s32[]{:S(2)}) async-start(s8[8388608]{0:T(1024)(128)(4,1)} %bitcast.277), calls=%async_computation.13 | async-start | bytes 8388608
  146.2 104.9 %copy-start.68 = (f32[2048]{0:T(1024)}, f32[2048]{0:T(1024)S(1)}, u32[]{:S(2)}) copy-start(f32[2048]{0:T(1024)S(1)} %convert_element_type.187) | copy-start | bytes 24580
  146.4 19.1 %copy-start.7 = (bf16[640,2048]{1,0:T(8,128)(2,1)S(1)}, bf16[640,2048]{1,0:T(8,128)(2,1)}, u32[]{:S(2)}) copy-start(bf16[640,2048]{1,0:T(8,128)(2,1)} %param.22) | copy-start | bytes 7864324
  146.4 19.1 %slice-start.5 = ((s8[8388608]{0:T(1024)(128)(4,1)}), s8[4194304]{0:T(1024)(128)(4,1)S(1)}, s32[]{:S(2)}) async-start(s8[8388608]{0:T(1024)(128)(4,1)} %bitcast.277), calls=%async_computation.14 | async-start | bytes 8388608
  165.5 5.6 copy-start.39
  246.9 4.8 copy-start.1
  246.9 5.6 copy-start.3
  253.3 18.2 %copy-start.9 = (bf16[640,2048]{1,0:T(8,128)(2,1)}, bf16[640,2048]{1,0:T(8,128)(2,1)S(1)}, u32[]{:S(2)}) copy-start(bf16[640,2048]{1,0:T(8,128)(2,1)S(1)} %multiply_convert_fusion.3) | copy-start | bytes 7864324
  253.3 18.2 %copy-start.20 = (bf16[2048,2,4,16]{0,3,2,1:T(8,128)(2,1)S(1)}, bf16[2048,2,4,16]{0,3,2,1:T(8,128)(2,1)}, u32[]{:S(2)}) copy-start(bf16[2048,2,4,16]{0,3,2,1:T(8,128)(2,1)} %param.35) | copy-start | bytes 1572868
  271.5 4.5 slice-start.2
  281.6 4.5 copy-start.11
  281.6 5.1 slice-start.6
  318.3 193.6 %reduce-scatter.7.cloned.1.call-start = ((), (), s32[]{:S(2)}) async-start(), calls=%async_computation.4 | async-start | bytes 884736
  326.5 52.1 %copy-start.69 = (f32[2048]{0:T(1024)S(1)}, f32[2048]{0:T(1024)}, u32[]{:S(2)}) copy-start(f32[2048]{0:T(1024)} %copy-done.68) | copy-start | bytes 24580
  378.6 5.5 copy-start.4
  378.6 5.6 copy-start.8
  378.6 6.4 copy-start.15
  384.9 4.6 copy-start.38
  411.0 24.2 %copy-start.31 = (bf16[640,8,32]{0,2,1:T(8,128)(2,1)S(1)}, bf16[640,8,32]{0,2,1:T(8,128)(2,1)}, u32[]{:S(2)}) copy-start(bf16[640,8,32]{0,2,1:T(8,128)(2,1)} %copy-done.30) | copy-start | bytes 983044
  411.0 24.2 %copy-start.33 = (bf16[640,8,32]{0,2,1:T(8,128)(2,1)S(1)}, bf16[640,8,32]{0,2,1:T(8,128)(2,1)}, u32[]{:S(2)}) copy-start(bf16[640,8,32]{0,2,1:T(8,128)(2,1)} %copy-done.32) | copy-start | bytes 983044
  449.1 128.2 %reduce-scatter.9.cloned.1.call-start = ((), (), s32[]{:S(2)}) async-start(), calls=%async_computation.5 | async-start | bytes 884736
  465.2 11.5 %copy-start.22 = (f32[640,32]{0,1:T(8,128)S(1)}, f32[640,32]{0,1:T(8,128)}, u32[]{:S(2)}) copy-start(f32[640,32]{0,1:T(8,128)} %copy-done.21) | copy-start | bytes 245764
  465.2 11.7 %copy-start.17 = (bf16[2,64,4,640]{3,1,2,0:T(8,128)(2,1)S(1)}, bf16[2,64,4,640]{3,1,2,0:T(8,128)(2,1)}, u32[]{:S(2)}) copy-start(bf16[2,64,4,640]{3,1,2,0:T(8,128)(2,1)} %copy-done.16) | copy-start | bytes 1966084
  465.2 192.8 %all-reduce.16.cloned.1.call-start = ((), (), s32[]{:S(2)}) async-start(), calls=%async_computation.7 | async-start | bytes 1835008 | tf_op jit(solution)/shard_map/psum | solution.py:369
  465.2 11.4 %copy-start.44 = (f32[640,32]{0,1:T(8,128)S(1)}, f32[640,32]{0,1:T(8,128)}, u32[]{:S(2)}) copy-start(f32[640,32]{0,1:T(8,128)} %get-tuple-element.44) | copy-start | bytes 245764
  465.2 11.6 %copy-start.49 = (bf16[640,64]{0,1:T(8,128)(2,1)S(1)}, bf16[640,64]{0,1:T(8,128)(2,1)}, u32[]{:S(2)}) copy-start(bf16[640,64]{0,1:T(8,128)(2,1)} %copy-done.48) | copy-start | bytes 245764
  473.4 6.3 copy-start.67
  473.4 7.2 copy-start.19
  480.6 32.3 %copy-start.42 = (f32[384,2,64]{0,2,1:T(8,128)S(1)}, f32[384,2,64]{0,2,1:T(8,128)}, u32[]{:S(2)}) copy-start(f32[384,2,64]{0,2,1:T(8,128)} %get-tuple-element.36) | copy-start | bytes 589828
  480.6 33.2 %copy-start.45 = (f32[640,32]{0,1:T(8,128)S(1)}, f32[640,32]{0,1:T(8,128)}, u32[]{:S(2)}) copy-start(f32[640,32]{0,1:T(8,128)} %get-tuple-element.44) | copy-start | bytes 245764
  480.6 33.3 %copy-start.63 = (bf16[8,8,2,128]{3,1,2,0:T(8,128)(2,1)S(1)}, bf16[8,8,2,128]{3,1,2,0:T(8,128)(2,1)}, u32[]{:S(2)}) copy-start(bf16[8,8,2,128]{3,1,2,0:T(8,128)(2,1)} %copy-done.62) | copy-start | bytes 98308
  480.6 97.7 %copy-start.43 = (f32[384,2,64]{0,2,1:T(8,128)S(1)}, f32[384,2,64]{0,2,1:T(8,128)}, u32[]{:S(2)}) copy-start(f32[384,2,64]{0,2,1:T(8,128)} %get-tuple-element.39) | copy-start | bytes 589828
  484.6 278.7 %all-reduce.18.cloned.1.call-start = ((), (), s32[]{:S(2)}) async-start(), calls=%async_computation.8 | async-start | bytes 10485760 | tf_op jit(solution)/shard_map/psum | solution.py:233
  588.4 323.2 %all-reduce.14.cloned.1.call-start = ((), (), s32[]{:S(2)}) async-start(), calls=%async_computation.6 | async-start | bytes 7340032 | tf_op jit(solution)/shard_map/psum | solution.py:375
  588.7 4.2 copy-start.10
  588.7 6.6 copy-start.28
  595.3 70.1 %copy-start.23 = (f32[640,64]{0,1:T(8,128)S(1)}, f32[640,64]{0,1:T(8,128)}, u32[]{:S(2)}) copy-start(f32[640,64]{0,1:T(8,128)} %fusion.112) | copy-start | bytes 491524
  595.3 70.1 %copy-start.24 = (f32[640,64]{0,1:T(8,128)S(1)}, f32[640,64]{0,1:T(8,128)}, u32[]{:S(2)}) copy-start(f32[640,64]{0,1:T(8,128)} %fusion.72) | copy-start | bytes 491524
  595.3 70.1 %copy-start.26 = (f32[640,64]{0,1:T(8,128)S(1)}, f32[640,64]{0,1:T(8,128)}, u32[]{:S(2)}) copy-start(f32[640,64]{0,1:T(8,128)} %copy-done.25) | copy-start | bytes 491524
  595.3 70.1 %copy-start.55 = (bf16[640,192]{0,1:T(8,128)(2,1)S(1)}, bf16[640,192]{0,1:T(8,128)(2,1)}, u32[]{:S(2)}) copy-start(bf16[640,192]{0,1:T(8,128)(2,1)} %copy-done.54) | copy-start | bytes 737284
  595.4 70.1 %copy-start.56 = (bf16[256,2,64]{0,2,1:T(8,128)(2,1)S(1)}, bf16[256,2,64]{0,2,1:T(8,128)(2,1)}, u32[]{:S(2)}) copy-start(bf16[256,2,64]{0,2,1:T(8,128)(2,1)} %slice.294) | copy-start | bytes 196612
  595.4 70.5 %copy-start.71 = (f32[2048]{0:T(1024)S(1)}, f32[2048]{0:T(1024)}, u32[]{:S(2)}) copy-start(f32[2048]{0:T(1024)} %copy-done.70) | copy-start | bytes 24580
  595.4 70.5 %copy-start.73 = (f32[640]{0:T(1024)S(1)}, f32[640]{0:T(1024)}, u32[]{:S(2)}) copy-start(f32[640]{0:T(1024)} %copy-done.72) | copy-start | bytes 7684
  911.6 6.9 copy-start.58
  (27 other events, 64.7 us)
Sparse Core Ops, SparseCore 0:
  142.5 104.2 all-reduce.9
  318.4 60.0 all-reduce.11
  449.2 62.6 reduce-scatter.6
  516.0 61.3 reduce-scatter.8
  582.2 75.7 all-reduce.15
  660.8 102.3 all-reduce.17
  770.4 141.1 all-reduce.13
where the time goes:
time: 934 us; the launch traced here: 927 us
  waiting for transfers between devices  458 us (49%)
  matrix products  213 us (23%)
  blocking collectives  104 us (11%)
  other arithmetic  82.7 us (9%)
  local copies, waits for them, and re-layouts  50.9 us (5%)
  between operations  17.9 us (2%)
    psum x1, waiting for transfers between devices, shards(): lax.psum((grad_a_attn, grad_b_out, grad_a_mlp, grad_b_down), ('dp', 'tens...  136 us
    unnamed x9, waiting for transfers between devices  90 us
    psum x1, waiting for transfers between devices, shards(): attn_total = lax.psum(attn_part, 'tensor')  72.6 us
    dot_general x16, matrix products, plain_dot(): jnp.dot(left, right, precision=precision, preferred_element_type=jnp.floa...  61.5 us
    psum x1, waiting for transfers between devices, shards(): lax.psum(grad_b_query.astype(jnp.bfloat16), 'dp').astype(jnp.float32)  57.7 us
    psum x1, waiting for transfers between devices, shards(): lax.psum(mlp_part.astype(jnp.bfloat16), 'tensor').astype(jnp.float32)  55.6 us
    dot_general x16, matrix products, cols_dot(): lax.dot_general(left, right, (((1,), (1,)), ((), ())), precision=precisio...  53.2 us
    psum x1, waiting for transfers between devices, shards(): lax.psum(normed_two_part.astype(jnp.bfloat16), 'tensor').astype(jnp.float32)  45.6 us
  transfers between devices with their start and end apart: 7, of which 7 were waited for; matrix products, arithmetic and copies ran while one was open for 14% of the time, Pallas kernels for 0%

commit v1 on v0

v1 whole, which is shorter than its diff:
```python
import functools
import math

import jax
import jax.numpy as jnp
import numpy as np
from jax import lax
from jax.experimental import pallas as pl
from jax.experimental.pallas import tpu as pltpu
from jax.sharding import PartitionSpec as P

HD = 64
R = 16
NA = 4
RK = NA * R
PLEN = 384
CLEN = 128
CONT_DEV = 2
ROWS = PLEN + CONT_DEV * CLEN
EPSILON = 1e-05
ROPE_BASE = 500000.0
MASKED_SCORE = -1e30

BF = jnp.bfloat16
F32 = jnp.float32
VM = pltpu.VMEM
LANE = 128


def dn(a, b):
    return jnp.dot(a, b, preferred_element_type=F32)


def dt(a, b):
    return lax.dot_general(a, b, (((1,), (1,)), ((), ())), preferred_element_type=F32)


def dr(a, b):
    return lax.dot_general(a, b, (((0,), (0,)), ((), ())), preferred_element_type=F32)


def sel_row(adapter):
    lane = lax.broadcasted_iota(jnp.int32, (1, RK), 1)
    return (lax.shift_right_logical(lane, 4) == adapter).astype(F32)


def swap_halves(v):
    lane = lax.broadcasted_iota(jnp.int32, v.shape, 1)
    return jnp.where((lane & 63) < 32, pltpu.roll(v, LANE - 32, 1), pltpu.roll(v, 32, 1))


def rot(v, cos, sin):
    return v * cos + swap_halves(v) * sin


def call(kernel, name, ins, outs, scratch=(), grid=None, in_specs=None, out_specs=None, flops=0, limit=56 << 20):
    nbytes = sum(int(np.prod(a.shape)) * a.dtype.itemsize for a in ins) + sum(
        int(np.prod(s)) * jnp.dtype(d).itemsize for s, d in outs
    )
    whole = pl.BlockSpec(memory_space=VM)
    smem = pl.BlockSpec(memory_space=pltpu.SMEM)
    if in_specs is None:
        in_specs = [smem] + [whole] * (len(ins) - 1)
    if out_specs is None:
        out_specs = [whole] * len(outs)
    kw = {} if grid is None else {"grid": grid}
    return pl.pallas_call(
        kernel,
        out_shape=[jax.ShapeDtypeStruct(s, d) for s, d in outs],
        in_specs=in_specs,
        out_specs=out_specs,
        scratch_shapes=list(scratch),
        compiler_params=pltpu.CompilerParams(vmem_limit_bytes=limit),
        cost_estimate=pl.CostEstimate(flops=int(flops), bytes_accessed=int(nbytes), transcendentals=0),
        name=name,
        **kw,
    )(*ins)


def qkv_kernel(sc, x_ref, gain, aT, wq, wkv, bq, bkv, cos_ref, sin_ref, n1_ref, q_ref, k_ref, v_ref, u_ref):
    rows = x_ref.shape[0]
    x = x_ref[...].astype(F32)
    inv = lax.rsqrt(jnp.mean(x * x, axis=-1, keepdims=True) + EPSILON)
    n1_ref[...] = (x * inv * gain[...].astype(F32)).astype(BF)
    n1 = n1_ref[...]
    row = pl.program_id(0) * rows + lax.broadcasted_iota(jnp.int32, (rows, RK), 0)
    adapter = jnp.where(row < PLEN, sc[0], jnp.where(row < PLEN + CLEN, sc[1], sc[2]))
    lane = lax.broadcasted_iota(jnp.int32, (rows, RK), 1)
    sel = (lax.shift_right_logical(lane, 4) == adapter).astype(F32)
    u = dt(n1, aT[...])
    for part in range(3):
        u_ref[:, part * RK : (part + 1) * RK] = (u[:, part * RK : (part + 1) * RK] * sel).astype(BF)
    cos = cos_ref[...]
    sin = sin_ref[...]
    q = dn(n1, wq[...]) + dn(u_ref[:, :RK], bq[...])
    for c in range(q.shape[1] // LANE):
        q_ref[:, c * LANE : (c + 1) * LANE] = (
            rot(q[:, c * LANE : (c + 1) * LANE], cos, sin).astype(BF) * BF(0.125)
        )
    kv = dn(n1, wkv[...])
    width = k_ref.shape[1]
    kp = kv[:, :width] + dn(u_ref[:, RK : 2 * RK], bkv[:, :width])
    k_ref[...] = rot(kp, cos, sin).astype(BF)
    v_ref[...] = (kv[:, width:] + dn(u_ref[:, 2 * RK :], bkv[:, width:])).astype(BF)


def stack_heads(ref, r0, g):
    return jnp.concatenate(
        [ref[r0 : r0 + CLEN, (4 * g + h) * HD : (4 * g + h + 1) * HD] for h in range(4)], axis=0
    )


def softmax_low(s):
    top = jnp.max(s, axis=-1, keepdims=True)
    e = jnp.exp(s - top)
    return (e * (1.0 / jnp.sum(e, axis=-1, keepdims=True))).astype(BF)


def causal_tile():
    r = lax.broadcasted_iota(jnp.int32, (4 * CLEN, CLEN), 0) & (CLEN - 1)
    c = lax.broadcasted_iota(jnp.int32, (4 * CLEN, CLEN), 1)
    return c <= r


def project_out(sc, o_ref, wo, aoT, mine, other, scr):
    half = mine.shape[0]
    o = o_ref[...]
    width = wo.shape[1]
    for n in range(0, width, 512):
        part = dn(o, wo[:, n : n + 512]).astype(BF)
        scr[0, :, n : n + 512] = part[:half]
        scr[1, :, n : n + 512] = part[half:]
    u = dt(o, aoT[...]).astype(BF)
    pad = jnp.zeros((half, LANE - RK), BF)
    scr[0, :, width:] = jnp.concatenate([u[:half], pad], axis=1)
    scr[1, :, width:] = jnp.concatenate([u[half:], pad], axis=1)
    lo = sc[3]
    mine[...] = scr[lo]
    other[...] = scr[1 - lo]


P_OFF = (0, 128, 384)


def attn_p_kernel(sc, q_ref, k_ref, v_ref, wo, aoT, p_ref, o_ref, mine, other, scr):
    mask = causal_tile()
    for g in range(2):
        kg = k_ref[:, g * HD : (g + 1) * HD]
        vg = v_ref[:, g * HD : (g + 1) * HD]
        for i in range(PLEN // CLEN):
            size = (i + 1) * CLEN
            s = dt(stack_heads(q_ref, i * CLEN, g), kg[:size])
            tail = jnp.where(mask, s[:, size - CLEN :], MASKED_SCORE)
            s = tail if i == 0 else jnp.concatenate([s[:, : size - CLEN], tail], axis=1)
            p = softmax_low(s)
            p_ref[g, :, P_OFF[i] : P_OFF[i] + size] = p
            o = dn(p, vg[:size]).astype(BF)
            for h in range(4):
                o_ref[i * CLEN : (i + 1) * CLEN, (4 * g + h) * HD : (4 * g + h + 1) * HD] = o[
                    h * CLEN : (h + 1) * CLEN
                ]
    project_out(sc, o_ref, wo, aoT, mine, other, scr)


def attn_c_kernel(sc, q_ref, k_ref, v_ref, far, wo, aoT, p_ref, o_ref, mine, other, scr):
    mask = causal_tile()
    width = k_ref.shape[1]
    for j in range(CONT_DEV):
        r0 = j * CLEN
        for g in range(2):
            lanes = slice(g * HD, (g + 1) * HD)
            vlanes = slice(width + g * HD, width + (g + 1) * HD)
            qs = stack_heads(q_ref, r0, g)
            sf = dt(qs, far[j, :, lanes])
            so = jnp.where(mask, dt(qs, k_ref[r0 : r0 + CLEN, lanes]), MASKED_SCORE)
            p = softmax_low(jnp.concatenate([sf, so], axis=1))
            p_ref[j, g] = p
            o = (dn(p[:, :PLEN], far[j, :, vlanes]) + dn(p[:, PLEN:], v_ref[r0 : r0 + CLEN, lanes])).astype(BF)
            for h in range(4):
                o_ref[r0 : r0 + CLEN, (4 * g + h) * HD : (4 * g + h + 1) * HD] = o[h * CLEN : (h + 1) * CLEN]
    project_out(sc, o_ref, wo, aoT, mine, other, scr)


def norm2_kernel(which, sc, s_ref, t_ref, x_ref, gain, bo, h_ref, n2u_ref):
    width = x_ref.shape[1]
    sel = sel_row(sc[which] if which == 0 else sc[1 + sc[3]])
    u = ((s_ref[:, width : width + RK].astype(F32) + t_ref[:, width : width + RK].astype(F32)) * sel).astype(BF)
    attn = s_ref[:, :width].astype(F32) + t_ref[:, :width].astype(F32) + dn(u, bo[...])
    h = x_ref[...].astype(F32) + attn
    h_ref[...] = h
    inv = lax.rsqrt(jnp.mean(h * h, axis=-1, keepdims=True) + EPSILON)
    n2u_ref[:, :width] = (h * inv * gain[...].astype(F32)).astype(BF)
    n2u_ref[:, width:] = jnp.concatenate([u, jnp.zeros((u.shape[0], LANE - RK), BF)], axis=1)


def row_sel(which, sc, rows):
    if which == 0:
        return sel_row(sc[0])
    return jnp.concatenate(
        [jnp.broadcast_to(sel_row(sc[1]), (rows // 2, RK)), jnp.broadcast_to(sel_row(sc[2]), (rows // 2, RK))], axis=0
    )


def dact_kernel(sc, dy_ref, wd, bd, adT, dact_ref, dud_ref):
    @pl.when(pl.program_id(0) == 0)
    def _():
        sel = jnp.concatenate(
            [
                jnp.broadcast_to(sel_row(sc[0]), (PLEN, RK)),
                jnp.broadcast_to(sel_row(sc[1]), (CLEN, RK)),
                jnp.broadcast_to(sel_row(sc[2]), (CLEN, RK)),
            ],
            axis=0,
        )
        dud_ref[...] = (dt(dy_ref[...], bd[...]) * sel).astype(BF)

    dact_ref[...] = dt(dy_ref[...], wd[...]) + dn(dud_ref[...], adT[...])


def mlp_kernel(
    which, sc, mine, other, dact, dud, wg, wu, wd, bg, bu, adT, amT,
    mlp_mine, mlp_other, dn2_mine, dn2_other, gbg, gbu, gadT,
    n2s, um, mlp_acc, dn2_acc, ud_acc, dum_acc,
):
    half, width = mine.shape[0], mlp_acc.shape[1]
    rows = 2 * half
    lo = sc[3]
    step = pl.program_id(0)

    @pl.when(step == 0)
    def _():
        n2s[lo] = mine[:, :width]
        n2s[1 - lo] = other[:, :width]
        sel = row_sel(which, sc, rows)
        u = dt(n2s[...].reshape(rows, width), amT[...])
        um[:, :RK] = (u[:, :RK] * sel).astype(BF)
        um[:, RK:] = (u[:, RK:] * sel).astype(BF)

    n2 = n2s[...].reshape(rows, width)
    ug = um[:, :RK]
    uu = um[:, RK:]
    gate = dn(n2, wg[...]) + dn(ug, bg[...])
    upper = dn(n2, wu[...]) + dn(uu, bu[...])
    sigma = 1.0 / (1.0 + jnp.exp(-gate))
    silu = gate * sigma
    act = (silu * upper).astype(BF)
    da = dact[...].astype(F32)
    dg = (da * upper * (sigma * (1.0 + gate * (1.0 - sigma)))).astype(BF)
    du = (da * silu).astype(BF)
    gbg[...] = dr(ug, dg)
    gbu[...] = dr(uu, du)
    gadT[...] = dr(dud[...], act)
    mlp_part = dn(act, wd[...])
    dn2_part = dt(dg, wg[...]) + dt(du, wu[...])
    ud_part = dt(act, adT[...])
    dum_part = jnp.concatenate([dt(dg, bg[...]), dt(du, bu[...])], axis=1)

    @pl.when(step == 0)
    def _():
        mlp_acc[...] = mlp_part
        dn2_acc[...] = dn2_part
        ud_acc[...] = ud_part
        dum_acc[...] = dum_part

    @pl.when(step > 0)
    def _():
        mlp_acc[...] += mlp_part
        dn2_acc[...] += dn2_part
        ud_acc[...] += ud_part
        dum_acc[...] += dum_part

    @pl.when(step == pl.num_programs(0) - 1)
    def _():
        pad = jnp.zeros((half, LANE - RK), BF)
        for ref, who in ((mlp_mine, lo), (mlp_other, 1 - lo)):
            start = pl.multiple_of(who * half, half)
            ref[:, :width] = mlp_acc[pl.ds(start, half)].astype(BF)
            ref[:, width:] = jnp.concatenate([ud_acc[pl.ds(start, half)].astype(BF), pad], axis=1)
        for ref, who in ((dn2_mine, lo), (dn2_other, 1 - lo)):
            start = pl.multiple_of(who * half, half)
            ref[:, :width] = dn2_acc[pl.ds(start, half)].astype(BF)
            ref[:, width:] = dum_acc[pl.ds(start, half)].astype(BF)


def norm_back(v, gain, upstream):
    inv = lax.rsqrt(jnp.mean(v * v, axis=-1, keepdims=True) + EPSILON)
    scaled = v * inv
    weighted = upstream * gain
    return inv * (weighted - scaled * jnp.mean(weighted * scaled, axis=-1, keepdims=True))


def nbwd_kernel(which, sc, s_ref, t_ref, h_ref, dy_ref, gain, amT, dh_ref, dau_ref):
    width = h_ref.shape[1]
    sel = sel_row(sc[which] if which == 0 else sc[1 + sc[3]])
    du = s_ref[:, width:].astype(F32) + t_ref[:, width:].astype(F32)
    dum = (du * jnp.concatenate([sel, sel], axis=1)).astype(BF)
    dn2 = s_ref[:, :width].astype(F32) + t_ref[:, :width].astype(F32) + dn(dum, amT[...])
    dh = dy_ref[...].astype(F32) + norm_back(h_ref[...], gain[...].astype(F32), dn2)
    dh_ref[...] = dh
    dau_ref[:, :width] = dh.astype(BF)
    dau_ref[:, width:] = dum


def out_kernel(which, sc, s_ref, t_ref, h_ref, bd, out_ref):
    width = h_ref.shape[1]
    sel = sel_row(sc[which] if which == 0 else sc[1 + sc[3]])
    u = ((s_ref[:, width : width + RK].astype(F32) + t_ref[:, width : width + RK].astype(F32)) * sel).astype(BF)
    mlp = s_ref[:, :width].astype(F32) + t_ref[:, :width].astype(F32) + dn(u, bd[...])
    out_ref[:, :width] = (h_ref[...] + mlp).astype(BF)
    out_ref[:, width:] = jnp.concatenate([u, jnp.zeros((u.shape[0], LANE - RK), BF)], axis=1)


def out_grads(which, sc, mine, other, n2_mine, n2_other, o_ref, wo, aoT, bo, do_ref, gaoT, gbo, gamT, das):
    half = mine.shape[0]
    width = das.shape[2]
    rows = 2 * half
    lo = sc[3]
    das[lo] = mine[:, :width]
    das[1 - lo] = other[:, :width]
    da = das[...].reshape(rows, width)
    duo = (dt(da, bo[...]) * row_sel(which, sc, rows)).astype(BF)
    do_ref[...] = (dt(da, wo[...]) + dn(duo, aoT[...])).astype(BF)
    gaoT[...] = dr(duo, o_ref[...])
    quarter = gbo.shape[1]
    col = pl.ds(pl.multiple_of(sc[4] * quarter, quarter), quarter)
    gbo[...] = dr(n2_mine[:, width : width + RK], mine[:, col]) + dr(n2_other[:, width : width + RK], other[:, col])
    gamT[...] = dr(mine[:, width:], n2_mine[:, col]) + dr(other[:, width:], n2_other[:, col])


def put_dq(dq, dq_ref, r0, g):
    for h in range(4):
        dq_ref[r0 : r0 + CLEN, (4 * g + h) * HD : (4 * g + h + 1) * HD] = dq[h * CLEN : (h + 1) * CLEN]


def back_scores(p, dp):
    pf = p.astype(F32)
    return (pf * (dp - jnp.sum(pf * dp, axis=-1, keepdims=True))).astype(BF)


def unrotate_q(dq_scr, cos_ref, sin_ref, dqp_ref):
    cos = cos_ref[...]
    sin = sin_ref[...]
    for c in range(dqp_ref.shape[1] // LANE):
        lanes = slice(c * LANE, (c + 1) * LANE)
        dqp_ref[:, lanes] = rot(dq_scr[:, lanes].astype(F32), cos, -sin).astype(BF)


def abwd_p_kernel(
    sc, mine, other, n2_mine, n2_other, o_ref, wo, aoT, bo, p_ref, q_ref, k_ref, v_ref, cos_ref, sin_ref,
    dqp_ref, dkv_ref, gaoT, gbo, gamT,
    das, do_ref, dq_scr,
):
    out_grads(0, sc, mine, other, n2_mine, n2_other, o_ref, wo, aoT, bo, do_ref, gaoT, gbo, gamT, das)
    width = k_ref.shape[1]
    for g in range(2):
        lanes = slice(g * HD, (g + 1) * HD)
        vlanes = slice(width + g * HD, width + (g + 1) * HD)
        kg = k_ref[:, lanes]
        vg = v_ref[:, lanes]
        for i in reversed(range(PLEN // CLEN)):
            size = (i + 1) * CLEN
            qi = stack_heads(q_ref, i * CLEN, g)
            doi = stack_heads(do_ref, i * CLEN, g)
            p = p_ref[g, :, P_OFF[i] : P_OFF[i] + size]
            ds = back_scores(p, dt(doi, vg[:size]))
            put_dq((dn(ds, kg[:size]) * 0.125).astype(BF), dq_scr, i * CLEN, g)
            dk = dr(ds, qi)
            dv = dr(p, doi)
            if size == PLEN:
                dkv_ref[:, lanes] = dk
                dkv_ref[:, vlanes] = dv
            else:
                dkv_ref[:size, lanes] += dk
                dkv_ref[:size, vlanes] += dv
    unrotate_q(dq_scr, cos_ref, sin_ref, dqp_ref)


def abwd_c_kernel(
    sc, mine, other, n2_mine, n2_other, o_ref, wo, aoT, bo, p_ref, q_ref, k_ref, v_ref, far, cos_ref, sin_ref,
    dqp_ref, dkvp_ref, dfar_ref, gaoT, gbo, gamT,
    das, do_ref, dq_scr, dkv_scr,
):
    out_grads(1, sc, mine, other, n2_mine, n2_other, o_ref, wo, aoT, bo, do_ref, gaoT, gbo, gamT, das)
    width = k_ref.shape[1]
    for j in range(CONT_DEV):
        r0 = j * CLEN
        for g in range(2):
            lanes = slice(g * HD, (g + 1) * HD)
            vlanes = slice(width + g * HD, width + (g + 1) * HD)
            qi = stack_heads(q_ref, r0, g)
            doi = stack_heads(do_ref, r0, g)
            p = p_ref[j, g]
            dp = jnp.concatenate([dt(doi, far[j, :, vlanes]), dt(doi, v_ref[r0 : r0 + CLEN, lanes])], axis=1)
            ds = back_scores(p, dp)
            dq = dn(ds[:, :PLEN], far[j, :, lanes]) + dn(ds[:, PLEN:], k_ref[r0 : r0 + CLEN, lanes])
            put_dq((dq * 0.125).astype(BF), dq_scr, r0, g)
            dk = dr(ds, qi)
            dv = dr(p, doi)
            dfar_ref[j, :, lanes] = dk[:PLEN]
            dfar_ref[j, :, vlanes] = dv[:PLEN]
            dkv_scr[r0 : r0 + CLEN, lanes] = dk[PLEN:]
            dkv_scr[r0 : r0 + CLEN, vlanes] = dv[PLEN:]
    unrotate_q(dq_scr, cos_ref, sin_ref, dqp_ref)
    dkvp_ref[:, :width] = rot(dkv_scr[:, :width].astype(BF).astype(F32), cos_ref[...], -sin_ref[...]).astype(BF)
    dkvp_ref[:, width:] = dkv_scr[:, width:].astype(BF)


def dn1_tail(sc, which, dqp, dkvp, u_ref, wq, wkv, bq, bkv, mine, other, gbq, gbkv, scr):
    half = mine.shape[0]
    width = wq.shape[0]
    kvw = dkvp.shape[1] // 2
    for n in range(0, width, 512):
        part = (dt(dqp, wq[n : n + 512]) + dt(dkvp, wkv[n : n + 512])).astype(BF)
        scr[0, :, n : n + 512] = part[:half]
        scr[1, :, n : n + 512] = part[half:]
    du = jnp.concatenate(
        [
            dt(dqp, bq[...]),
            dt(dkvp[:, :kvw], bkv[:, :kvw]),
            dt(dkvp[:, kvw:], bkv[:, kvw:]),
            jnp.zeros((2 * half, RK), F32),
        ],
        axis=1,
    ).astype(BF)
    scr[0, :, width:] = du[:half]
    scr[1, :, width:] = du[half:]
    gbq[...] = dr(u_ref[:, :RK], dqp)
    gbkv[:, :kvw] = dr(u_ref[:, RK : 2 * RK], dkvp[:, :kvw])
    gbkv[:, kvw:] = dr(u_ref[:, 2 * RK :], dkvp[:, kvw:])
    lo = sc[3]
    mine[...] = scr[lo]
    other[...] = scr[1 - lo]


def dn1_c_kernel(sc, dqp, dkvp, u_ref, wq, wkv, bq, bkv, mine, other, gbq, gbkv, scr):
    dn1_tail(sc, 1, dqp[...], dkvp[...], u_ref, wq, wkv, bq, bkv, mine, other, gbq, gbkv, scr)


def dn1_p_kernel(
    sc, dqp, dkv, own, u_ref, wq, wkv, bq, bkv, cos_ref, sin_ref, mine, other, gbq, gbkv, scr, dkvp_scr
):
    kvw = dkv.shape[1] // 2
    tot = dkv[...] + own[...].astype(F32)
    dkvp_scr[:, :kvw] = rot(tot[:, :kvw].astype(BF).astype(F32), cos_ref[...], -sin_ref[...]).astype(BF)
    dkvp_scr[:, kvw:] = tot[:, kvw:].astype(BF)
    dn1_tail(sc, 0, dqp[...], dkvp_scr[...], u_ref, wq, wkv, bq, bkv, mine, other, gbq, gbkv, scr)


def fin_kernel(which, sc, s_ref, t_ref, x_ref, dh_ref, gain, aT, out_ref):
    width = x_ref.shape[1]
    sel = sel_row(sc[which] if which == 0 else sc[1 + sc[3]])
    du = s_ref[:, width : width + 3 * RK].astype(F32) + t_ref[:, width : width + 3 * RK].astype(F32)
    duq = (du * jnp.concatenate([sel, sel, sel], axis=1)).astype(BF)
    dn1 = s_ref[:, :width].astype(F32) + t_ref[:, :width].astype(F32) + dn(duq, aT[...])
    grad = dh_ref[...] + norm_back(x_ref[...].astype(F32), gain[...].astype(F32), dn1)
    out_ref[:, :width] = grad.astype(BF)
    out_ref[:, width:] = jnp.concatenate([duq, jnp.zeros((duq.shape[0], RK), BF)], axis=1)


MESH = pl.DeviceIdType.MESH


def rows_loop(total, step, body):
    def one(i, carry):
        body(pl.multiple_of(i * step, step))
        return carry

    lax.fori_loop(0, total // step, one, 0)


def place():
    d = lax.axis_index("dp")
    t = lax.axis_index("tensor")
    return d, t


def remote(src, dst, send, recv, device):
    return pltpu.make_async_remote_copy(
        src_ref=src, dst_ref=dst, send_sem=send, recv_sem=recv, device_id=device, device_id_type=MESH
    )


def greet(d, t, n_dp):
    barrier = pltpu.get_barrier_semaphore()
    for device in ((d, t ^ 1), (d, t ^ 2), (d ^ 1, t), ((d + 2) % n_dp, t), ((d + n_dp - 2) % n_dp, t)):
        pl.semaphore_signal(barrier, inc=1, device_id=device, device_id_type=MESH)


def greeted():
    pl.semaphore_wait(pltpu.get_barrier_semaphore(), 5)


class Spread:
    def __init__(self, every, sems, d, t, hi):
        self.every, self.sems, self.d, self.t, self.hi = every, sems, d, t, hi
        self.z, self.x = d // 2, d % 2

    def across(self, z):
        block = z * 2 + self.x
        up_s, up_r, down_s, down_r, x_s, x_r = self.sems
        return remote(self.every.at[block], self.every.at[block], x_s.at[z], x_r.at[z], (self.d ^ 1, self.t))

    def along(self, z, s, up):
        block = z * 2 + self.x
        up_s, up_r, down_s, down_r, x_s, x_r = self.sems
        send, recv, step = (up_s, up_r, 2) if up else (down_s, down_r, -2)
        return remote(self.every.at[block], self.every.at[block], send.at[s], recv.at[s], (self.d + step, self.t))

    def start(self):
        self.across(self.z).start()

        @pl.when(self.z < self.hi - 1)
        def _():
            self.along(self.z, 1, True).start()

        @pl.when(self.z > 0)
        def _():
            self.along(self.z, 1, False).start()

    def hop(self, s):
        if s > self.hi - 1:
            return
        for up in (True, False):
            origin = self.z - s if up else self.z + s
            held = origin >= 0 if up else origin < self.hi
            further = self.z < self.hi - 1 if up else self.z > 0

            @pl.when(held)
            def _(origin=origin, up=up, further=further):
                self.along(origin, s, up).wait_recv()
                self.across(origin).start()
                if s + 1 <= self.hi - 1:

                    @pl.when(further)
                    def _():
                        self.along(origin, s + 1, up).start()

    def finish(self):
        for z in range(self.hi):
            across = self.across(z)
            across.wait_send()
            block = z * 2 + 1 - self.x
            up_s, up_r, down_s, down_r, x_s, x_r = self.sems
            remote(self.every.at[block], self.every.at[block], x_s.at[z], x_r.at[z], (self.d ^ 1, self.t)).wait_recv()
        for s in range(1, self.hi):
            for up in (True, False):
                origin = self.z - s + 1 if up else self.z + s - 1
                held = origin >= 0 if up else origin < self.hi
                further = self.z < self.hi - 1 if up else self.z > 0

                @pl.when(held & further)
                def _(origin=origin, up=up, s=s):
                    self.along(origin, s, up).wait_send()


class TensorSum:
    def __init__(self, snd, got, mine, theirs, sems, d, t):
        self.snd, self.got, self.mine, self.theirs, self.sems, self.t = snd, got, mine, theirs, sems, t
        self.lo = t % 2
        self.core = remote(snd.at[1 - self.lo], got, sems.at[0], sems.at[1], (d, t ^ 1))
        self.chip = remote(mine, theirs, sems.at[2], sems.at[3], (d, t ^ 2))

    def begin(self):
        self.core.start()

    def middle(self):
        self.core.wait_recv()

        def add(r):
            rows = pl.ds(r, 16)
            self.mine[rows] = (self.snd[self.lo, rows].astype(F32) + self.got[rows].astype(F32)).astype(BF)

        rows_loop(self.mine.shape[0], 16, add)
        self.chip.start()

    def end(self):
        self.chip.wait_recv()

    def drain(self):
        self.core.wait_send()
        self.chip.wait_send()


def all_sel(sc):
    return jnp.concatenate(
        [
            jnp.broadcast_to(sel_row(sc[0]), (PLEN, RK)),
            jnp.broadcast_to(sel_row(sc[1]), (CLEN, RK)),
            jnp.broadcast_to(sel_row(sc[2]), (CLEN, RK)),
        ],
        axis=0,
    )


def front_kernel(
    n_dp, sc, gain1, gain2, aT, bq, bkvd, aoT, bo, bd, cos, sin, tok_h, wq_h, wkv_h, wo_h, dy_h, wd_h, adp_h,
    n1q_h, q_h, kv_h, u_h, pp_h, pc_h, o_h, far_h, hp_h, hc_h, n2p_h, n2c_h, dact_h, dud_h,
    tok, n1, wq, wkv, wo, dyu, wdc, dact, every, kv, q, u, far, pp, pc, o,
    snd_p, got_p, s_p, t_p, snd_c, got_c, s_c, t_c, n2p, n2c, hp, hc, tmp,
    lsem, osem, wsem, dsem, psem, csem, nsem, up_s, up_r, down_s, down_r, x_s, x_r,
):
    d, t = place()
    lo = t % 2
    hi = n_dp // 2
    rows, width = tok.shape
    qw = wq.shape[1]
    kvw = wkv.shape[1] // 2
    hidden = wd_h.shape[0]
    ht = wdc.shape[1]
    steps = hidden // ht
    hpn, hcn = PLEN // 2, CLEN
    quarter = n1q_h.shape[1]
    greet(d, t, n_dp)
    loads = [
        pltpu.make_async_copy(src, dst, lsem.at[i])
        for i, (src, dst) in enumerate(
            [(tok_h, tok), (wkv_h, wkv), (wq_h, wq), (wo_h, wo), (dy_h, dyu.at[:, :width])]
        )
    ]
    for c in loads:
        c.start()

    def wd_copies(i, slot):
        return (
            pltpu.make_async_copy(wd_h.at[pl.ds(i * ht, ht)], wdc.at[slot, :, :width], wsem.at[slot, 0]),
            pltpu.make_async_copy(adp_h.at[pl.ds(i * ht, ht)], wdc.at[slot, :, width:], wsem.at[slot, 1]),
        )

    for i in range(2):
        for c in wd_copies(i, i):
            c.start()
    stores = []

    def store(src, dst):
        c = pltpu.make_async_copy(src, dst, osem.at[len(stores)])
        c.start()
        stores.append(c)

    loads[0].wait()

    def norm1(r):
        x = tok[pl.ds(r, 16)].astype(F32)
        inv = lax.rsqrt(jnp.mean(x * x, axis=-1, keepdims=True) + EPSILON)
        n1[pl.ds(r, 16)] = (x * inv * gain1[...].astype(F32)).astype(BF)

    rows_loop(rows, 16, norm1)
    sel = all_sel(sc)
    uf = dt(n1[...], aT[...])
    for part in range(3):
        u[:, part * RK : (part + 1) * RK] = (uf[:, part * RK : (part + 1) * RK] * sel).astype(BF)
    loads[1].wait()
    kvf = dn(n1[...], wkv[...]) + dn(u[:, RK : 3 * RK], bkvd[...])
    kv[:, :kvw] = rot(kvf[:, :kvw], cos[...], sin[...]).astype(BF)
    kv[:, kvw:] = kvf[:, kvw:].astype(BF)
    every[d] = kv[:PLEN]
    greeted()
    spread = Spread(every, (up_s, up_r, down_s, down_r, x_s, x_r), d, t, hi)
    spread.start()

    loads[2].wait()
    qf = dn(n1[...], wq[...]) + dn(u[:, :RK], bq[...])
    for c in range(qw // LANE):
        lanes = slice(c * LANE, (c + 1) * LANE)
        q[:, lanes] = rot(qf[:, lanes], cos[...], sin[...]).astype(BF) * BF(0.125)
    store(n1.at[:, pl.ds(pl.multiple_of(t * quarter, quarter), quarter)], n1q_h)
    store(q, q_h)
    store(kv, kv_h)
    store(u, u_h)

    def keep_o(of, r0, g):
        for h in range(4):
            o[r0 : r0 + CLEN, (4 * g + h) * HD : (4 * g + h + 1) * HD] = of[h * CLEN : (h + 1) * CLEN]

    mask = causal_tile()
    spread.hop(1)
    for g in range(2):
        kg = kv[:PLEN, g * HD : (g + 1) * HD]
        vg = kv[:PLEN, kvw + g * HD : kvw + (g + 1) * HD]
        for i in range(PLEN // CLEN):
            size = (i + 1) * CLEN
            s = dt(stack_heads(q, i * CLEN, g), kg[:size])
            tail = jnp.where(mask, s[:, size - CLEN :], MASKED_SCORE)
            s = tail if i == 0 else jnp.concatenate([s[:, : size - CLEN], tail], axis=1)
            p = softmax_low(s)
            pp[g, :, P_OFF[i] : P_OFF[i] + size] = p
            keep_o(dn(p, vg[:size]).astype(BF), i * CLEN, g)
    store(pp, pp_h)
    spread.hop(2)

    def project(r0, half, snd):
        ov = o[r0 : r0 + 2 * half]
        for n in range(0, width, 512):
            part = dn(ov, wo[:, n : n + 512]).astype(BF)
            snd[0, :, n : n + 512] = part[:half]
            snd[1, :, n : n + 512] = part[half:]
        uo = dt(ov, aoT[...]).astype(BF)
        pad = jnp.zeros((half, LANE - RK), BF)
        snd[0, :, width:] = jnp.concatenate([uo[:half], pad], axis=1)
        snd[1, :, width:] = jnp.concatenate([uo[half:], pad], axis=1)

    loads[3].wait()
    project(0, hpn, snd_p)
    sum_p = TensorSum(snd_p, got_p, s_p, t_p, psem, d, t)
    sum_p.begin()
    spread.hop(3)

    loads[4].wait()
    dud = (dt(dyu[:, :width], bd[...]) * sel).astype(BF)
    dyu[:, width:] = jnp.concatenate([dud, jnp.zeros((rows, LANE - RK), BF)], axis=1)
    store(dyu.at[:, width:], dud_h)
    outs = []

    def act_grad(i):
        slot = i % 2
        for c in wd_copies(i, slot):
            c.wait()
        if i >= 2:
            outs[i - 2].wait()
        dact[slot] = dt(dyu[...], wdc[slot]).astype(BF)
        c = pltpu.make_async_copy(dact.at[slot], dact_h.at[:, pl.ds(i * ht, ht)], dsem.at[slot])
        c.start()
        outs.append(c)
        if i + 2 < steps:
            for c in wd_copies(i + 2, slot):
                c.start()

    act_grad(0)
    sum_p.middle()
    for i in range(1, steps):
        act_grad(i)
        spread.hop(i + 3)
    for s in range(steps + 3, hi):
        spread.hop(s)
    spread.finish()

    far[0] = every[sc[3]]
    far[1] = every[sc[4]]
    store(far, far_h)
    for j in range(CONT_DEV):
        r0 = PLEN + j * CLEN
        for g in range(2):
            lanes = slice(g * HD, (g + 1) * HD)
            vlanes = slice(kvw + g * HD, kvw + (g + 1) * HD)
            qs = stack_heads(q, r0, g)
            sf = dt(qs, far[j, :, lanes])
            so = jnp.where(mask, dt(qs, kv[r0 : r0 + CLEN, lanes]), MASKED_SCORE)
            p = softmax_low(jnp.concatenate([sf, so], axis=1))
            pc[2 * j + g] = p
            keep_o((dn(p[:, :PLEN], far[j, :, vlanes]) + dn(p[:, PLEN:], kv[r0 : r0 + CLEN, vlanes])).astype(BF), r0, g)
    store(pc, pc_h)
    store(o, o_h)
    project(PLEN, hcn, snd_c)
    sum_c = TensorSum(snd_c, got_c, s_c, t_c, csem, d, t)
    sum_c.begin()
    sum_c.middle()

    def norm2(which, total, r0, h, n2, adapter):
        half = h.shape[0]
        total.end()
        sr = sel_row(adapter)
        uo = ((total.mine[:, width : width + RK].astype(F32) + total.theirs[:, width : width + RK].astype(F32)) * sr).astype(BF)
        tmp[:half] = dn(uo, bo[...])
        start = r0 + lo * half

        def one(r):
            here = pl.ds(r, 16)
            hv = (
                tok[pl.ds(pl.multiple_of(start + r, 16), 16)].astype(F32)
                + total.mine[here, :width].astype(F32)
                + total.theirs[here, :width].astype(F32)
                + tmp[here]
            )
            h[here] = hv
            inv = lax.rsqrt(jnp.mean(hv * hv, axis=-1, keepdims=True) + EPSILON)
            n2[lo, here, :width] = (hv * inv * gain2[...].astype(F32)).astype(BF)

        rows_loop(half, 16, one)
        n2[lo, :, width:] = jnp.concatenate([uo, jnp.zeros((half, LANE - RK), BF)], axis=1)
        c = remote(n2.at[lo], n2.at[lo], nsem.at[which, 0], nsem.at[which, 1], (d, t ^ 1))
        c.start()
        return c

    n2_copy_p = norm2(0, sum_p, 0, hp, n2p, sc[0])
    store(hp, hp_h)
    n2_copy_c = norm2(1, sum_c, PLEN, hc, n2c, jnp.where(lo == 0, sc[1], sc[2]))
    store(hc, hc_h)

    def arrived(which, n2):
        remote(n2.at[1 - lo], n2.at[1 - lo], nsem.at[which, 0], nsem.at[which, 1], (d, t ^ 1)).wait_recv()

    arrived(0, n2p)
    store(n2p, n2p_h)
    arrived(1, n2c)
    store(n2c, n2c_h)
    n2_copy_p.wait_send()
    n2_copy_c.wait_send()
    sum_p.drain()
    sum_c.drain()
    for c in outs[-2:]:
        c.wait()
    for c in stores:
        c.wait()


def front(n_dp, sc, small, large):
    rows, width = large[0].shape
    qw = large[1].shape[1]
    kvw2 = large[2].shape[1]
    hidden = large[5].shape[0]
    quarter = width // 4
    wide = width + LANE
    ht = 512
    hpn, hcn = PLEN // 2, CLEN
    outs = [
        ((rows, quarter), BF), ((rows, qw), BF), ((rows, kvw2), BF), ((rows, 3 * RK), BF), ((2, 4 * CLEN, 768), BF),
        ((4, 4 * CLEN, 4 * CLEN), BF), ((rows, qw), BF), ((CONT_DEV, PLEN, kvw2), BF), ((hpn, width), F32),
        ((hcn, width), F32), ((2, hpn, wide), BF), ((2, hcn, wide), BF), ((rows, hidden), BF), ((rows, LANE), BF),
    ]
    dma = pltpu.SemaphoreType.DMA
    scratch = [
        VM((rows, width), BF), VM((rows, width), BF), VM((width, qw), BF), VM((width, kvw2), BF), VM((qw, width), BF),
        VM((rows, wide), BF), VM((2, ht, wide), BF), VM((2, rows, ht), BF), VM((n_dp, PLEN, kvw2), BF), VM((rows, kvw2), BF),
        VM((rows, qw), BF), VM((rows, 3 * RK), BF), VM((CONT_DEV, PLEN, kvw2), BF), VM((2, 4 * CLEN, 768), BF),
        VM((4, 4 * CLEN, 4 * CLEN), BF), VM((rows, qw), BF),
        VM((2, hpn, wide), BF), VM((hpn, wide), BF), VM((hpn, wide), BF), VM((hpn, wide), BF),
        VM((2, hcn, wide), BF), VM((hcn, wide), BF), VM((hcn, wide), BF), VM((hcn, wide), BF),
        VM((2, hpn, wide), BF), VM((2, hcn, wide), BF), VM((hpn, width), F32), VM((hcn, width), F32), VM((hpn, width), F32),
        dma((5,)), dma((13,)), dma((2, 2)), dma((2,)), dma((4,)), dma((4,)), dma((2, 2)),
    ] + [dma((n_dp // 2 + 1,))] * 6
    vm = pl.BlockSpec(memory_space=VM)
    anyspace = pl.BlockSpec(memory_space=pl.ANY)
    return pl.pallas_call(
        functools.partial(front_kernel, n_dp),
        out_shape=[jax.ShapeDtypeStruct(s, dtype) for s, dtype in outs],
        in_specs=[pl.BlockSpec(memory_space=pltpu.SMEM)] + [vm] * len(small) + [anyspace] * len(large),
        out_specs=[anyspace] * len(outs),
        scratch_shapes=scratch,
        compiler_params=pltpu.CompilerParams(vmem_limit_bytes=60 << 20, collective_id=1, has_side_effects=True),
        cost_estimate=pl.CostEstimate(flops=2 * rows * width * 4096, bytes_accessed=40 << 20, transcendentals=0),
        name="front",
    )(sc, *small, *large)


def rope_tables():
    position = np.concatenate([np.arange(PLEN)] + [PLEN + np.arange(CLEN)] * CONT_DEV).astype(np.float32)
    exponent = np.arange(HD // 2, dtype=np.float32) * np.float32(2.0 / HD)
    frequency = np.exp(np.float32(-math.log(ROPE_BASE)) * exponent).astype(np.float32)
    angle = position[:, None] * frequency[None, :]
    cos, sin = np.cos(angle).astype(np.float32), np.sin(angle).astype(np.float32)
    return np.tile(cos, (1, 4)), np.concatenate([-sin, sin, -sin, sin], axis=1)


def shards(
    tokens, cotangent, gain_attn, gain_mlp, w_query, w_kv, w_out, w_gate_up, w_down, a_attn, b_query, b_kv,
    a_out, b_out, a_mlp, b_mlp, a_down, b_down, prompt_adapter, cont_adapter, group_map,
):
    rows, width = tokens.shape
    qw = w_query.shape[1]
    kvw = w_kv.shape[2]
    hidden = w_down.shape[0]
    n_dp = lax.axis_size("dp")
    n_t = lax.axis_size("tensor")
    quarter = width // n_t
    t = lax.axis_index("tensor")
    lo = t & 1
    sc = jnp.concatenate(
        [prompt_adapter, cont_adapter, jnp.stack([lo, t]).astype(jnp.int32), jnp.zeros((3,), jnp.int32)]
    )
    partners = lax.dynamic_slice_in_dim(group_map, lax.axis_index("dp") * CONT_DEV, CONT_DEV)
    cos_np, sin_np = rope_tables()
    cos, sin = jnp.asarray(cos_np), jnp.asarray(sin_np)
    gain1 = gain_attn.reshape(1, width)
    gain2 = gain_mlp.reshape(1, width)
    aT = a_attn.transpose(1, 2, 3, 0).reshape(3 * RK, width)
    aoT = a_out.transpose(1, 2, 0).reshape(RK, qw)
    amT = a_mlp.transpose(1, 2, 3, 0).reshape(2 * RK, width)
    adT = a_down.transpose(1, 2, 0).reshape(RK, hidden)
    bq = b_query.reshape(RK, qw)
    bkv = b_kv.reshape(RK, 2 * kvw)
    bo = b_out.reshape(RK, width)
    bm = b_mlp.reshape(RK, 2 * hidden)
    bd = b_down.reshape(RK, width)
    wkv = w_kv.reshape(width, 2 * kvw)
    wgu = w_gate_up.reshape(width, 2 * hidden)

    core_pairs = [(i, i ^ 1) for i in range(n_t)]
    chip_pairs = [(i, i ^ 2) for i in range(n_t)]

    def to_core(v):
        return lax.ppermute(v, "tensor", core_pairs)

    def to_chip(v):
        return lax.ppermute(v, "tensor", chip_pairs)

    def tensor_sum(mine, other):
        s = (mine.astype(F32) + to_core(other).astype(F32)).astype(BF)
        return s, to_chip(s)

    def join(mine, other):
        return jnp.where(lo == 0, jnp.concatenate([mine, other], 0), jnp.concatenate([other, mine], 0))

    def mine_rows(v):
        hp = PLEN // 2
        hc = CLEN
        return (
            lax.dynamic_slice_in_dim(v, lo * hp, hp, 0),
            lax.dynamic_slice_in_dim(v, PLEN + lo * hc, hc, 0),
        )

    x_p, x_c = mine_rows(tokens)
    dy_p, dy_c = mine_rows(cotangent)

    hp, hc = PLEN // 2, CLEN
    wide = width + LANE
    zero_kv = jnp.zeros((RK, kvw), BF)
    bkvd = jnp.concatenate(
        [jnp.concatenate([bkv[:, :kvw], zero_kv], 1), jnp.concatenate([zero_kv, bkv[:, kvw:]], 1)], 0
    )
    adp = jnp.concatenate([adT.T, jnp.zeros((hidden, LANE - RK), BF)], axis=1)
    fsc = jnp.concatenate([prompt_adapter, cont_adapter, partners, jnp.zeros((3,), jnp.int32)])
    (n1q, q, kv, u, p_p, p_c, o, far, h_p, h_c, n2pa, n2ca, dact, dud) = front(
        n_dp, fsc,
        [gain1, gain2, aT, bq, bkvd, aoT, bo, bd, cos, sin],
        [tokens, w_query, wkv, w_out, cotangent, w_down, adp],
    )
    k, v = kv[:, :kvw], kv[:, kvw:]
    p_c = p_c.reshape(2, 2, 4 * CLEN, 4 * CLEN)
    o_p, o_c = o[:PLEN], o[PLEN:]
    dud = dud[:, :RK]
    n2_p, n2_po = n2pa[lo], n2pa[1 - lo]
    n2_c, n2_co = n2ca[lo], n2ca[1 - lo]
    ht = 256
    steps = hidden // ht
    smem = pl.BlockSpec(memory_space=pltpu.SMEM)
    fixed = lambda a: pl.BlockSpec(a.shape, lambda i: (0, 0))
    down_rows = pl.BlockSpec((ht, width), lambda i: (i, 0))
    hid_cols = lambda r: pl.BlockSpec((r, ht), lambda i: (0, i))
    hid_cols2 = lambda r: pl.BlockSpec((r, ht), lambda i: (0, i + steps))

    def mlp(which, n2u, n2u_other, r0):
        half = n2u.shape[0]
        r = 2 * half
        blk = pl.BlockSpec((r, ht), lambda i: (0, i))
        hold = pl.BlockSpec((half, wide), lambda i: (0, 0))
        return call(
            functools.partial(mlp_kernel, which), "mlp_pc"[: 5 + which],
            [sc, n2u, n2u_other, dact[r0 : r0 + r], dud[r0 : r0 + r], wgu, wgu, w_down, bm, bm, adT, amT],
            [((half, wide), BF)] * 4 + [((RK, hidden), F32)] * 3,
            grid=(steps,),
            in_specs=[smem, hold, hold, blk, pl.BlockSpec((r, RK), lambda i: (0, 0)), hid_cols(width), hid_cols2(width),
                      down_rows, hid_cols(RK), hid_cols2(RK), hid_cols(RK), fixed(amT)],
            out_specs=[hold] * 4 + [hid_cols(RK)] * 3,
            scratch=[VM((2, half, width), BF), VM((r, 2 * RK), BF), VM((r, width), F32), VM((r, width), F32),
                     VM((r, RK), F32), VM((r, 2 * RK), F32)],
            flops=2 * r * width * hidden * 5,
        )

    mlp_pm, mlp_po, dn2_pm, dn2_po, gbg_p, gbu_p, gad_p = mlp(0, n2_p, n2_po, 0)
    sd_p, td_p = tensor_sum(dn2_pm, dn2_po)
    mlp_cm, mlp_co, dn2_cm, dn2_co, gbg_c, gbu_c, gad_c = mlp(1, n2_c, n2_co, PLEN)
    sd_c, td_c = tensor_sum(dn2_cm, dn2_co)
    sm_p, tm_p = tensor_sum(mlp_pm, mlp_po)
    sm_c, tm_c = tensor_sum(mlp_cm, mlp_co)

    def back(which, s, tt, h, dy):
        half = s.shape[0]
        dh, dau = call(
            functools.partial(nbwd_kernel, which), "nbwd_pc"[: 6 + which],
            [sc, s, tt, h, dy, gain2, amT], [((half, width), F32), ((half, wide), BF)], flops=2 * half * 256 * width,
        )
        return dh, dau, to_core(dau)

    grad_outs = [((RK, qw), F32), ((RK, quarter), F32), ((2 * RK, quarter), F32)]
    dh_c, da_c, da_co = back(1, sd_c, td_c, h_c, dy_c)
    rc = 2 * CLEN
    dqp_c, dkvp_c, dfar, gao_c, gbo_c, gam_c = call(
        abwd_c_kernel, "abwd_c",
        [sc, da_c, da_co, n2_c, n2_co, o_c, w_out, aoT, bo, p_c, q[PLEN:], k[PLEN:], v[PLEN:], far, cos[PLEN:], sin[PLEN:]],
        [((rc, qw), BF), ((rc, 2 * kvw), BF), ((CONT_DEV, PLEN, 2 * kvw), F32)] + grad_outs,
        scratch=[VM((2, hc, width), BF), VM((rc, qw), BF), VM((rc, qw), BF), VM((rc, 2 * kvw), F32)],
        flops=2 * rc * width * qw * 3,
    )
    slot = jnp.arange(n_dp, dtype=jnp.int32)[:, None, None]
    scatter = sum(jnp.where(slot == partners[j], dfar[j][None], 0.0) for j in range(CONT_DEV)).astype(BF)
    own = lax.psum_scatter(scatter.reshape(n_dp * PLEN, 2 * kvw), "dp", scatter_dimension=0, tiled=True)

    dh_p, da_p, da_po = back(0, sd_p, td_p, h_p, dy_p)
    dqp_p, dkv_p, gao_p, gbo_p, gam_p = call(
        abwd_p_kernel, "abwd_p",
        [sc, da_p, da_po, n2_p, n2_po, o_p, w_out, aoT, bo, p_p, q[:PLEN], k[:PLEN], v[:PLEN], cos[:PLEN], sin[:PLEN]],
        [((PLEN, qw), BF), ((PLEN, 2 * kvw), F32)] + grad_outs,
        scratch=[VM((2, hp, width), BF), VM((PLEN, qw), BF), VM((PLEN, qw), BF)],
        flops=2 * PLEN * width * qw * 3,
    )

    far_wide = width + 2 * LANE
    gq = [((RK, qw), F32), ((RK, 2 * kvw), F32)]
    mine, other, gbq_c, gbkv_c = call(
        dn1_c_kernel, "dn1_c",
        [sc, dqp_c, dkvp_c, u[PLEN:], w_query, wkv, bq, bkv],
        [((hc, far_wide), BF)] * 2 + gq, scratch=[VM((2, hc, far_wide), BF)], flops=2 * rc * width * (qw + 2 * kvw),
    )
    s1_c, t1_c = tensor_sum(mine, other)
    mine, other, gbq_p, gbkv_p = call(
        dn1_p_kernel, "dn1_p",
        [sc, dqp_p, dkv_p, own, u[:PLEN], w_query, wkv, bq, bkv, cos[:PLEN], sin[:PLEN]],
        [((hp, far_wide), BF)] * 2 + gq, scratch=[VM((2, hp, far_wide), BF), VM((PLEN, 2 * kvw), BF)],
        flops=2 * PLEN * width * (qw + 2 * kvw),
    )
    s1_p, t1_p = tensor_sum(mine, other)

    def last(which, s, tt, x, dh):
        half = s.shape[0]
        (out,) = call(
            functools.partial(fin_kernel, which), "fin_pc"[: 5 + which],
            [sc, s, tt, x, dh, gain1, aT], [((half, far_wide), BF)], flops=2 * half * 256 * width,
        )
        return out, to_core(out)

    tg_p = join(*last(0, s1_p, t1_p, x_p, dh_p))
    tg_c = join(*last(1, s1_c, t1_c, x_c, dh_c))
    tokens_grad = jnp.concatenate([tg_p[:, :width], tg_c[:, :width]], 0)
    duq = jnp.concatenate([tg_p[:, width : width + 3 * RK], tg_c[:, width : width + 3 * RK]], 0)

    def finish(which, s, tt, h):
        half = s.shape[0]
        (out,) = call(
            functools.partial(out_kernel, which), "out_pc"[: 5 + which],
            [sc, s, tt, h, bd], [((half, wide), BF)], flops=2 * half * 256 * width,
        )
        return out, to_core(out)

    out_p = join(*finish(0, sm_p, tm_p, h_p))
    out_c = join(*finish(1, sm_c, tm_c, h_c))
    output = jnp.concatenate([out_p[:, :width], out_c[:, :width]], 0)
    ud = jnp.concatenate([out_p[:, width : width + RK], out_c[:, width : width + RK]], 0)

    dyq = lax.dynamic_slice_in_dim(cotangent, t * quarter, quarter, 1)
    gbd = dr(ud, dyq)
    gaT = dr(duq, n1q)
    gam = gam_p + gam_c
    early = jnp.concatenate(
        [gbg_p + gbg_c, gbu_p + gbu_c, gad_p + gad_c, gao_p + gao_c, gbo_p + gbo_c, gbd, gam[:RK], gam[RK:]], axis=1
    ).astype(BF)
    late = jnp.concatenate([gbq_p + gbq_c, gbkv_p + gbkv_c, gaT[:RK], gaT[RK : 2 * RK], gaT[2 * RK :]], axis=1).astype(BF)
    early = lax.psum(early, "dp")
    late = lax.psum(late, "dp")
    cuts = np.cumsum([hidden, hidden, hidden, qw])
    grad_b_mlp = early[:, : 2 * hidden].astype(F32)
    grad_a_down = early[:, cuts[1] : cuts[2]].astype(F32)
    grad_a_out = early[:, cuts[2] : cuts[3]].astype(F32)
    grad_b_query = late[:, :qw].astype(F32)
    grad_b_kv = late[:, qw : qw + 2 * kvw].astype(F32)

    def gather_quarters(v):
        return lax.all_gather(v, "tensor", axis=0, tiled=False)

    eq = gather_quarters(early[:, cuts[3] :])
    lq = gather_quarters(late[:, qw + 2 * kvw :])

    def columns(g, i):
        return jnp.transpose(g[:, :, i * quarter : (i + 1) * quarter], (1, 0, 2)).reshape(RK, width).astype(F32)

    grad_b_out = columns(eq, 0)
    grad_b_down = columns(eq, 1)
    grad_amT = jnp.concatenate([columns(eq, 2), columns(eq, 3)], axis=0)
    grad_aT = jnp.concatenate([columns(lq, 0), columns(lq, 1), columns(lq, 2)], axis=0)
    return (
        output,
        tokens_grad,
        grad_aT.reshape(3, NA, R, width).transpose(3, 0, 1, 2),
        grad_b_query.reshape(b_query.shape),
        grad_b_kv.reshape(b_kv.shape),
        grad_a_out.reshape(NA, R, qw).transpose(2, 0, 1),
        grad_b_out.reshape(b_out.shape),
        grad_amT.reshape(2, NA, R, width).transpose(3, 0, 1, 2),
        grad_b_mlp.reshape(b_mlp.shape),
        grad_a_down.reshape(NA, R, hidden).transpose(2, 0, 1),
        grad_b_down.reshape(b_down.shape),
    )


def solution(mesh):
    in_specs = (
        P("dp", None), P("dp", None), P(), P(), P(None, "tensor"), P(None, None, "tensor"), P("tensor", None),
        P(None, None, "tensor"), P("tensor", None), P(), P(None, None, "tensor"), P(None, None, None, "tensor"),
        P("tensor", None, None), P(), P(), P(None, None, None, "tensor"), P("tensor", None, None), P(),
        P("dp"), P("dp"), P(),
    )
    out_specs = (
        P("dp", None), P("dp", None), P(), P(None, None, "tensor"), P(None, None, None, "tensor"),
        P("tensor", None, None), P(), P(), P(None, None, None, "tensor"), P("tensor", None, None), P(),
    )
    return jax.shard_map(shards, mesh=mesh, in_specs=in_specs, out_specs=out_specs, check_vma=False)
```

time: 934 us -> 462 us (0.49)
  waiting for transfers between devices: 458 us -> 139 us
  matrix products: 213 us -> 2.34 us
  Pallas kernels: 0 us -> 181 us
  blocking collectives: 104 us -> 8.59 us
  other arithmetic: 82.7 us -> 28.4 us
  local copies, waits for them, and re-layouts: 50.9 us -> 71.2 us
    psum x5 -> x1, waiting for transfers between devices: 368 us -> 77.2 us  [shards(): late = lax.psum(late, 'dp')]
    dot_general x49 -> x2, matrix products: 213 us -> 2.34 us  [dr(): lax.dot_general(a, b, (((0,), (0,)), ((), ())), preferred_element_type=F32)]
    pallas_call x0 -> x13, Pallas kernels: none -> 181 us  [the longest x12 113 us: call(): pl.pallas_call(kernel, out_shape=[jax.ShapeDtypeStruct(s, d) for s, d in...]
    unnamed x9 -> x3, waiting for transfers between devices: 90 us -> 0.05 us
    ppermute x0 -> x18, waiting for transfers between devices: none -> 60.9 us  [the longest x6 59.6 us: to_chip(): return lax.ppermute(v, 'tensor', chip_pairs)]
    all_gather x2 -> x1, blocking collectives: 68 us -> 8.59 us  [gather_quarters(): return lax.all_gather(v, 'tensor', axis=0, tiled=False)]
    psum x1 -> x0, blocking collectives: 35.7 us -> none  [shards(): lax.psum(grad_b_kv.astype(jnp.bfloat16), 'dp').astype(jnp.float32)]
    reduce_sum x6 -> x0, other arithmetic: 27.7 us -> none  [the longest x1 11.7 us: shards(): total = jnp.sum(weight, axis=-1, keepdims=True)]
  transfers between devices with their start and end apart: 7 -> 21, of which waited for: 7 -> 9; matrix products, arithmetic and copies ran while one was open for 14% -> 11% of each run, Pallas kernels for 0% -> 19%
where the time goes in v1:
time: 462 us; the launch traced here: 454 us
  Pallas kernels  181 us (39%)
  waiting for transfers between devices  139 us (30%)
  local copies, waits for them, and re-layouts  71.2 us (15%)
  other arithmetic  28.4 us (6%)
  between operations  15.5 us (3%)
  starting transfers between devices  8.6 us (2%)
  blocking collectives  8.59 us (2%)
    pallas_call x12, Pallas kernels, call(): pl.pallas_call(kernel, out_shape=[jax.ShapeDtypeStruct(s, d) for s, d in...  113 us
    psum x1, waiting for transfers between devices, shards(): late = lax.psum(late, 'dp')  77.2 us
    pallas_call x1, Pallas kernels, front(): pl.pallas_call(functools.partial(front_kernel, n_dp), out_shape=[jax.Shap...  68.2 us
    ppermute x6, waiting for transfers between devices, to_chip(): return lax.ppermute(v, 'tensor', chip_pairs)  59.6 us
    unnamed x136, local copies, waits for them, and re-layouts  31.5 us
  transfers between devices with their start and end apart: 21, of which 9 were waited for; matrix products, arithmetic and copies ran while one was open for 11% of the time, Pallas kernels for 19%

profile of v1, /device:TPU:0, one launch (start us, length us, event | category | flops | bytes accessed | tf_op | source)
XLA Modules:
  0.0 454.4 jit_solution(8672420048650108281)
XLA Ops:
  9.5 2.3 copy.64
  14.1 0.9 concatenate.75.clone.adp_h
  15.6 68.2 %front.1 = (bf16[640,512]{1,0:T(8,128)(2,1)}, bf16[640,512]{1,0:T(8,128)(2,1)}, bf16[640,256]{1,0:T(8,128)(2,1)}, bf16[640,192]{1,0:T(8,128)(2,1)}, bf16[2,512,7...) custom-call(s32[8]{0:T(128)} %pad_add_fusion.sc, ...), custom_call_target="tpu_custom_call" | custom-call | flops 10737418240 | bytes 41943040 | tf_op jit(solution)/shard_map/front/pallas_call | solution.py:832
  83.8 2.3 slice.172.dact
  86.8 17.4 %copy.53 = bf16[256,8,2,2048]{3,1,2,0:T(8,128)(2,1)} copy(bf16[256,8,2,2048]{3,2,1,0:T(2,128)(2,1)} %bitcast.104) | data formatting | bytes 33554432
  104.2 1.0 copy.54
  105.8 1.1 dynamic-slice_bitcast_fusion.2
  106.9 25.7 %mlp_pc.1 = (bf16[128,2176]{1,0:T(8,128)(2,1)}, bf16[128,2176]{1,0:T(8,128)(2,1)}, bf16[128,2176]{1,0:T(8,128)(2,1)}, bf16[128,2176]{1,0:T(8,128)(2,1)}, f32[64,...) custom-call(s32[8]{0:T(128)} %concatenate.70.sc, bf16[128,2176]{1,0:T(8,128)(2,1)} %get-tuple-element.120.mine.n2_mine, ...), custom_call_target="tpu_custom_call" | custom-call | flops 10737418240 | bytes 49774624 | tf_op jit(solution)/shard_map/mlp_pc/pallas_call | solution.py:67
  132.6 1.1 collective-permute-start.9
  133.7 1.3 slice.169.dact
  135.7 1.3 dynamic-slice_bitcast_fusion
  136.9 34.4 %mlp_p.1 = (bf16[192,2176]{1,0:T(8,128)(2,1)}, bf16[192,2176]{1,0:T(8,128)(2,1)}, bf16[192,2176]{1,0:T(8,128)(2,1)}, bf16[192,2176]{1,0:T(8,128)(2,1)}, f32[64,2...) custom-call(s32[8]{0:T(128)} %concatenate.70.sc, bf16[192,2176]{1,0:T(8,128)(2,1)} %get-tuple-element.116.mine.n2_mine, ...), custom_call_target="tpu_custom_call" | custom-call | flops 16106127360 | bytes 51986464 | tf_op jit(solution)/shard_map/mlp_p/pallas_call | solution.py:67
  172.8 1.5 fusion.25
  174.3 1.7 slice.182.o_ref
  176.0 1.7 slice.183.q_ref
  178.2 0.9 constant_dynamic-slice_fusion.3.dy_ref
  179.2 2.2 constant_dynamic-slice_fusion.1.x_ref
  181.4 1.2 add_convert_fusion.4.s_ref
  184.7 12.9 %collective-permute-done.10.t_ref = bf16[128,2176]{1,0:T(8,128)(2,1)S(1)} collective-permute-done((bf16[128,2176]{1,0:T(8,128)(2,1)S(1)}, bf16[128,2176]{1,0:T(8,128)(2,1)S(1)}, u32[]{:S(2)}, u32[]{:S(2)}) %collective-permute-start.10) | collective-permute-done | bytes 557088 | tf_op jit(solution)/shard_map/ppermute | solution.py:893
  198.4 3.7 nbwd_pc.1
  205.1 9.6 %abwd_c.1 = (bf16[256,512]{1,0:T(8,128)(2,1)}, bf16[256,256]{1,0:T(8,128)(2,1)}, f32[2,384,256]{2,1,0:T(8,128)}, f32[64,512]{1,0:T(8,128)}, f32[64,512]{1,0:T(8,128)}, /*index=5*/f32[128,512]{1,0:T(8,128)}) custom-call(s32[8]{0:T(128)} %concatenate.70.sc, bf16[128,2176]{1,0:T(8,128)(2,1)} %get-tuple-element.83.mine, bf16[128,2176]{1,0:T(8,128)(2,1)} %copy-done.28, ...), custom_call_target="tpu_custom_call" | custom-call | flops 1610612736 | bytes 9764896 | tf_op jit(solution)/shard_map/abwd_c/pallas_call | solution.py:67
  214.8 1.2 slice_bitcast_fusion.1
  215.9 2.0 fusion.1
  218.2 1.4 add_convert_fusion.1.s_ref
  220.2 1.2 add_convert_fusion.5.s_ref
  221.4 1.6 collective-permute-start.4
  223.8 17.4 %collective-permute-done.7.t_ref = bf16[192,2176]{1,0:T(8,128)(2,1)S(1)} collective-permute-done((bf16[192,2176]{1,0:T(8,128)(2,1)S(1)}, bf16[192,2176]{1,0:T(8,128)(2,1)S(1)}, u32[]{:S(2)}, u32[]{:S(2)}) %collective-permute-start.7) | collective-permute-done | bytes 835616 | tf_op jit(solution)/shard_map/ppermute | solution.py:893
  241.2 0.9 copy-done.19
  242.1 4.7 %nbwd_p.1 = (f32[192,2048]{1,0:T(8,128)}, bf16[192,2176]{1,0:T(8,128)(2,1)}) custom-call(s32[8]{0:T(128)} %concatenate.70.sc, bf16[192,2176]{1,0:T(8,128)(2,1)} %copy-done.4, bf16[192,2176]{1,0:T(8,128)(2,1)} %copy-done.19, f32[192,2048]{1,0:T(8,128)} %get-tuple-element.67.h_ref, bf16[192,2048]{1,0:T(8,128)(2,1)} %constant_dynamic-slice_fusion.3.dy_ref, ...), custom_call_target="tpu_custom_call" | custom-call | flops 201326592 | bytes 6967328 | tf_op jit(solution)/shard_map/nbwd_p/pallas_call | solution.py:67
  247.0 2.0 constant_dynamic-slice_fusion.x_ref
  250.5 1.6 slice.191.u_ref
  252.1 1.6 slice.193.u_ref
  254.5 2.8 out_pc.1
  258.3 4.4 dn1_c.1
  262.8 7.4 %collective-permute-done.1.t_ref = bf16[192,2176]{1,0:T(8,128)(2,1)S(1)} collective-permute-done((bf16[192,2176]{1,0:T(8,128)(2,1)S(1)}, bf16[192,2176]{1,0:T(8,128)(2,1)S(1)}, u32[]{:S(2)}, u32[]{:S(2)}) %collective-permute-start.1) | collective-permute-done | bytes 835616 | tf_op jit(solution)/shard_map/ppermute | solution.py:893
  270.2 0.9 copy-done.22
  271.2 3.3 out_p.1
  274.4 10.8 %abwd_p.1 = (bf16[384,512]{1,0:T(8,128)(2,1)}, f32[384,256]{1,0:T(8,128)}, f32[64,512]{1,0:T(8,128)}, f32[64,512]{1,0:T(8,128)}, f32[128,512]{1,0:T(8,128)}) custom-call(s32[8]{0:T(128)} %concatenate.70.sc, bf16[192,2176]{1,0:T(8,128)(2,1)} %get-tuple-element.74.mine, bf16[192,2176]{1,0:T(8,128)(2,1)} %collective-permute-done.8.other, ...), custom_call_target="tpu_custom_call" | custom-call | flops 2415919104 | bytes 10027040 | tf_op jit(solution)/shard_map/abwd_p/pallas_call | solution.py:67
  285.3 5.4 %dn1_p.1 = (bf16[192,2304]{1,0:T(8,128)(2,1)}, bf16[192,2304]{1,0:T(8,128)(2,1)}, f32[64,512]{1,0:T(8,128)}, f32[64,256]{1,0:T(8,128)}) custom-call(s32[8]{0:T(128)} %concatenate.70.sc, bf16[384,512]{1,0:T(8,128)(2,1)} %get-tuple-element.79.dqp, f32[384,256]{1,0:T(8,128)} %get-tuple-element.80.dkv, bf16[384,256]{1,0:T(8,128)(2,1)} %reduce-scatter.2.cloned.1.call-done.own, ...), custom_call_target="tpu_custom_call" | custom-call | flops 1207959552 | bytes 6733856 | tf_op jit(solution)/shard_map/dn1_p/pallas_call | solution.py:67
  291.6 0.8 copy-done.27
  292.4 1.2 add_convert_fusion.3.s_ref
  294.4 1.6 collective-permute-start.13
  296.1 2.2 maximum_select_fusion.1
  299.6 10.3 %collective-permute-done.16.t_ref = bf16[128,2304]{1,0:T(8,128)(2,1)S(1)} collective-permute-done((bf16[128,2304]{1,0:T(8,128)(2,1)S(1)}, bf16[128,2304]{1,0:T(8,128)(2,1)S(1)}, u32[]{:S(2)}, u32[]{:S(2)}) %collective-permute-start.16) | collective-permute-done | bytes 589856 | tf_op jit(solution)/shard_map/ppermute | solution.py:893
  310.7 3.6 fin_pc.1
  314.3 2.0 fusion.2
  316.3 11.6 %collective-permute-done.13.t_ref = bf16[192,2304]{1,0:T(8,128)(2,1)S(1)} collective-permute-done((bf16[192,2304]{1,0:T(8,128)(2,1)S(1)}, bf16[192,2304]{1,0:T(8,128)(2,1)S(1)}, u32[]{:S(2)}, u32[]{:S(2)}) %collective-permute-start.13) | collective-permute-done | bytes 884768 | tf_op jit(solution)/shard_map/ppermute | solution.py:893
  327.9 0.9 copy-done.18
  328.8 4.3 fin_p.1
  334.3 0.9 copy-done
  338.5 1.0 slice-done.2
  339.5 1.8 pad_maximum_fusion
  341.5 1.0 slice-done
  342.5 1.8 pad_maximum_fusion.1
  344.4 77.2 %all-reduce.5.cloned.1.call-done = (bf16[64,2304]{1,0:T(8,128)(2,1)}, bf16[64,8704]{1,0:T(8,128)(2,1)}) async-done(((bf16[64,2304]{1,0:T(8,128)(2,1)}, bf16[64,8704]{1,0:T(8,128)(2,1)}), (bf16[64,2304]{1,0:T(8,128)(2,1)}, bf16[64,8704]{1,0:T(8,128)(2,1)})) %all-reduce.5.cloned.1.call-update) | async-done | bytes 1409040 | tf_op jit(solution)/shard_map/psum | solution.py:1047
  421.6 1.8 fusion.22
  423.4 1.1 slice_convert_fusion
  425.4 8.6 %all-gather = bf16[256,1536]{1,0:T(8,128)(2,1)S(1)} all-gather(bf16[64,1536]{1,0:T(8,128)(2,1)S(1)} %slice.228), channel_id=2, replica_groups=mesh['dp'=8,'tensor'=4] {'tensor'}, dimensions={0}, use_global_device_ids=true | all-gather | bytes 983040 | tf_op jit(solution)/shard_map/all_gather | solution.py:1056
  434.9 1.9 reshape.168
  439.7 1.3 convert_bitcast_fusion
  441.6 1.4 convert_bitcast_fusion.3
  443.5 1.1 convert_bitcast_fusion.1
  445.0 1.2 reshape.166
  446.4 1.2 reshape.169
  (223 shorter events, 34.1 us)
Async XLA Ops:
  7.2 4.7 %copy-start.54 = (bf16[2048]{0:T(1024)(128)(2,1)S(1)}, bf16[2048]{0:T(1024)(128)(2,1)}, u32[]{:S(2)}) copy-start(bf16[2048]{0:T(1024)(128)(2,1)} %param.25) | copy-start | bytes 12292
  7.2 5.3 %copy-start.55 = (bf16[2048]{0:T(1024)(128)(2,1)S(1)}, bf16[2048]{0:T(1024)(128)(2,1)}, u32[]{:S(2)}) copy-start(bf16[2048]{0:T(1024)(128)(2,1)} %param.26) | copy-start | bytes 12292
  7.2 5.9 %copy-start.16 = (bf16[2048,4,16]{0,2,1:T(8,128)(2,1)S(1)}, bf16[2048,4,16]{0,2,1:T(8,128)(2,1)}, u32[]{:S(2)}) copy-start(bf16[2048,4,16]{0,2,1:T(8,128)(2,1)} %param.39) | copy-start | bytes 786436
  7.2 6.1 %copy-start.57 = (s32[16]{0:T(128)S(1)}, s32[16]{0:T(128)}, u32[]{:S(2)}) copy-start(s32[16]{0:T(128)} %param.43) | copy-start | bytes 196
  7.2 278.1 %reduce-scatter.2.cloned.1.call-start = ((), (), s32[]{:S(2)}) async-start(), calls=%async_computation.1 | async-start | bytes 1769472 | tf_op jit(solution)/shard_map/reduce_scatter | solution.py:985
  8.7 6.3 %copy-start.40 = (bf16[8,8,2,128]{3,1,2,0:T(8,128)(2,1)}, bf16[8,8,2,128]{3,1,2,0:T(8,128)(2,1)S(1)}, u32[]{:S(2)}) copy-start(bf16[8,8,2,128]{3,1,2,0:T(8,128)(2,1)S(1)} %copy.65) | copy-start | bytes 98308
  9.5 5.5 %copy-start.56 = (s32[2]{0:T(128)S(1)}, s32[2]{0:T(128)}, u32[]{:S(2)}) copy-start(s32[2]{0:T(128)} %param.42) | copy-start | bytes 28
  83.8 2.4 copy-start.45
  86.8 17.4 %copy-start.32 = (bf16[4,16,2,2048]{3,2,1,0:T(2,128)(2,1)S(1)}, bf16[4,16,2,2048]{3,2,1,0:T(2,128)(2,1)}, u32[]{:S(2)}) copy-start(bf16[4,16,2,2048]{3,2,1,0:T(2,128)(2,1)} %param.38) | copy-start | bytes 1572868
  86.8 19.0 %copy-start.15 = (bf16[2,128,2176]{2,1,0:T(8,128)(2,1)S(1)}, bf16[2,128,2176]{2,1,0:T(8,128)(2,1)}, u32[]{:S(2)}) copy-start(bf16[2,128,2176]{2,1,0:T(8,128)(2,1)} %get-tuple-element.68) | copy-start | bytes 3342340
  106.9 26.7 %copy-start.7 = (bf16[640,2048]{1,0:T(8,128)(2,1)S(1)}, bf16[640,2048]{1,0:T(8,128)(2,1)}, u32[]{:S(2)}) copy-start(bf16[640,2048]{1,0:T(8,128)(2,1)} %get-tuple-element.63) | copy-start | bytes 7864324
  132.6 3.0 copy-start.13
  132.6 48.8 %collective-permute-start.9 = (bf16[128,2176]{1,0:T(8,128)(2,1)}, bf16[128,2176]{1,0:T(8,128)(2,1)}, u32[]{:S(2)}, u32[]{:S(2)}) collective-permute-start(bf16[128,2176]{1,0:T(8,128)(2,1)} %get-tuple-element.82), channel_id=1, source_target_pairs={{0,1},{1,0},{2,3},{3,2},{4,5},{5,4},{6,7},{7,6},{8,9},{9,8},{10,11... | collective-permute-start | bytes 1671176 | tf_op jit(solution)/shard_map/ppermute | solution.py:890
  136.9 35.1 %copy-start.14 = (bf16[640,2048]{1,0:T(8,128)(2,1)S(1)}, bf16[640,2048]{1,0:T(8,128)(2,1)}, u32[]{:S(2)}) copy-start(bf16[640,2048]{1,0:T(8,128)(2,1)} %dy_h.1) | copy-start | bytes 7864324
  171.3 46.9 %collective-permute-start.6 = (bf16[192,2176]{1,0:T(8,128)(2,1)}, bf16[192,2176]{1,0:T(8,128)(2,1)}, u32[]{:S(2)}, u32[]{:S(2)}) collective-permute-start(bf16[192,2176]{1,0:T(8,128)(2,1)} %get-tuple-element.73), channel_id=1, source_target_pairs={{0,1},{1,0},{2,3},{3,2},{4,5},{5,4},{6,7},{7,6},{8,9},{9,8},{10,11... | collective-permute-start | bytes 2506760 | tf_op jit(solution)/shard_map/ppermute | solution.py:890
  171.4 51.6 %collective-permute-start = (bf16[192,2176]{1,0:T(8,128)(2,1)}, bf16[192,2176]{1,0:T(8,128)(2,1)S(1)}, u32[]{:S(2)}, u32[]{:S(2)}) collective-permute-start(bf16[192,2176]{1,0:T(8,128)(2,1)} %get-tuple-element.66), channel_id=1, source_target_pairs={{0,1},{1,0},{2,3},{3,2},{4,5},{5,4},{6,7},{7,6},{8,9},{9,8},{10,11... | collective-permute-start | bytes 2506760 | tf_op jit(solution)/shard_map/ppermute | solution.py:890
  171.9 48.3 %collective-permute-start.3 = (bf16[128,2176]{1,0:T(8,128)(2,1)}, bf16[128,2176]{1,0:T(8,128)(2,1)}, u32[]{:S(2)}, u32[]{:S(2)}) collective-permute-start(bf16[128,2176]{1,0:T(8,128)(2,1)} %get-tuple-element.70), channel_id=1, source_target_pairs={{0,1},{1,0},{2,3},{3,2},{4,5},{5,4},{6,7},{7,6},{8,9},{9,8},{10,11... | collective-permute-start | bytes 1671176 | tf_op jit(solution)/shard_map/ppermute | solution.py:890
  177.7 3.7 copy-start.30
  179.2 4.7 %copy-start.36 = (f32[64,2048]{1,0:T(8,128)S(1)}, f32[64,2048]{1,0:T(8,128)}, u32[]{:S(2)}) copy-start(f32[64,2048]{1,0:T(8,128)} %get-tuple-element.102) | copy-start | bytes 1572868
  179.2 4.7 %copy-start.38 = (f32[64,2048]{1,0:T(8,128)S(1)}, f32[64,2048]{1,0:T(8,128)}, u32[]{:S(2)}) copy-start(f32[64,2048]{1,0:T(8,128)} %get-tuple-element.101) | copy-start | bytes 1572868
  182.6 15.1 %copy-start.12 = (bf16[128,2176]{1,0:T(8,128)(2,1)}, bf16[128,2176]{1,0:T(8,128)(2,1)S(1)}, u32[]{:S(2)}) copy-start(bf16[128,2176]{1,0:T(8,128)(2,1)S(1)} %add_convert_fusion.4.s_ref) | copy-start | bytes 1671172
  182.6 15.0 %collective-permute-start.10 = (bf16[128,2176]{1,0:T(8,128)(2,1)S(1)}, bf16[128,2176]{1,0:T(8,128)(2,1)S(1)}, u32[]{:S(2)}, u32[]{:S(2)}) collective-permute-start(bf16[128,2176]{1,0:T(8,128)(2,1)S(1)} %add_convert_fusion.4.s_ref), channel_id=1, source_target_pairs={{0,2},{1,3},{2,0},{3,1},{4,6},{5,7},{6,4},{7,5},{8,10},{9,11},{10,... | collective-permute-start | bytes 1671176 | tf_op jit(solution)/shard_map/ppermute | solution.py:893
  184.7 18.2 %copy-start.35 = (f32[64,2048]{1,0:T(8,128)S(1)}, f32[64,2048]{1,0:T(8,128)}, u32[]{:S(2)}) copy-start(f32[64,2048]{1,0:T(8,128)} %get-tuple-element.104) | copy-start | bytes 1572868
  184.7 18.2 %copy-start.37 = (f32[64,2048]{1,0:T(8,128)S(1)}, f32[64,2048]{1,0:T(8,128)}, u32[]{:S(2)}) copy-start(f32[64,2048]{1,0:T(8,128)} %get-tuple-element.103) | copy-start | bytes 1572868
  202.2 2.2 collective-permute-start.11
  218.0 203.6 %all-reduce.5.cloned.1.call-start = ((), (), s32[]{:S(2)}) async-start(), calls=%async_computation.3 | async-start | bytes 2818048 | tf_op jit(solution)/shard_map/psum | solution.py:1047
  218.2 4.8 %copy-start.20 = (bf16[192,2176]{1,0:T(8,128)(2,1)S(1)}, bf16[192,2176]{1,0:T(8,128)(2,1)}, u32[]{:S(2)}) copy-start(bf16[192,2176]{1,0:T(8,128)(2,1)} %get-tuple-element.65) | copy-start | bytes 2506756
  219.7 3.6 copy-start.4
  219.7 21.5 %collective-permute-start.7 = (bf16[192,2176]{1,0:T(8,128)(2,1)S(1)}, bf16[192,2176]{1,0:T(8,128)(2,1)S(1)}, u32[]{:S(2)}, u32[]{:S(2)}) collective-permute-start(bf16[192,2176]{1,0:T(8,128)(2,1)S(1)} %add_convert_fusion.1.s_ref), channel_id=1, source_target_pairs={{0,2},{1,3},{2,0},{3,1},{4,6},{5,7},{6,4},{7,5},{8,10},{9,11},{10,... | collective-permute-start | bytes 2506760 | tf_op jit(solution)/shard_map/ppermute | solution.py:893
  221.4 25.4 %copy-start.11 = (bf16[128,2176]{1,0:T(8,128)(2,1)}, bf16[128,2176]{1,0:T(8,128)(2,1)S(1)}, u32[]{:S(2)}) copy-start(bf16[128,2176]{1,0:T(8,128)(2,1)S(1)} %add_convert_fusion.5.s_ref) | copy-start | bytes 1671172
  221.4 33.0 %collective-permute-start.4 = (bf16[128,2176]{1,0:T(8,128)(2,1)S(1)}, bf16[128,2176]{1,0:T(8,128)(2,1)}, u32[]{:S(2)}, u32[]{:S(2)}) collective-permute-start(bf16[128,2176]{1,0:T(8,128)(2,1)S(1)} %add_convert_fusion.5.s_ref), channel_id=1, source_target_pairs={{0,2},{1,3},{2,0},{3,1},{4,6},{5,7},{6,4},{7,5},{8,10},{9,11},{10,... | collective-permute-start | bytes 1671176 | tf_op jit(solution)/shard_map/ppermute | solution.py:893
  223.3 23.6 %copy-start.5 = (bf16[192,2176]{1,0:T(8,128)(2,1)}, bf16[192,2176]{1,0:T(8,128)(2,1)S(1)}, u32[]{:S(2)}) copy-start(bf16[192,2176]{1,0:T(8,128)(2,1)S(1)} %add_convert_fusion.2.s_ref) | copy-start | bytes 2506756
  223.3 47.0 %collective-permute-start.1 = (bf16[192,2176]{1,0:T(8,128)(2,1)S(1)}, bf16[192,2176]{1,0:T(8,128)(2,1)S(1)}, u32[]{:S(2)}, u32[]{:S(2)}) collective-permute-start(bf16[192,2176]{1,0:T(8,128)(2,1)S(1)} %add_convert_fusion.2.s_ref), channel_id=1, source_target_pairs={{0,2},{1,3},{2,0},{3,1},{4,6},{5,7},{6,4},{7,5},{8,10},{9,11},{10,... | collective-permute-start | bytes 2506760 | tf_op jit(solution)/shard_map/ppermute | solution.py:893
  242.1 6.9 %copy-start.24 = (bf16[640,512]{1,0:T(8,128)(2,1)S(1)}, bf16[640,512]{1,0:T(8,128)(2,1)}, u32[]{:S(2)}) copy-start(bf16[640,512]{1,0:T(8,128)(2,1)} %get-tuple-element.75) | copy-start | bytes 1966084
  246.8 2.9 copy-start.23
  246.9 6.8 %copy-start.33 = (f32[64,2048]{1,0:T(8,128)S(1)}, f32[64,2048]{1,0:T(8,128)}, u32[]{:S(2)}) copy-start(f32[64,2048]{1,0:T(8,128)} %get-tuple-element.106) | copy-start | bytes 1572868
  246.9 6.8 %copy-start.34 = (f32[64,2048]{1,0:T(8,128)S(1)}, f32[64,2048]{1,0:T(8,128)}, u32[]{:S(2)}) copy-start(f32[64,2048]{1,0:T(8,128)} %get-tuple-element.105) | copy-start | bytes 1572868
  246.9 27.6 %collective-permute-start.8 = (bf16[192,2176]{1,0:T(8,128)(2,1)}, bf16[192,2176]{1,0:T(8,128)(2,1)}, u32[]{:S(2)}, u32[]{:S(2)}) collective-permute-start(bf16[192,2176]{1,0:T(8,128)(2,1)} %get-tuple-element.74.mine), channel_id=1, source_target_pairs={{0,1},{1,0},{2,3},{3,2},{4,5},{5,4},{6,7},{7,6},{8,9},{9,8},{10,11... | collective-permute-start | bytes 2506760 | tf_op jit(solution)/shard_map/ppermute | solution.py:890
  254.5 3.1 copy-start.41
  257.2 34.0 %collective-permute-start.5 = (bf16[128,2176]{1,0:T(8,128)(2,1)}, bf16[128,2176]{1,0:T(8,128)(2,1)S(1)}, u32[]{:S(2)}, u32[]{:S(2)}) collective-permute-start(bf16[128,2176]{1,0:T(8,128)(2,1)} %out_pc.1), channel_id=1, source_target_pairs={{0,1},{1,0},{2,3},{3,2},{4,5},{5,4},{6,7},{7,6},{8,9},{9,8},{10,11... | collective-permute-start | bytes 1671176 | tf_op jit(solution)/shard_map/ppermute | solution.py:890
  262.7 28.8 %collective-permute-start.15 = (bf16[128,2304]{1,0:T(8,128)(2,1)}, bf16[128,2304]{1,0:T(8,128)(2,1)S(1)}, u32[]{:S(2)}, u32[]{:S(2)}) collective-permute-start(bf16[128,2304]{1,0:T(8,128)(2,1)} %get-tuple-element.94), channel_id=1, source_target_pairs={{0,1},{1,0},{2,3},{3,2},{4,5},{5,4},{6,7},{7,6},{8,9},{9,8},{10,11... | collective-permute-start | bytes 1769480 | tf_op jit(solution)/shard_map/ppermute | solution.py:890
  274.4 21.6 %collective-permute-start.2 = (bf16[192,2176]{1,0:T(8,128)(2,1)}, bf16[192,2176]{1,0:T(8,128)(2,1)}, u32[]{:S(2)}, u32[]{:S(2)}) collective-permute-start(bf16[192,2176]{1,0:T(8,128)(2,1)} %out_p.1), channel_id=1, source_target_pairs={{0,1},{1,0},{2,3},{3,2},{4,5},{5,4},{6,7},{7,6},{8,9},{9,8},{10,11... | collective-permute-start | bytes 2506760 | tf_op jit(solution)/shard_map/ppermute | solution.py:890
  285.3 6.0 %copy-start.10 = (bf16[128,2176]{1,0:T(8,128)(2,1)S(1)}, bf16[128,2176]{1,0:T(8,128)(2,1)}, u32[]{:S(2)}) copy-start(bf16[128,2176]{1,0:T(8,128)(2,1)} %out_pc.1) | copy-start | bytes 1671172
  290.7 3.4 copy-start.17
  290.7 3.4 collective-permute-start.12
  291.5 2.9 copy-start.1
  293.6 4.6 %copy-start.8 = (bf16[128,2304]{1,0:T(8,128)(2,1)}, bf16[128,2304]{1,0:T(8,128)(2,1)S(1)}, u32[]{:S(2)}) copy-start(bf16[128,2304]{1,0:T(8,128)(2,1)S(1)} %add_convert_fusion.3.s_ref) | copy-start | bytes 1769476
  293.6 2.5 copy-start.6
  293.6 16.3 %collective-permute-start.16 = (bf16[128,2304]{1,0:T(8,128)(2,1)S(1)}, bf16[128,2304]{1,0:T(8,128)(2,1)S(1)}, u32[]{:S(2)}, u32[]{:S(2)}) collective-permute-start(bf16[128,2304]{1,0:T(8,128)(2,1)S(1)} %add_convert_fusion.3.s_ref), channel_id=1, source_target_pairs={{0,2},{1,3},{2,0},{3,1},{4,6},{5,7},{6,4},{7,5},{8,10},{9,11},{10,... | collective-permute-start | bytes 1769480 | tf_op jit(solution)/shard_map/ppermute | solution.py:893
  294.4 3.9 copy-start.2
  294.4 3.9 copy-start.47
  294.4 3.9 copy-start.51
  294.4 4.5 copy-start.46
  294.4 4.5 copy-start.50
  294.4 33.4 %collective-permute-start.13 = (bf16[192,2304]{1,0:T(8,128)(2,1)S(1)}, bf16[192,2304]{1,0:T(8,128)(2,1)S(1)}, u32[]{:S(2)}, u32[]{:S(2)}) collective-permute-start(bf16[192,2304]{1,0:T(8,128)(2,1)S(1)} %add_convert_fusion.s_ref), channel_id=1, source_target_pairs={{0,2},{1,3},{2,0},{3,1},{4,6},{5,7},{6,4},{7,5},{8,10},{9,11},{10,... | collective-permute-start | bytes 2654216 | tf_op jit(solution)/shard_map/ppermute | solution.py:893
  310.7 3.6 slice-start.1
  310.7 5.6 %copy-start.43 = (f32[128,512]{1,0:T(8,128)S(1)}, f32[128,512]{1,0:T(8,128)}, u32[]{:S(2)}) copy-start(f32[128,512]{1,0:T(8,128)} %get-tuple-element.112) | copy-start | bytes 786436
  310.7 5.6 %copy-start.44 = (f32[128,512]{1,0:T(8,128)S(1)}, f32[128,512]{1,0:T(8,128)}, u32[]{:S(2)}) copy-start(f32[128,512]{1,0:T(8,128)} %get-tuple-element.111) | copy-start | bytes 786436
  314.3 19.6 %collective-permute-start.17 = (bf16[128,2304]{1,0:T(8,128)(2,1)}, bf16[128,2304]{1,0:T(8,128)(2,1)S(1)}, u32[]{:S(2)}, u32[]{:S(2)}) collective-permute-start(bf16[128,2304]{1,0:T(8,128)(2,1)} %fin_pc.1), channel_id=1, source_target_pairs={{0,1},{1,0},{2,3},{3,2},{4,5},{5,4},{6,7},{7,6},{8,9},{9,8},{10,11... | collective-permute-start | bytes 1769480 | tf_op jit(solution)/shard_map/ppermute | solution.py:890
  328.8 5.1 %copy-start.9 = (bf16[128,2304]{1,0:T(8,128)(2,1)S(1)}, bf16[128,2304]{1,0:T(8,128)(2,1)}, u32[]{:S(2)}) copy-start(bf16[128,2304]{1,0:T(8,128)(2,1)} %fin_pc.1) | copy-start | bytes 1769476
  333.2 2.7 copy-start.3
  333.2 2.7 collective-permute-start.14
  338.2 103.4 %all-gather.4.cloned.1.call-start = ((), (), s32[]{:S(2)}) async-start(), calls=%async_computation.2 | async-start | bytes 1310720 | tf_op jit(solution)/shard_map/all_gather | solution.py:1056
  421.6 2.9 copy-start.42
  (19 other events, 22.0 us)
Sparse Core Ops, SparseCore 0:
  218.1 62.0 reduce-scatter.1
  338.3 83.1 all-reduce.4
  425.5 15.9 all-gather.3

commit v2 on v1

v2 whole, which is shorter than its diff:
```python
import functools
import math

import jax
import jax.numpy as jnp
import numpy as np
from jax import lax
from jax.experimental import pallas as pl
from jax.experimental.pallas import tpu as pltpu
from jax.sharding import PartitionSpec as P

HD = 64
R = 16
NA = 4
RK = NA * R
PLEN = 384
CLEN = 128
CONT_DEV = 2
ROWS = PLEN + CONT_DEV * CLEN
EPSILON = 1e-05
ROPE_BASE = 500000.0
MASKED_SCORE = -1e30

BF = jnp.bfloat16
F32 = jnp.float32
VM = pltpu.VMEM
LANE = 128


def dn(a, b):
    return jnp.dot(a, b, preferred_element_type=F32)


def dt(a, b):
    return lax.dot_general(a, b, (((1,), (1,)), ((), ())), preferred_element_type=F32)


def dr(a, b):
    return lax.dot_general(a, b, (((0,), (0,)), ((), ())), preferred_element_type=F32)


def sel_row(adapter):
    lane = lax.broadcasted_iota(jnp.int32, (1, RK), 1)
    return (lax.shift_right_logical(lane, 4) == adapter).astype(F32)


def swap_halves(v):
    lane = lax.broadcasted_iota(jnp.int32, v.shape, 1)
    return jnp.where((lane & 63) < 32, pltpu.roll(v, LANE - 32, 1), pltpu.roll(v, 32, 1))


def rot(v, cos, sin):
    return v * cos + swap_halves(v) * sin


def stack_heads(ref, r0, g):
    return jnp.concatenate(
        [ref[r0 : r0 + CLEN, (4 * g + h) * HD : (4 * g + h + 1) * HD] for h in range(4)], axis=0
    )


def softmax_low(s):
    top = jnp.max(s, axis=-1, keepdims=True)
    e = jnp.exp(s - top)
    return (e * (1.0 / jnp.sum(e, axis=-1, keepdims=True))).astype(BF)


def causal_tile():
    r = lax.broadcasted_iota(jnp.int32, (4 * CLEN, CLEN), 0) & (CLEN - 1)
    c = lax.broadcasted_iota(jnp.int32, (4 * CLEN, CLEN), 1)
    return c <= r


P_OFF = (0, 128, 384)


def norm_back(v, gain, upstream):
    inv = lax.rsqrt(jnp.mean(v * v, axis=-1, keepdims=True) + EPSILON)
    scaled = v * inv
    weighted = upstream * gain
    return inv * (weighted - scaled * jnp.mean(weighted * scaled, axis=-1, keepdims=True))


def put_dq(dq, dq_ref, r0, g):
    for h in range(4):
        dq_ref[r0 : r0 + CLEN, (4 * g + h) * HD : (4 * g + h + 1) * HD] = dq[h * CLEN : (h + 1) * CLEN]


def back_scores(p, dp):
    pf = p.astype(F32)
    return (pf * (dp - jnp.sum(pf * dp, axis=-1, keepdims=True))).astype(BF)


MESH = pl.DeviceIdType.MESH


def rows_loop(total, step, body):
    def one(i, carry):
        body(pl.multiple_of(i * step, step))
        return carry

    lax.fori_loop(0, total // step, one, 0)


def place():
    d = lax.axis_index("dp")
    t = lax.axis_index("tensor")
    return d, t


def remote(src, dst, send, recv, device):
    return pltpu.make_async_remote_copy(
        src_ref=src, dst_ref=dst, send_sem=send, recv_sem=recv, device_id=device, device_id_type=MESH
    )


def greet(d, t, n_dp):
    barrier = pltpu.get_barrier_semaphore()
    for device in [(d, t ^ 1), (d, t ^ 2)] + [((d + k) % n_dp, t) for k in range(1, n_dp)]:
        pl.semaphore_signal(barrier, inc=1, device_id=device, device_id_type=MESH)


def greeted(n_dp):
    pl.semaphore_wait(pltpu.get_barrier_semaphore(), n_dp + 1)


class Spread:
    def __init__(self, every, sems, d, t, hi):
        self.every, self.sems, self.d, self.t, self.hi = every, sems, d, t, hi
        self.z, self.x = d // 2, d % 2

    def across(self, z):
        block = z * 2 + self.x
        up_s, up_r, down_s, down_r, x_s, x_r = self.sems
        return remote(self.every.at[block], self.every.at[block], x_s.at[z], x_r.at[z], (self.d ^ 1, self.t))

    def along(self, z, s, up):
        block = z * 2 + self.x
        up_s, up_r, down_s, down_r, x_s, x_r = self.sems
        send, recv, step = (up_s, up_r, 2) if up else (down_s, down_r, -2)
        return remote(self.every.at[block], self.every.at[block], send.at[s], recv.at[s], (self.d + step, self.t))

    def start(self):
        self.across(self.z).start()

        @pl.when(self.z < self.hi - 1)
        def _():
            self.along(self.z, 1, True).start()

        @pl.when(self.z > 0)
        def _():
            self.along(self.z, 1, False).start()

    def hop(self, s):
        if s > self.hi - 1:
            return
        for up in (True, False):
            origin = self.z - s if up else self.z + s
            held = origin >= 0 if up else origin < self.hi
            further = self.z < self.hi - 1 if up else self.z > 0

            @pl.when(held)
            def _(origin=origin, up=up, further=further):
                self.along(origin, s, up).wait_recv()
                self.across(origin).start()
                if s + 1 <= self.hi - 1:

                    @pl.when(further)
                    def _():
                        self.along(origin, s + 1, up).start()

    def finish(self):
        for z in range(self.hi):
            across = self.across(z)
            across.wait_send()
            block = z * 2 + 1 - self.x
            up_s, up_r, down_s, down_r, x_s, x_r = self.sems
            remote(self.every.at[block], self.every.at[block], x_s.at[z], x_r.at[z], (self.d ^ 1, self.t)).wait_recv()
        for s in range(1, self.hi):
            for up in (True, False):
                origin = self.z - s + 1 if up else self.z + s - 1
                held = origin >= 0 if up else origin < self.hi
                further = self.z < self.hi - 1 if up else self.z > 0

                @pl.when(held & further)
                def _(origin=origin, up=up, s=s):
                    self.along(origin, s, up).wait_send()


class TensorSum:
    def __init__(self, snd, got, mine, theirs, sems, d, t):
        self.snd, self.got, self.mine, self.theirs, self.sems, self.t = snd, got, mine, theirs, sems, t
        self.lo = t % 2
        self.core = remote(snd.at[1 - self.lo], got, sems.at[0], sems.at[1], (d, t ^ 1))
        self.chip = remote(mine, theirs, sems.at[2], sems.at[3], (d, t ^ 2))

    def begin(self):
        self.core.start()

    def middle(self):
        self.core.wait_recv()

        def add(r):
            rows = pl.ds(r, 64)
            self.mine[rows] = (self.snd[self.lo, rows].astype(F32) + self.got[rows].astype(F32)).astype(BF)

        rows_loop(self.mine.shape[0], 64, add)
        self.chip.start()

    def end(self):
        self.chip.wait_recv()

    def drain(self):
        self.core.wait_send()
        self.chip.wait_send()


UNIT = (16, LANE)


def put_units(blocks, first, value):
    for b in range(value.shape[1] // LANE):
        for r in range(RK // 16):
            blocks[first + b * (RK // 16) + r] = value[r * 16 : (r + 1) * 16, b * LANE : (b + 1) * LANE]


class DirectReduce:
    def __init__(self, src, got, out, sems, d, t, n_dp):
        self.src, self.got, self.out, self.sems, self.d, self.t, self.n = src, got, out, sems, d, t, n_dp
        self.share = out.shape[0] // n_dp

    def part(self, d):
        return pl.ds(d * self.share, self.share)

    def to(self, k):
        peer = (self.d + k) % self.n
        return remote(self.src.at[self.part(peer)], self.got.at[k], self.sems[0].at[k], self.sems[1].at[k], (peer, self.t))

    def back(self, k):
        peer = (self.d + k) % self.n
        here = self.part(self.d)
        return remote(self.out.at[here], self.out.at[here], self.sems[2].at[k], self.sems[3].at[k], (peer, self.t))

    def from_back(self, k):
        peer = (self.d + self.n - k) % self.n
        there = self.part(peer)
        return remote(self.out.at[there], self.out.at[there], self.sems[2].at[k], self.sems[3].at[k], (peer, self.t))

    def start(self):
        for k in range(1, self.n):
            self.to(k).start()

    def add(self):
        for k in range(1, self.n):
            self.to(k).wait_recv()
        here = self.part(self.d)
        total = self.src[here].astype(F32)
        for k in range(1, self.n):
            total = total + self.got[k].astype(F32)
        self.out[here] = total.astype(BF)

    def sent(self):
        for k in range(1, self.n):
            self.to(k).wait_send()

    def spread(self):
        for k in range(1, self.n):
            self.back(k).start()

    def finish(self):
        for k in range(1, self.n):
            self.from_back(k).wait_recv()

    def spread_sent(self):
        for k in range(1, self.n):
            self.back(k).wait_send()


class QuarterGather:
    def __init__(self, buf, sems, d, t):
        self.buf, self.sems, self.d, self.t = buf, sems, d, t

    def copy(self, slot, n, peer):
        return remote(self.buf.at[slot], self.buf.at[slot], self.sems.at[n, 0], self.sems.at[n, 1], (self.d, peer))

    def start(self):
        self.copy(self.t, 0, self.t ^ 2).start()
        self.copy(self.t, 1, self.t ^ 1).start()

    def relay(self):
        self.copy(self.t ^ 2, 0, self.t ^ 2).wait_recv()
        self.copy(self.t ^ 2, 2, self.t ^ 1).start()

    def finish(self):
        self.copy(self.t ^ 1, 1, self.t ^ 1).wait_recv()
        self.copy(self.t ^ 3, 2, self.t ^ 1).wait_recv()
        self.copy(self.t, 0, self.t ^ 2).wait_send()
        self.copy(self.t, 1, self.t ^ 1).wait_send()
        self.copy(self.t ^ 2, 2, self.t ^ 1).wait_send()


def evens_first(n):
    r = lax.broadcasted_iota(jnp.int32, (n, n), 0)
    c = lax.broadcasted_iota(jnp.int32, (n, n), 1)
    return (c == jnp.where(r < n // 2, 2 * r, 2 * (r - n // 2) + 1)).astype(BF)


def all_sel(sc):
    return jnp.concatenate(
        [
            jnp.broadcast_to(sel_row(sc[0]), (PLEN, RK)),
            jnp.broadcast_to(sel_row(sc[1]), (CLEN, RK)),
            jnp.broadcast_to(sel_row(sc[2]), (CLEN, RK)),
        ],
        axis=0,
    )


def front_kernel(
    n_dp, ids_p, ids_c, group_map, gain1, gain2, bkv_ref, bm_ref,
    tok_h, aT_h, wkv_h, cos_h, sin_h, wq_h, bq_h, aoT_h, wo_h, dy_h, bd_h, adT_h, bo_h, wd_h, raw_h,
    n1q_h, q_h, kv_h, u_h, pp_h, pc_h, o_h, far_h, hp_h, hc_h, n2p_h, n2c_h, dact_h, dud_h, wgu_h,
    tok, n1, aT, wkv, cos, sin, wq, bq, aoT, wo, dyu, bd, adT, bo, wdc, raw, flat, bflat, dact, every, kv, q, u, far, pp, pc, o,
    snd_p, got_p, s_p, t_p, snd_c, got_c, s_c, t_c, n2p, n2c, hp, hc, tmp,
    lsem, osem, wsem, dsem, rsem, fsem, psem, csem, nsem, up_s, up_r, down_s, down_r, x_s, x_r,
):
    d, t = place()
    sc = [ids_p[0], ids_c[0], ids_c[1], group_map[d * CONT_DEV], group_map[d * CONT_DEV + 1]]
    lo = t % 2
    hi = n_dp // 2
    rows, width = tok.shape
    qw = wq.shape[1]
    kvw = wkv.shape[1] // 2
    hidden = wd_h.shape[0]
    ht = wdc.shape[1]
    steps = hidden // ht
    hpn, hcn = PLEN // 2, CLEN
    quarter = n1q_h.shape[1]
    greet(d, t, n_dp)
    loads = {}
    for i, (src, dst) in enumerate(
        [(tok_h, tok), (aT_h, aT), (wkv_h, wkv), (cos_h, cos), (sin_h, sin), (wq_h, wq), (bq_h, bq), (aoT_h, aoT), (wo_h, wo),
         (dy_h, dyu.at[:, :width]), (bd_h, bd), (adT_h, adT), (bo_h, bo)]
    ):
        loads[i] = pltpu.make_async_copy(src, dst, lsem.at[i])
        loads[i].start()

    def need(*which):
        for i in which:
            loads.pop(i).wait()

    def wd_copies(i, slot):
        return (
            pltpu.make_async_copy(wd_h.at[pl.ds(i * ht, ht)], wdc.at[slot, :, :width], wsem.at[slot]),
        )

    kt = raw.shape[1]
    raw_steps = width // kt

    def raw_copy(i, slot):
        return pltpu.make_async_copy(raw_h.at[pl.ds(i * kt, kt)], raw.at[slot], rsem.at[slot])

    def flat_copies(i, slot):
        here = pl.ds(i * kt, kt)
        return (
            pltpu.make_async_copy(flat.at[slot, 0], wgu_h.at[here, :hidden], fsem.at[slot, 0]),
            pltpu.make_async_copy(flat.at[slot, 1], wgu_h.at[here, hidden:], fsem.at[slot, 1]),
        )

    for i in range(2):
        for c in wd_copies(i, i):
            c.start()
        raw_copy(i, i).start()
    stores = []

    def store(src, dst):
        c = pltpu.make_async_copy(src, dst, osem.at[len(stores)])
        c.start()
        stores.append(c)

    b2 = 2 * RK
    bkv = dn(evens_first(b2), bkv_ref[...].reshape(b2, kvw)).astype(BF)
    gain_row = gain1[...].astype(F32)
    need(0)

    def norm1(r):
        x = tok[pl.ds(r, 128)].astype(F32)
        inv = lax.rsqrt(jnp.mean(x * x, axis=-1, keepdims=True) + EPSILON)
        n1[pl.ds(r, 128)] = (x * inv * gain_row).astype(BF)

    rows_loop(rows, 128, norm1)
    need(1)
    sel = all_sel(sc)
    uf = dt(n1[...], aT[...])
    for part in range(3):
        u[:, part * RK : (part + 1) * RK] = (uf[:, part * RK : (part + 1) * RK] * sel).astype(BF)
    need(2, 3, 4)
    kvf = dn(n1[...], wkv[...])
    kv[:, :kvw] = rot(kvf[:, :kvw] + dn(u[:, RK : 2 * RK], bkv[:RK]), cos[...], sin[...]).astype(BF)
    kv[:, kvw:] = (kvf[:, kvw:] + dn(u[:, 2 * RK :], bkv[RK:])).astype(BF)
    every[d] = kv[:PLEN]
    greeted(n_dp)
    spread = Spread(every, (up_s, up_r, down_s, down_r, x_s, x_r), d, t, hi)
    spread.start()

    need(5, 6)
    qf = dn(n1[...], wq[...]) + dn(u[:, :RK], bq[...])
    for c in range(qw // LANE):
        lanes = slice(c * LANE, (c + 1) * LANE)
        q[:, lanes] = rot(qf[:, lanes], cos[...], sin[...]).astype(BF) * BF(0.125)
    store(n1.at[:, pl.ds(pl.multiple_of(t * quarter, quarter), quarter)], n1q_h)
    store(q, q_h)
    store(kv, kv_h)
    store(u, u_h)

    def keep_o(of, r0, g):
        for h in range(4):
            o[r0 : r0 + CLEN, (4 * g + h) * HD : (4 * g + h + 1) * HD] = of[h * CLEN : (h + 1) * CLEN]

    mask = causal_tile()
    spread.hop(1)
    for g in range(2):
        kg = kv[:PLEN, g * HD : (g + 1) * HD]
        vg = kv[:PLEN, kvw + g * HD : kvw + (g + 1) * HD]
        for i in range(PLEN // CLEN):
            size = (i + 1) * CLEN
            s = dt(stack_heads(q, i * CLEN, g), kg[:size])
            tail = jnp.where(mask, s[:, size - CLEN :], MASKED_SCORE)
            s = tail if i == 0 else jnp.concatenate([s[:, : size - CLEN], tail], axis=1)
            p = softmax_low(s)
            pp[g, :, P_OFF[i] : P_OFF[i] + size] = p
            keep_o(dn(p, vg[:size]).astype(BF), i * CLEN, g)
    store(pp, pp_h)
    spread.hop(2)

    def project(r0, half, snd):
        ov = o[r0 : r0 + 2 * half]
        for n in range(0, width, 512):
            part = dn(ov, wo[:, n : n + 512]).astype(BF)
            snd[0, :, n : n + 512] = part[:half]
            snd[1, :, n : n + 512] = part[half:]
        uo = dt(ov, aoT[...]).astype(BF)
        pad = jnp.zeros((half, LANE - RK), BF)
        snd[0, :, width:] = jnp.concatenate([uo[:half], pad], axis=1)
        snd[1, :, width:] = jnp.concatenate([uo[half:], pad], axis=1)

    need(7, 8)
    project(0, hpn, snd_p)
    sum_p = TensorSum(snd_p, got_p, s_p, t_p, psem, d, t)
    sum_p.begin()
    spread.hop(3)

    need(9, 10, 11)
    dud = (dt(dyu[:, :width], bd[...]) * sel).astype(BF)
    dyu[:, width:] = jnp.concatenate([dud, jnp.zeros((rows, LANE - RK), BF)], axis=1)
    store(dyu.at[:, width:], dud_h)
    outs = []
    flats = []
    eye = (lax.broadcasted_iota(jnp.int32, (RK, RK), 0) == lax.broadcasted_iota(jnp.int32, (RK, RK), 1)).astype(BF)
    split = evens_first(256)

    def part_weights(i):
        slot = i % 2
        raw_copy(i, slot).wait()
        if i >= 2:
            for c in flats[i - 2]:
                c.wait()
        pairs = raw[slot].reshape(2 * kt, hidden)
        for n in range(2 * kt // 256):
            apart = dn(split, pairs[n * 256 : (n + 1) * 256]).astype(BF)
            flat[slot, 0, n * 128 : (n + 1) * 128] = apart[:128]
            flat[slot, 1, n * 128 : (n + 1) * 128] = apart[128:]
        flats.append(flat_copies(i, slot))
        for c in flats[i]:
            c.start()
        if i + 2 < raw_steps:
            raw_copy(i + 2, slot).start()

    def act_grad(i):
        slot = i % 2
        for c in wd_copies(i, slot):
            c.wait()
        if i >= 2:
            outs[i - 2].wait()
        ad = dr(adT[:, i * ht : (i + 1) * ht], eye).astype(BF)
        wdc[slot, :, width:] = jnp.concatenate([ad, jnp.zeros((ht, LANE - RK), BF)], axis=1)
        dact[slot] = dt(dyu[...], wdc[slot]).astype(BF)
        c = pltpu.make_async_copy(dact.at[slot], dact_h.at[:, pl.ds(i * ht, ht)], dsem.at[slot])
        c.start()
        outs.append(c)
        if i + 2 < steps:
            for c in wd_copies(i + 2, slot):
                c.start()

    act_grad(0)
    sum_p.middle()
    bsplit = dn(evens_first(b2), bm_ref[...].reshape(b2, hidden)).astype(BF)
    zero = jnp.zeros((RK, hidden), BF)
    bflat[:RK, :hidden] = bsplit[:RK]
    bflat[:RK, hidden:] = zero
    bflat[RK:, :hidden] = zero
    bflat[RK:, hidden:] = bsplit[RK:]
    store(bflat, wgu_h.at[pl.ds(width, b2)])
    for i in range(1, steps):
        act_grad(i)
        spread.hop(i + 3)
    for s in range(steps + 3, hi):
        spread.hop(s)
    for i in range(raw_steps):
        part_weights(i)
    spread.finish()

    far[0] = every[sc[3]]
    far[1] = every[sc[4]]
    store(far, far_h)
    for j in range(CONT_DEV):
        r0 = PLEN + j * CLEN
        for g in range(2):
            lanes = slice(g * HD, (g + 1) * HD)
            vlanes = slice(kvw + g * HD, kvw + (g + 1) * HD)
            qs = stack_heads(q, r0, g)
            sf = dt(qs, far[j, :, lanes])
            so = jnp.where(mask, dt(qs, kv[r0 : r0 + CLEN, lanes]), MASKED_SCORE)
            p = softmax_low(jnp.concatenate([sf, so], axis=1))
            pc[2 * j + g] = p
            keep_o((dn(p[:, :PLEN], far[j, :, vlanes]) + dn(p[:, PLEN:], kv[r0 : r0 + CLEN, vlanes])).astype(BF), r0, g)
    store(pc, pc_h)
    store(o, o_h)
    project(PLEN, hcn, snd_c)
    sum_c = TensorSum(snd_c, got_c, s_c, t_c, csem, d, t)
    sum_c.begin()
    sum_c.middle()

    def norm2(which, total, r0, h, n2, adapter):
        half = h.shape[0]
        total.end()
        sr = sel_row(adapter)
        uo = ((total.mine[:, width : width + RK].astype(F32) + total.theirs[:, width : width + RK].astype(F32)) * sr).astype(BF)
        tmp[:half] = dn(uo, bo[...])
        start = r0 + lo * half
        gain_two = gain2[...].astype(F32)

        def one(r):
            here = pl.ds(r, 64)
            hv = (
                tok[pl.ds(pl.multiple_of(start + r, 64), 64)].astype(F32)
                + (total.mine[here, :width].astype(F32) + total.theirs[here, :width].astype(F32))
                + tmp[here]
            )
            h[here] = hv
            inv = lax.rsqrt(jnp.mean(hv * hv, axis=-1, keepdims=True) + EPSILON)
            n2[lo, here, :width] = (hv * inv * gain_two).astype(BF)

        rows_loop(half, 64, one)
        n2[lo, :, width:] = jnp.concatenate([uo, jnp.zeros((half, LANE - RK), BF)], axis=1)
        c = remote(n2.at[lo], n2.at[lo], nsem.at[which, 0], nsem.at[which, 1], (d, t ^ 1))
        c.start()
        return c

    need(12)
    n2_copy_p = norm2(0, sum_p, 0, hp, n2p, sc[0])
    store(hp, hp_h)
    n2_copy_c = norm2(1, sum_c, PLEN, hc, n2c, jnp.where(lo == 0, sc[1], sc[2]))
    store(hc, hc_h)

    def arrived(which, n2):
        remote(n2.at[1 - lo], n2.at[1 - lo], nsem.at[which, 0], nsem.at[which, 1], (d, t ^ 1)).wait_recv()

    arrived(0, n2p)
    store(n2p, n2p_h)
    arrived(1, n2c)
    store(n2c, n2c_h)
    n2_copy_p.wait_send()
    n2_copy_c.wait_send()
    sum_p.drain()
    sum_c.drain()
    for c in outs[-2:]:
        c.wait()
    for pair in flats[-2:]:
        for c in pair:
            c.wait()
    for c in stores:
        c.wait()


def front(n_dp, scalars, small, large):
    tok, aT, wkv, cos, sin, wq, bq, aoT, wo, dy, bd, adT, bo, wd, raw = large
    rows, width = tok.shape
    qw = wq.shape[1]
    kvw2 = wkv.shape[1]
    hidden = wd.shape[0]
    quarter = width // 4
    wide = width + LANE
    ht, kt = 512, 256
    hpn, hcn = PLEN // 2, CLEN
    outs = [
        ((rows, quarter), BF), ((rows, qw), BF), ((rows, kvw2), BF), ((rows, 3 * RK), BF), ((2, 4 * CLEN, 768), BF),
        ((4, 4 * CLEN, 4 * CLEN), BF), ((rows, qw), BF), ((CONT_DEV, PLEN, kvw2), BF), ((hpn, width), F32),
        ((hcn, width), F32), ((2, hpn, wide), BF), ((2, hcn, wide), BF), ((rows, hidden), BF), ((rows, LANE), BF),
        ((width + 2 * RK, 2 * hidden), BF),
    ]
    dma = pltpu.SemaphoreType.DMA
    same = lambda a: VM(a.shape, a.dtype)
    scratch = [
        same(tok), same(tok), same(aT), same(wkv), same(cos), same(sin), same(wq), same(bq), same(aoT), same(wo),
        VM((rows, wide), BF), same(bd), same(adT), same(bo), VM((2, ht, wide), BF), VM((2, kt, 2, hidden), BF),
        VM((2, 2, kt, hidden), BF), VM((2 * RK, 2 * hidden), BF),
        VM((2, rows, ht), BF), VM((n_dp, PLEN, kvw2), BF), VM((rows, kvw2), BF),
        VM((rows, qw), BF), VM((rows, 3 * RK), BF), VM((CONT_DEV, PLEN, kvw2), BF), VM((2, 4 * CLEN, 768), BF),
        VM((4, 4 * CLEN, 4 * CLEN), BF), VM((rows, qw), BF),
        VM((2, hpn, wide), BF), VM((hpn, wide), BF), VM((hpn, wide), BF), VM((hpn, wide), BF),
        VM((2, hcn, wide), BF), VM((hcn, wide), BF), VM((hcn, wide), BF), VM((hcn, wide), BF),
        VM((2, hpn, wide), BF), VM((2, hcn, wide), BF), VM((hpn, width), F32), VM((hcn, width), F32), VM((hpn, width), F32),
        dma((13,)), dma((14,)), dma((2,)), dma((2,)), dma((2,)), dma((2, 2)), dma((4,)), dma((4,)), dma((2, 2)),
    ] + [dma((n_dp // 2 + 1,))] * 6
    vm = pl.BlockSpec(memory_space=VM)
    anyspace = pl.BlockSpec(memory_space=pl.ANY)
    return pl.pallas_call(
        functools.partial(front_kernel, n_dp),
        out_shape=[jax.ShapeDtypeStruct(s, dtype) for s, dtype in outs],
        in_specs=[pl.BlockSpec(memory_space=pltpu.SMEM)] * 3 + [vm] * len(small) + [anyspace] * len(large),
        out_specs=[anyspace] * len(outs),
        scratch_shapes=scratch,
        compiler_params=pltpu.CompilerParams(vmem_limit_bytes=61 << 20, collective_id=1, has_side_effects=True),
        cost_estimate=pl.CostEstimate(flops=2 * rows * width * 4096, bytes_accessed=80 << 20, transcendentals=0),
        name="front",
    )(*scalars, *small, *large)


def middle_kernel(
    n_dp, ids_p, ids_c, gain2, amT, adT, n2p_h, n2c_h, dact_h, dud_h, wgu_h, wd_h, hp_h, hc_h, dy_h,
    dhp_h, dhc_h, dap_h, dac_h, smp_h, smc_h, ge_h,
    wcat, wdn, n2p, n2c, dact, dud, acc, gu, dga, act, gg, ge, gots, gsum,
    snd_p, got_p, s_p, t_p, snd_c, got_c, s_c, t_c, msnd_p, mgot_p, msnd_c, mgot_c, hp, hc, dyp, dyc, dap, dac, tmp,
    lsem, osem, wsem, vsem, psem, csem, msem, nsem, g0, g1,
):
    d, t = place()
    sc = [ids_p[0], ids_c[0], ids_c[1]]
    lo = t % 2
    width = hp.shape[1]
    wide = n2p.shape[2]
    hidden = wd_h.shape[0]
    ht = wcat.shape[2] // 2
    nt = wdn.shape[2]
    steps = hidden // ht
    hpn, hcn = PLEN // 2, CLEN
    greet(d, t, n_dp)

    def weights(k, slot):
        i = k % steps
        here = pl.ds(pl.multiple_of(i * ht, ht), ht)
        there = pl.ds(pl.multiple_of(hidden + i * ht, ht), ht)
        return [
            pltpu.make_async_copy(src, dst, wsem.at[slot, n])
            for n, (src, dst) in enumerate(
                [(wgu_h.at[:, here], wcat.at[slot, :, :ht]), (wgu_h.at[:, there], wcat.at[slot, :, ht:])]
            )
        ]

    def down(n, slot):
        return pltpu.make_async_copy(wd_h.at[:, pl.ds(n * nt, nt)], wdn.at[slot], vsem.at[slot])

    def load(n, src, dst):
        c = pltpu.make_async_copy(src, dst, lsem.at[n])
        c.start()
        return c

    load_p = load(0, n2p_h, n2p)
    for c in weights(0, 0):
        c.start()
    load_da = load(1, dact_h, dact)
    load_du = load(2, dud_h, dud)
    load_c = load(3, n2c_h, n2c)
    load_hp = load(4, hp_h, hp)
    load_hc = load(5, hc_h, hc)
    load_dyp = load(6, dy_h.at[pl.ds(pl.multiple_of(lo * hpn, hpn), hpn)], dyp)
    load_dyc = load(7, dy_h.at[pl.ds(pl.multiple_of(PLEN + lo * hcn, hcn), hcn)], dyc)
    for n in range(2):
        down(n, n).start()
    stores = []

    def store(src, dst):
        c = pltpu.make_async_copy(src, dst, osem.at[len(stores)])
        c.start()
        stores.append(c)

    def begin(n2, sel):
        half = n2.shape[1]
        r = 2 * half
        u = dt(n2[:, :, :width].reshape(r, width), amT[...])
        um = jnp.concatenate([(u[:, :RK] * sel).astype(BF), (u[:, RK:] * sel).astype(BF)], axis=1)
        n2[:, :, width:] = um.reshape(2, half, 2 * RK)

        acc[:r] = jnp.zeros((r, wide), F32)

    def tile(k, n2, base, add):
        r = 2 * n2.shape[1]
        slot = k % 2
        i = k % steps
        for c in weights(k, slot):
            c.wait()

        @pl.when(k + 1 < 2 * steps)
        def _():
            for c in weights(k + 1, 1 - slot):
                c.start()

        gu[:r] = dn(n2[...].reshape(r, wide), wcat[slot])
        lanes = pl.ds(pl.multiple_of(i * ht, ht), ht)

        def swiglu(r0):
            here = pl.ds(r0, 64)
            gate = gu[here, :ht]
            upper = gu[here, ht:]
            sigma = 1.0 / (1.0 + jnp.exp(-gate))
            silu = gate * sigma
            there = pl.ds(pl.multiple_of(base + r0, 64), 64)
            da = dact[there, lanes].astype(F32)
            dga[here, :ht] = (da * upper * (sigma * (1.0 + gate * (1.0 - sigma)))).astype(BF)
            dga[here, ht : 2 * ht] = (da * silu).astype(BF)
            av = (silu * upper).astype(BF)
            dga[here, 2 * ht :] = av
            act[there, lanes] = av

        rows_loop(r, 64, swiglu)
        acc[:r] += dt(dga[:r, : 2 * ht], wcat[slot])
        small = jnp.concatenate([n2[:, :, width:].reshape(r, 2 * RK), dud[base : base + r, :RK]], axis=1)
        g = dr(small, dga[:r])
        for n in range(3):
            part = g[n * RK : (n + 1) * RK, n * ht : (n + 1) * ht]
            if add:
                total = (gg[n, :, lanes] + part).astype(BF)
                units = ht // LANE * (RK // 16)
                put_units(ge, n * (hidden // LANE * (RK // 16)) + i * units, total)
            else:
                gg[n, :, lanes] = part

    def halves(a, snd):
        half = snd.shape[1]

        def one(r0):
            for n in range(2):
                snd[n, pl.ds(r0, 64)] = a[pl.ds(pl.multiple_of(n * half + r0, 64), 64)].astype(BF)

        rows_loop(half, 64, one)

    load_p.wait()
    begin(n2p, sel_row(sc[0]))
    load_da.wait()
    load_du.wait()

    def loop_p(k, carry):
        tile(k, n2p, 0, False)
        return carry

    lax.fori_loop(0, steps, loop_p, 0)
    halves(acc, snd_p)
    greeted(n_dp)
    sum_p = TensorSum(snd_p, got_p, s_p, t_p, psem, d, t)
    sum_p.begin()

    load_c.wait()
    begin(n2c, jnp.concatenate([jnp.broadcast_to(sel_row(sc[1]), (hcn, RK)), jnp.broadcast_to(sel_row(sc[2]), (hcn, RK))], axis=0))
    tile(steps, n2c, PLEN, True)
    sum_p.middle()

    def loop_c(k, carry):
        tile(k, n2c, PLEN, True)
        return carry

    lax.fori_loop(steps + 1, 2 * steps, loop_c, 0)
    halves(acc, snd_c)
    sum_c = TensorSum(snd_c, got_c, s_c, t_c, csem, d, t)
    sum_c.begin()
    reduce = DirectReduce(ge, gots, gsum, (g0, g1, None, None), d, t, n_dp)
    reduce.start()

    ud = dt(act[...], adT[...]).astype(BF)
    pad = jnp.zeros((hpn, LANE - RK), BF)
    for n in range(2):
        msnd_p[n, :, width:] = jnp.concatenate([ud[n * hpn : (n + 1) * hpn], pad], axis=1)
        msnd_c[n, :, width:] = jnp.concatenate([ud[PLEN + n * hcn : PLEN + (n + 1) * hcn], pad[:hcn]], axis=1)
    sum_c.middle()
    for n in range(width // nt):
        slot = n % 2
        down(n, slot).wait()
        part = dn(act[...], wdn[slot]).astype(BF)
        lanes = slice(n * nt, (n + 1) * nt)
        for i in range(2):
            msnd_p[i, :, lanes] = part[i * hpn : (i + 1) * hpn]
            msnd_c[i, :, lanes] = part[PLEN + i * hcn : PLEN + (i + 1) * hcn]
        if n + 2 < width // nt:
            down(n + 2, slot).start()
    mcore_p = remote(msnd_p.at[1 - lo], mgot_p, msem.at[0], msem.at[1], (d, t ^ 1))
    mcore_p.start()
    mcore_c = remote(msnd_c.at[1 - lo], mgot_c, msem.at[2], msem.at[3], (d, t ^ 1))
    mcore_c.start()

    def mlp_sum(core, snd, got, out):
        core.wait_recv()

        def add(r0):
            rows = pl.ds(r0, 64)
            got[rows] = (snd[lo, rows].astype(F32) + got[rows].astype(F32)).astype(BF)

        rows_loop(got.shape[0], 64, add)
        store(got, out)

    def back(which, total, h, dy, da, adapter):
        half = h.shape[0]
        total.end()
        sr = sel_row(adapter)
        du = total.mine[:, width:].astype(F32) + total.theirs[:, width:].astype(F32)
        dum = (du * jnp.concatenate([sr, sr], axis=1)).astype(BF)
        tmp[:half] = dn(dum, amT[...])
        gain = gain2[...].astype(F32)

        def one(r0):
            here = pl.ds(r0, 64)
            dn2 = total.mine[here, :width].astype(F32) + total.theirs[here, :width].astype(F32) + tmp[here]
            dh = dy[here].astype(F32) + norm_back(h[here], gain, dn2)
            h[here] = dh
            da[lo, here, :width] = dh.astype(BF)

        rows_loop(half, 64, one)
        da[lo, :, width:] = dum
        c = remote(da.at[lo], da.at[lo], nsem.at[which, 0], nsem.at[which, 1], (d, t ^ 1))
        c.start()
        return c

    load_hp.wait()
    load_dyp.wait()
    copy_p = back(0, sum_p, hp, dyp, dap, sc[0])
    store(hp, dhp_h)
    mlp_sum(mcore_p, msnd_p, mgot_p, smp_h)
    mlp_sum(mcore_c, msnd_c, mgot_c, smc_h)
    reduce.add()
    store(gsum.at[reduce.part(d)], ge_h)
    load_hc.wait()
    load_dyc.wait()
    copy_c = back(1, sum_c, hc, dyc, dac, jnp.where(lo == 0, sc[1], sc[2]))
    store(hc, dhc_h)

    def arrived(which, da):
        remote(da.at[1 - lo], da.at[1 - lo], nsem.at[which, 0], nsem.at[which, 1], (d, t ^ 1)).wait_recv()

    arrived(0, dap)
    store(dap, dap_h)
    arrived(1, dac)
    store(dac, dac_h)
    copy_p.wait_send()
    copy_c.wait_send()
    sum_p.drain()
    sum_c.drain()
    mcore_p.wait_send()
    mcore_c.wait_send()
    reduce.sent()
    for c in stores:
        c.wait()


def middle(n_dp, scalars, small, large):
    n2p, n2c, dact, dud, wgu, wd, hp, hc, dy = large
    rows, width = dy.shape
    hidden = wd.shape[0]
    wide = n2p.shape[2]
    ht, nt = 512, 512
    hpn, hcn = PLEN // 2, CLEN
    units = 3 * hidden // LANE * (RK // 16)
    share = units // n_dp
    outs = [
        ((hpn, width), F32), ((hcn, width), F32), ((2, hpn, wide), BF), ((2, hcn, wide), BF), ((hpn, wide), BF),
        ((hcn, wide), BF), ((share, *UNIT), BF),
    ]
    dma = pltpu.SemaphoreType.DMA
    scratch = [
        VM((2, wide, 2 * ht), BF), VM((2, hidden, nt), BF), VM((2, hpn, wide), BF), VM((2, hcn, wide), BF),
        VM((rows, hidden), BF), VM((rows, LANE), BF), VM((PLEN, wide), F32),
        VM((PLEN, 2 * ht), F32), VM((PLEN, 3 * ht), BF), VM((rows, hidden), BF), VM((3, RK, hidden), F32),
        VM((units, *UNIT), BF), VM((n_dp, share, *UNIT), BF), VM((units, *UNIT), BF),
        VM((2, hpn, wide), BF), VM((hpn, wide), BF), VM((hpn, wide), BF), VM((hpn, wide), BF),
        VM((2, hcn, wide), BF), VM((hcn, wide), BF), VM((hcn, wide), BF), VM((hcn, wide), BF),
        VM((2, hpn, wide), BF), VM((hpn, wide), BF), VM((2, hcn, wide), BF), VM((hcn, wide), BF),
        VM((hpn, width), F32), VM((hcn, width), F32), VM((hpn, width), BF), VM((hcn, width), BF),
        VM((2, hpn, wide), BF), VM((2, hcn, wide), BF), VM((hpn, width), F32),
        dma((8,)), dma((7,)), dma((2, 2)), dma((2,)), dma((4,)), dma((4,)), dma((4,)), dma((2, 2)), dma((n_dp,)), dma((n_dp,)),
    ]
    vm = pl.BlockSpec(memory_space=VM)
    anyspace = pl.BlockSpec(memory_space=pl.ANY)
    return pl.pallas_call(
        functools.partial(middle_kernel, n_dp),
        out_shape=[jax.ShapeDtypeStruct(s, dtype) for s, dtype in outs],
        in_specs=[pl.BlockSpec(memory_space=pltpu.SMEM)] * 2 + [vm] * len(small) + [anyspace] * len(large),
        out_specs=[anyspace] * len(outs),
        scratch_shapes=scratch,
        compiler_params=pltpu.CompilerParams(vmem_limit_bytes=61 << 20, collective_id=2, has_side_effects=True),
        cost_estimate=pl.CostEstimate(flops=10 * rows * width * hidden, bytes_accessed=60 << 20, transcendentals=0),
        name="middle",
    )(*scalars, *small, *large)


class Fold:
    def __init__(self, dfar, xs, xr, ur, dr_, sems, sc, d, t, hi):
        self.dfar, self.xs, self.xr, self.ur, self.dr, self.sems, self.sc = dfar, xs, xr, ur, dr_, sems, sc
        self.d, self.t, self.hi = d, t, hi
        self.z, self.x = d // 2, d % 2
        self.order = []
        low, high = 0, hi - 1
        while low <= high:
            self.order.append(high)
            if low != high:
                self.order.append(low)
            low, high = low + 1, high - 1

    def piece(self, dest, rows):
        first = (self.sc[3] == dest).astype(F32)
        second = (self.sc[4] == dest).astype(F32)
        return self.dfar[0, rows] * first + self.dfar[1, rows] * second

    def across(self, z):
        return remote(self.xs.at[z], self.xr.at[z], self.sems[0].at[z], self.sems[1].at[z], (self.d ^ 1, self.t))

    def up(self, z):
        return remote(self.xr.at[z], self.ur.at[z], self.sems[2].at[z], self.sems[3].at[z], (self.d + 2, self.t))

    def down(self, z):
        return remote(self.xr.at[z], self.dr.at[z], self.sems[4].at[z], self.sems[5].at[z], (self.d - 2, self.t))

    def start(self):
        for z in self.order:

            def put(r, z=z):
                rows = pl.ds(r, 64)
                self.xs[z, rows] = self.piece(z * 2 + 1 - self.x, rows).astype(BF)

            rows_loop(PLEN, 64, put)
            self.across(z).start()

    def fold(self, n):
        z = self.order[n]
        self.across(z).wait_recv()

        def add(r):
            rows = pl.ds(r, 64)
            self.xr[z, rows] = (self.xr[z, rows].astype(F32) + self.piece(z * 2 + self.x, rows)).astype(BF)

        rows_loop(PLEN, 64, add)
        if z > 0:

            @pl.when(self.z == 0)
            def _():
                self.up(z).start()

        if z < self.hi - 1:

            @pl.when(self.z == self.hi - 1)
            def _():
                self.down(z).start()

    def forward(self, k):
        up, down = self.hi - 1 - k, k

        def add(z, got):
            def one(r):
                rows = pl.ds(r, 64)
                self.xr[z, rows] = (self.xr[z, rows].astype(F32) + got[z, rows].astype(F32)).astype(BF)

            rows_loop(PLEN, 64, one)

        @pl.when((self.z > 0) & (self.z < up))
        def _():
            self.up(up).wait_recv()
            add(up, self.ur)
            self.up(up).start()

        @pl.when((self.z > down) & (self.z < self.hi - 1))
        def _():
            self.down(down).wait_recv()
            add(down, self.dr)
            self.down(down).start()

    def finish(self, total):
        total[...] += self.xr[self.z].astype(F32)

        @pl.when(self.z > 0)
        def _():
            self.up(self.z).wait_recv()
            total[...] += self.ur[self.z].astype(F32)

        @pl.when(self.z < self.hi - 1)
        def _():
            self.down(self.z).wait_recv()
            total[...] += self.dr[self.z].astype(F32)

    def drain(self):
        for z in range(self.hi):
            self.across(z).wait_send()
            if z > 0:

                @pl.when(z > self.z)
                def _(z=z):
                    self.up(z).wait_send()

            if z < self.hi - 1:

                @pl.when(z < self.z)
                def _(z=z):
                    self.down(z).wait_send()


def back_kernel(
    n_dp, ids_p, ids_c, group_map, gain1, bkv_ref,
    dac_h, wo_h, o_h, aoT_h, bo_h, n2c_h, q_h, kv_h, far_h, pc_h, cos_h, sin_h, dap_h, pp_h, n2p_h, u_h, wq_h, wkv_h, bq_h,
    smp_h, hp_h, bd_h, smc_h, hc_h, dy_h, n1q_h, dhc_h, aT_h, dhp_h, tok_h, ge_h,
    out_h, tg_h, gef_h, l1_h, l2_h, t1_h, t2_h,
    dac, wo, o, aoT, bo, n2c, uoc, q, kv, far, pc, cos, sin, dap, pp, n2p, uop, u, wq, wkv, bq,
    smp, hp, bd, smc, hc, dyq, n1q, aT, xc, xp, gef, tmp_p, tmp_c,
    do, dq, dqp, dkv, dkvp, dfar, gacc, snd_p, got_p, s_p, t_p, snd_c, got_c, s_c, t_c,
    dsnd_p, dgot_p, ds_p, dt_p, dsnd_c, dgot_c, ds_c, dt_c, dup, duc, outp, outc, tgp, tgc, tmp,
    l1s, l1g, l1, l2s, l2g, l2, t1, t2, xs, xr, ur, dr_,
    lsem, osem, ysem, psem, csem, dpsem, dcsem, nsem, q1, q2, f0, f1, f2, f3, f4, f5, *rsems,
):
    d, t = place()
    sc = [ids_p[0], ids_c[0], ids_c[1], group_map[d * CONT_DEV], group_map[d * CONT_DEV + 1]]
    lo = t % 2
    hi = n_dp // 2
    width = wq.shape[0]
    qw = wq.shape[1]
    kvw = wkv.shape[1] // 2
    quarter = n1q.shape[1]
    hpn, hcn = PLEN // 2, CLEN
    greet(d, t, n_dp)
    qlanes = pl.ds(pl.multiple_of(t * quarter, quarter), quarter)
    every = DirectReduce(None, None, gef, (None, None, rsems[0], rsems[1]), d, t, n_dp)
    pairs = [
        (ge_h, gef.at[every.part(d)]), (dac_h, dac), (wo_h, wo), (o_h, o), (aoT_h, aoT), (bo_h, bo), (n2c_h.at[:, :, qlanes], n2c),
        (n2c_h.at[:, :, width:], uoc), (q_h, q), (kv_h, kv), (far_h, far), (pc_h, pc), (cos_h, cos), (sin_h, sin), (dap_h, dap),
        (pp_h, pp), (n2p_h.at[:, :, qlanes], n2p), (n2p_h.at[:, :, width:], uop), (u_h, u), (wq_h, wq), (wkv_h, wkv), (bq_h, bq),
        (smp_h, smp), (hp_h, hp), (bd_h, bd), (smc_h, smc), (hc_h, hc), (dy_h.at[:, qlanes], dyq), (n1q_h, n1q),
        (aT_h, aT), (tok_h.at[pl.ds(pl.multiple_of(PLEN + lo * hcn, hcn), hcn)], xc),
        (tok_h.at[pl.ds(pl.multiple_of(lo * hpn, hpn), hpn)], xp),
    ]
    loads = {}
    for n, (src, dst) in enumerate(pairs):
        c = pltpu.make_async_copy(src, dst, lsem.at[n])
        c.start()
        loads[id(dst) if n else 0] = c

    def need(*refs):
        for ref in refs:
            loads.pop(id(ref)).wait()

    stores = []

    def store(src, dst):
        c = pltpu.make_async_copy(src, dst, osem.at[len(stores)])
        c.start()
        stores.append(c)

    greeted(n_dp)
    loads.pop(0).wait()
    every.spread()
    mlp_p = remote(smp_h, tmp_p, ysem.at[0], ysem.at[1], (d, t ^ 2))
    mlp_p.start()
    mlp_c = remote(smc_h, tmp_c, ysem.at[2], ysem.at[3], (d, t ^ 2))
    mlp_c.start()

    at = np.cumsum([0, qw, quarter, quarter, quarter, qw, 2 * kvw]).tolist()
    bkv = dn(evens_first(2 * RK), bkv_ref[...].reshape(2 * RK, kvw)).astype(BF)

    def out_grads(da, n2, uo, sel, r0, first):
        half = da.shape[1]
        r = 2 * half
        dav = da[:, :, :width].reshape(r, width)
        duo = (dt(dav, bo[...]) * sel).astype(BF)
        do[r0 : r0 + r] = (dt(dav, wo[...]) + dn(duo, aoT[...])).astype(BF)
        gao = dr(duo, o[r0 : r0 + r])
        dum = da[:, :, width:].reshape(r, 2 * RK)
        gam = dr(dum, n2[...].reshape(r, quarter))
        gbo = dr(uo[:, :, :RK].reshape(r, RK), da[:, :, qlanes].reshape(r, quarter))
        parts = (gao, gbo, gam[:RK], gam[RK:])
        for n, part in enumerate(parts):
            lanes = slice(at[n], at[n + 1])
            gacc[:, lanes] = part if first else gacc[:, lanes] + part

    def unrotate(r0, r):
        here = slice(r0, r0 + r)
        for c in range(qw // LANE):
            lanes = slice(c * LANE, (c + 1) * LANE)
            dqp[here, lanes] = rot(dq[here, lanes].astype(F32), cos[here], -sin[here]).astype(BF)
        dkvp[here, :kvw] = rot(dkv[here, :kvw].astype(BF).astype(F32), cos[here], -sin[here]).astype(BF)
        dkvp[here, kvw:] = dkv[here, kvw:].astype(BF)

    need(dac, wo, o, aoT, bo, n2c, uoc)
    sel_c = jnp.concatenate([jnp.broadcast_to(sel_row(sc[1]), (hcn, RK)), jnp.broadcast_to(sel_row(sc[2]), (hcn, RK))], axis=0)
    out_grads(dac, n2c, uoc, sel_c, PLEN, True)
    need(q, kv, far, pc)
    for j in range(CONT_DEV):
        r0 = PLEN + j * CLEN
        for g in range(2):
            lanes = slice(g * HD, (g + 1) * HD)
            vlanes = slice(kvw + g * HD, kvw + (g + 1) * HD)
            qi = stack_heads(q, r0, g)
            doi = stack_heads(do, r0, g)
            p = pc[2 * j + g]
            dp = jnp.concatenate([dt(doi, far[j, :, vlanes]), dt(doi, kv[r0 : r0 + CLEN, vlanes])], axis=1)
            ds = back_scores(p, dp)
            dqv = dn(ds[:, :PLEN], far[j, :, lanes]) + dn(ds[:, PLEN:], kv[r0 : r0 + CLEN, lanes])
            put_dq((dqv * 0.125).astype(BF), dq, r0, g)
            dk = dr(ds, qi)
            dv = dr(p, doi)
            dfar[j, :, lanes] = dk[:PLEN]
            dfar[j, :, vlanes] = dv[:PLEN]
            dkv[r0 : r0 + CLEN, lanes] = dk[PLEN:]
            dkv[r0 : r0 + CLEN, vlanes] = dv[PLEN:]
    fold = Fold(dfar, xs, xr, ur, dr_, (f0, f1, f2, f3, f4, f5), sc, d, t, hi)
    fold.start()
    need(cos, sin)
    unrotate(PLEN, 2 * hcn)

    def dn1(r0, snd, dsnd, dsum, first):
        half = snd.shape[1]
        r = 2 * half
        here = slice(r0, r0 + r)
        a, b = dqp[here], dkvp[here]
        du = jnp.concatenate(
            [dt(a, bq[...]), dt(b[:, :kvw], bkv[:RK]), dt(b[:, kvw:], bkv[RK:]), jnp.zeros((r, RK), F32)], axis=1
        ).astype(BF)
        dsnd[0] = du[:half]
        dsnd[1] = du[half:]
        dsum.begin()
        for n in range(0, width, 512):
            part = (dt(a, wq[n : n + 512]) + dt(b, wkv[n : n + 512])).astype(BF)
            snd[0, :, n : n + 512] = part[:half]
            snd[1, :, n : n + 512] = part[half:]
        gbq = dr(u[here, :RK], a)
        gkv = dr(u[here, RK:], b)
        parts = (gbq, gkv[:RK, :kvw], gkv[RK:, kvw:])
        for part, start in zip(parts, (at[4], at[5], at[5] + kvw)):
            lanes = slice(start, start + part.shape[1])
            gacc[:, lanes] = part if first else gacc[:, lanes] + part

    need(wq, wkv, u, bq)
    dsum_c = TensorSum(dsnd_c, dgot_c, ds_c, dt_c, dcsem, d, t)
    dn1(PLEN, snd_c, dsnd_c, dsum_c, True)
    sum_c = TensorSum(snd_c, got_c, s_c, t_c, csem, d, t)
    sum_c.begin()
    fold.fold(0)
    if hi > 1:
        fold.fold(1)

    need(dap, n2p, uop)
    out_grads(dap, n2p, uop, jnp.broadcast_to(sel_row(sc[0]), (PLEN, RK)), 0, False)
    dsum_c.middle()
    sum_c.middle()
    need(pp)
    for g in range(2):
        lanes = slice(g * HD, (g + 1) * HD)
        vlanes = slice(kvw + g * HD, kvw + (g + 1) * HD)
        kg = kv[:PLEN, lanes]
        vg = kv[:PLEN, vlanes]
        for i in reversed(range(PLEN // CLEN)):
            size = (i + 1) * CLEN
            qi = stack_heads(q, i * CLEN, g)
            doi = stack_heads(do, i * CLEN, g)
            p = pp[g, :, P_OFF[i] : P_OFF[i] + size]
            ds = back_scores(p, dt(doi, vg[:size]))
            put_dq((dn(ds, kg[:size]) * 0.125).astype(BF), dq, i * CLEN, g)
            dk = dr(ds, qi)
            dv = dr(p, doi)
            if size == PLEN:
                dkv[:size, lanes] = dk
                dkv[:size, vlanes] = dv
            else:
                dkv[:size, lanes] += dk
                dkv[:size, vlanes] += dv
        if g == 0:
            for n in range(2, hi):
                fold.fold(n)
            fold.forward(0)
    for k in range(1, hi - 1):
        fold.forward(k)

    def finish_out(which, sm, theirs, copy, h, out, r0, adapter):
        half = h.shape[0]
        copy.wait_recv()
        sr = sel_row(adapter)
        ud = ((sm[:, width : width + RK].astype(F32) + theirs[:, width : width + RK].astype(F32)) * sr).astype(BF)
        tmp[:half] = dn(ud, bd[...])

        def one(r):
            here = pl.ds(r, 64)
            out[lo, here, :width] = (
                h[here] + (sm[here, :width].astype(F32) + theirs[here, :width].astype(F32)) + tmp[here]
            ).astype(BF)

        rows_loop(half, 64, one)
        out[lo, :, width:] = jnp.concatenate([ud, jnp.zeros((half, LANE - RK), BF)], axis=1)
        c = remote(out.at[lo], out.at[lo], nsem.at[which, 0], nsem.at[which, 1], (d, t ^ 1))
        c.start()
        return c

    def arrived(which, out):
        remote(out.at[1 - lo], out.at[1 - lo], nsem.at[which, 0], nsem.at[which, 1], (d, t ^ 1)).wait_recv()

    need(smp, hp, bd)
    out_copy_p = finish_out(0, smp, tmp_p, mlp_p, hp, outp, 0, sc[0])
    load_dhp = pltpu.make_async_copy(dhp_h, hp, lsem.at[32])
    load_dhp.start()

    put_units(l1s, 0, gacc[:, : at[4]].astype(BF))
    red1 = DirectReduce(l1s, l1g, l1, rsems[2:6], d, t, n_dp)
    red1.start()

    fold.finish(dkv.at[:PLEN])
    unrotate(0, PLEN)
    dsum_p = TensorSum(dsnd_p, dgot_p, ds_p, dt_p, dpsem, d, t)
    dn1(0, snd_p, dsnd_p, dsum_p, False)
    sum_p = TensorSum(snd_p, got_p, s_p, t_p, psem, d, t)
    sum_p.begin()
    dsum_p.middle()
    need(smc, hc)
    adapter_c = jnp.where(lo == 0, sc[1], sc[2])
    sum_p.middle()
    out_copy_c = finish_out(1, smc, tmp_c, mlp_c, hc, outc, PLEN, adapter_c)
    load_dhc = pltpu.make_async_copy(dhc_h, hc, lsem.at[33])
    load_dhc.start()
    put_units(l2s, 0, gacc[:, at[4] :].astype(BF))

    def share_du(which, total, du, adapter):
        total.end()
        sr = sel_row(adapter)
        raw = total.mine[:, : 3 * RK].astype(F32) + total.theirs[:, : 3 * RK].astype(F32)
        duq = (raw * jnp.concatenate([sr, sr, sr], axis=1)).astype(BF)
        du[lo] = jnp.concatenate([duq, jnp.zeros((duq.shape[0], RK), BF)], axis=1)
        c = remote(du.at[lo], du.at[lo], nsem.at[which, 0], nsem.at[which, 1], (d, t ^ 1))
        c.start()
        return c

    du_copy_c = share_du(4, dsum_c, duc, adapter_c)
    arrived(0, outp)
    arrived(1, outc)
    for n in range(2):
        store(outp.at[n, :, :width], out_h.at[pl.ds(n * hpn, hpn)])
        store(outc.at[n, :, :width], out_h.at[pl.ds(PLEN + n * hcn, hcn)])
    need(dyq, n1q)
    gbd = dr(outp[:, :, width : width + RK].reshape(PLEN, RK), dyq[:PLEN])
    gbd = gbd + dr(outc[:, :, width : width + RK].reshape(2 * hcn, RK), dyq[PLEN:])
    part1 = (at[6] - at[4]) // LANE * (RK // 16)
    put_units(l2s, part1, gbd.astype(BF))
    arrived(4, duc)
    ga = dr(duc[:, :, : 3 * RK].reshape(2 * hcn, 3 * RK), n1q[PLEN:])
    du_copy_p = share_du(5, dsum_p, dup, sc[0])
    arrived(5, dup)
    ga = (ga + dr(dup[:, :, : 3 * RK].reshape(PLEN, 3 * RK), n1q[:PLEN])).astype(BF)
    per = quarter // LANE * (RK // 16)
    for n in range(3):
        put_units(l2s, part1 + (1 + n) * per, ga[n * RK : (n + 1) * RK])
    if l2s.shape[0] > part1 + 4 * per:
        l2s[part1 + 4 * per :] = jnp.zeros((l2s.shape[0] - part1 - 4 * per, *UNIT), BF)
    red2 = DirectReduce(l2s, l2g, l2, rsems[6:10], d, t, n_dp)
    red2.start()

    def last(which, total, du, x, dh, tg):
        half = x.shape[0]
        tmp[:half] = dn(du[lo, :, : 3 * RK], aT[...])
        gain = gain1[...].astype(F32)
        total.end()

        def one(r):
            here = pl.ds(r, 64)
            dn1v = total.mine[here].astype(F32) + total.theirs[here].astype(F32) + tmp[here]
            grad = dh[here] + norm_back(x[here].astype(F32), gain, dn1v)
            tg[lo, here] = grad.astype(BF)

        rows_loop(half, 64, one)
        c = remote(tg.at[lo], tg.at[lo], nsem.at[which, 0], nsem.at[which, 1], (d, t ^ 1))
        c.start()
        return c

    need(xc, aT)
    load_dhc.wait()
    tg_copy_c = last(2, sum_c, duc, xc, hc, tgc)
    red1.add()
    red1.spread()
    arrived(2, tgc)
    for n in range(2):
        store(tgc.at[n], tg_h.at[pl.ds(PLEN + n * hcn, hcn)])
    every.finish()
    store(gef, gef_h)
    red2.add()
    red2.spread()
    need(xp)
    load_dhp.wait()
    tg_copy_p = last(3, sum_p, dup, xp, hp, tgp)
    red1.finish()
    store(l1, l1_h)
    t1[t] = l1[per : 4 * per]
    gather1 = QuarterGather(t1, q1, d, t)
    gather1.start()
    red2.finish()
    store(l2, l2_h)
    t2[t] = l2[part1 : part1 + 4 * per]
    gather2 = QuarterGather(t2, q2, d, t)
    gather2.start()
    arrived(3, tgp)
    for n in range(2):
        store(tgp.at[n], tg_h.at[pl.ds(n * hpn, hpn)])
    gather1.relay()
    gather2.relay()
    gather1.finish()
    store(t1, t1_h)
    gather2.finish()
    store(t2, t2_h)
    for c in (out_copy_p, out_copy_c, tg_copy_c, tg_copy_p, du_copy_c, du_copy_p, mlp_p, mlp_c):
        c.wait_send()
    for total in (sum_p, sum_c, dsum_p, dsum_c):
        total.drain()
    fold.drain()
    every.spread_sent()
    for red in (red1, red2):
        red.sent()
        red.spread_sent()
    for c in stores:
        c.wait()


def backward(n_dp, scalars, small, large):
    (dac, wo, o, aoT, bo, n2c, q, kv, far, pc, cos, sin, dap, pp, n2p, u, wq, wkv, bq, smp, hp, bd, smc, hc, dy, n1q, dhc, aT, dhp,
     tok, ge) = large
    rows, width = tok.shape
    qw = wq.shape[1]
    kvw2 = wkv.shape[1]
    quarter = n1q.shape[1]
    wide = dap.shape[2]
    hpn, hcn = PLEN // 2, CLEN
    per = quarter // LANE * (RK // 16)
    up = lambda a: -(-a // n_dp) * n_dp
    ue = ge.shape[0] * n_dp
    u1 = up((qw + 3 * quarter) // LANE * (RK // 16))
    u2 = up((qw + kvw2 + 4 * quarter) // LANE * (RK // 16))
    outs = [
        ((rows, width), BF), ((rows, width), BF), ((ue, *UNIT), BF), ((u1, *UNIT), BF), ((u2, *UNIT), BF),
        ((4, 3 * per, *UNIT), BF), ((4, 4 * per, *UNIT), BF),
    ]
    dma = pltpu.SemaphoreType.DMA
    hi = n_dp // 2
    same = lambda a: VM(a.shape, a.dtype)

    def sums(half, n):
        return [VM((2, half, n), BF), VM((half, n), BF), VM((half, n), BF), VM((half, n), BF)]

    scratch = [
        same(dac), same(wo), same(o), same(aoT), same(bo), VM((2, hcn, quarter), BF), VM((2, hcn, LANE), BF), same(q), same(kv),
        same(far), same(pc), same(cos), same(sin), same(dap), same(pp), VM((2, hpn, quarter), BF), VM((2, hpn, LANE), BF),
        same(u), same(wq), same(wkv), same(bq), same(smp), same(hp), same(bd), same(smc), same(hc), VM((rows, quarter), BF),
        same(n1q), same(aT), VM((hcn, width), BF), VM((hpn, width), BF), VM((ue, *UNIT), BF),
        same(smp), same(smc),
        VM((rows, qw), BF), VM((rows, qw), BF), VM((rows, qw), BF), VM((rows, kvw2), F32), VM((rows, kvw2), BF),
        VM((CONT_DEV, PLEN, kvw2), F32), VM((RK, 2 * qw + 3 * quarter + kvw2), F32),
        *sums(hpn, width), *sums(hcn, width), *sums(hpn, 2 * LANE), *sums(hcn, 2 * LANE),
        VM((2, hpn, 2 * LANE), BF), VM((2, hcn, 2 * LANE), BF),
        VM((2, hpn, wide), BF), VM((2, hcn, wide), BF), VM((2, hpn, width), BF), VM((2, hcn, width), BF), VM((hpn, width), F32),
        VM((u1, *UNIT), BF), VM((n_dp, u1 // n_dp, *UNIT), BF), VM((u1, *UNIT), BF),
        VM((u2, *UNIT), BF), VM((n_dp, u2 // n_dp, *UNIT), BF), VM((u2, *UNIT), BF),
        VM((4, 3 * per, *UNIT), BF), VM((4, 4 * per, *UNIT), BF),
        VM((hi, PLEN, kvw2), BF), VM((hi, PLEN, kvw2), BF), VM((hi, PLEN, kvw2), BF), VM((hi, PLEN, kvw2), BF),
        dma((34,)), dma((13,)), dma((4,)), dma((4,)), dma((4,)), dma((4,)), dma((4,)), dma((6, 2)), dma((3, 2)), dma((3, 2)),
    ] + [dma((hi,))] * 6 + [dma((n_dp,))] * 10
    vm = pl.BlockSpec(memory_space=VM)
    anyspace = pl.BlockSpec(memory_space=pl.ANY)
    return pl.pallas_call(
        functools.partial(back_kernel, n_dp),
        out_shape=[jax.ShapeDtypeStruct(s, dtype) for s, dtype in outs],
        in_specs=[pl.BlockSpec(memory_space=pltpu.SMEM)] * 3 + [vm] * len(small) + [anyspace] * len(large),
        out_specs=[anyspace] * len(outs),
        scratch_shapes=scratch,
        compiler_params=pltpu.CompilerParams(vmem_limit_bytes=63 << 20, collective_id=3, has_side_effects=True),
        cost_estimate=pl.CostEstimate(flops=6 * rows * width * (2 * qw + kvw2), bytes_accessed=40 << 20, transcendentals=0),
        name="back",
    )(*scalars, *small, *large)


def emit_kernel(
    qw, kvw, quarter, hidden, ge, l1, l2, t1, t2, out_h, tg_h,
    gbm, gad, gao, gbq, gbkv, gbo, gam, gbd, ga, out_o, tg_o, sem,
):
    copies = [pltpu.make_async_copy(out_h, out_o, sem.at[0]), pltpu.make_async_copy(tg_h, tg_o, sem.at[1])]
    for c in copies:
        c.start()
    high = RK // 16

    def take(blocks, first, count, put):
        for b in range(count // LANE):
            for r in range(high):
                put(slice(r * 16, (r + 1) * 16), slice(b * LANE, (b + 1) * LANE), blocks[first + b * high + r].astype(F32))

    def plain(dst, row=0, lane=0):
        def put(rows, lanes, value):
            dst[rows.start + row : rows.stop + row, lanes.start + lane : lanes.stop + lane] = value

        return put

    def paired(dst, n):
        def put(rows, lanes, value):
            dst[rows, n, lanes] = value

        return put

    seg = hidden // LANE * high
    take(ge, 0, hidden, paired(gbm, 0))
    take(ge, seg, hidden, paired(gbm, 1))
    take(ge, 2 * seg, hidden, plain(gad))
    take(l1, 0, qw, plain(gao))
    take(l2, 0, qw, plain(gbq))
    first = qw // LANE * high
    half = kvw // LANE * high
    take(l2, first, kvw, paired(gbkv, 0))
    take(l2, first + half, kvw, paired(gbkv, 1))
    per = quarter // LANE * high
    for t in range(t1.shape[0]):
        take(t1.at[t], 0, quarter, plain(gbo, 0, t * quarter))
        take(t1.at[t], per, quarter, plain(gam, 0, t * quarter))
        take(t1.at[t], 2 * per, quarter, plain(gam, RK, t * quarter))
        take(t2.at[t], 0, quarter, plain(gbd, 0, t * quarter))
        for n in range(3):
            take(t2.at[t], (1 + n) * per, quarter, plain(ga, n * RK, t * quarter))
    for c in copies:
        c.wait()


def emit(qw, kvw, quarter, hidden, grads, results):
    width = 4 * quarter
    outs = [
        ((RK, 2, hidden), F32), ((RK, hidden), F32), ((RK, qw), F32), ((RK, qw), F32), ((RK, 2, kvw), F32), ((RK, width), F32),
        ((2 * RK, width), F32), ((RK, width), F32), ((3 * RK, width), F32),
    ] + [(a.shape, a.dtype) for a in results]
    vm = pl.BlockSpec(memory_space=VM)
    anyspace = pl.BlockSpec(memory_space=pl.ANY)
    return pl.pallas_call(
        functools.partial(emit_kernel, qw, kvw, quarter, hidden),
        out_shape=[jax.ShapeDtypeStruct(s, dtype) for s, dtype in outs],
        in_specs=[vm] * len(grads) + [anyspace] * len(results),
        out_specs=[vm] * 9 + [anyspace] * 2,
        scratch_shapes=[pltpu.SemaphoreType.DMA((2,))],
        compiler_params=pltpu.CompilerParams(vmem_limit_bytes=61 << 20),
        cost_estimate=pl.CostEstimate(flops=0, bytes_accessed=20 << 20, transcendentals=0),
        name="emit",
    )(*grads, *results)


def rope_tables():
    position = np.concatenate([np.arange(PLEN)] + [PLEN + np.arange(CLEN)] * CONT_DEV).astype(np.float32)
    exponent = np.arange(HD // 2, dtype=np.float32) * np.float32(2.0 / HD)
    frequency = np.exp(np.float32(-math.log(ROPE_BASE)) * exponent).astype(np.float32)
    angle = position[:, None] * frequency[None, :]
    cos, sin = np.cos(angle).astype(np.float32), np.sin(angle).astype(np.float32)
    return np.tile(cos, (1, 4)), np.concatenate([-sin, sin, -sin, sin], axis=1)


def shards(
    tokens, cotangent, gain_attn, gain_mlp, w_query, w_kv, w_out, w_gate_up, w_down, a_attn, b_query, b_kv,
    a_out, b_out, a_mlp, b_mlp, a_down, b_down, prompt_adapter, cont_adapter, group_map,
):
    rows, width = tokens.shape
    qw = w_query.shape[1]
    kvw = w_kv.shape[2]
    hidden = w_down.shape[0]
    n_dp = lax.axis_size("dp")
    quarter = width // lax.axis_size("tensor")
    cos_np, sin_np = rope_tables()
    cos, sin = jnp.asarray(cos_np), jnp.asarray(sin_np)
    gain1 = gain_attn.reshape(1, width)
    gain2 = gain_mlp.reshape(1, width)
    aT = a_attn.transpose(1, 2, 3, 0).reshape(3 * RK, width)
    aoT = a_out.transpose(1, 2, 0).reshape(RK, qw)
    amT = a_mlp.transpose(1, 2, 3, 0).reshape(2 * RK, width)
    adT = a_down.transpose(1, 2, 0).reshape(RK, hidden)
    bq = b_query.reshape(RK, qw)
    bkv = b_kv.reshape(RK, 2, kvw)
    bo = b_out.reshape(RK, width)
    bm = b_mlp.reshape(RK, 2, hidden)
    bd = b_down.reshape(RK, width)
    wkv = w_kv.reshape(width, 2 * kvw)
    n1q, q, kv, u, pp, pc, o, far, h_p, h_c, n2p, n2c, dact, dud, wgu = front(
        n_dp, [prompt_adapter, cont_adapter, group_map], [gain1, gain2, bkv, bm],
        [tokens, aT, wkv, cos, sin, w_query, bq, aoT, w_out, cotangent, bd, adT, bo, w_down, w_gate_up],
    )
    dh_p, dh_c, dap, dac, sm_p, sm_c, ge = middle(
        n_dp, [prompt_adapter, cont_adapter], [gain2, amT, adT], [n2p, n2c, dact, dud, wgu, w_down, h_p, h_c, cotangent]
    )
    results = backward(
        n_dp, [prompt_adapter, cont_adapter, group_map], [gain1, bkv],
        [dac, w_out, o, aoT, bo, n2c, q, kv, far, pc, cos, sin, dap, pp, n2p, u, w_query, wkv, bq, sm_p, h_p, bd, sm_c, h_c,
         cotangent, n1q, dh_c, aT, dh_p, tokens, ge],
    )
    gbm, gad, gao, gbq, gbkv, gbo, gam, gbd, ga, output, tokens_grad = emit(qw, kvw, quarter, hidden, results[2:], results[:2])
    return (
        output,
        tokens_grad,
        ga.reshape(3, NA, R, width).transpose(3, 0, 1, 2),
        gbq.reshape(b_query.shape),
        gbkv.reshape(b_kv.shape),
        gao.reshape(NA, R, qw).transpose(2, 0, 1),
        gbo.reshape(b_out.shape),
        gam.reshape(2, NA, R, width).transpose(3, 0, 1, 2),
        gbm.reshape(b_mlp.shape),
        gad.reshape(NA, R, hidden).transpose(2, 0, 1),
        gbd.reshape(b_down.shape),
    )


def solution(mesh):
    in_specs = (
        P("dp", None), P("dp", None), P(), P(), P(None, "tensor"), P(None, None, "tensor"), P("tensor", None),
        P(None, None, "tensor"), P("tensor", None), P(), P(None, None, "tensor"), P(None, None, None, "tensor"),
        P("tensor", None, None), P(), P(), P(None, None, None, "tensor"), P("tensor", None, None), P(),
        P("dp"), P("dp"), P(),
    )
    out_specs = (
        P("dp", None), P("dp", None), P(), P(None, None, "tensor"), P(None, None, None, "tensor"),
        P("tensor", None, None), P(), P(), P(None, None, None, "tensor"), P("tensor", None, None), P(),
    )
    return jax.shard_map(shards, mesh=mesh, in_specs=in_specs, out_specs=out_specs, check_vma=False)
```

time: 462 us -> 406 us (0.88)
  Pallas kernels: 181 us -> 393 us
  waiting for transfers between devices: 139 us -> 0 us
  local copies, waits for them, and re-layouts: 71.2 us -> 4.91 us
  other arithmetic: 28.4 us -> 0 us
  between operations: 15.5 us -> 1.78 us
  starting transfers between devices: 8.6 us -> 0 us
  blocking collectives: 8.59 us -> 0 us
    pallas_call x12 -> x3, Pallas kernels: 113 us -> 323 us  [the longest x1 164 us: emit(): pl.pallas_call(functools.partial(emit_kernel, qw, kvw, quarter, hidden),...]
    psum x1 -> x0, waiting for transfers between devices: 77.2 us -> none  [shards(): late = lax.psum(late, 'dp')]
    ppermute x18 -> x0, waiting for transfers between devices: 60.9 us -> none  [the longest x6 59.6 us: to_chip(): return lax.ppermute(v, 'tensor', chip_pairs)]
    unnamed x136 -> x1, local copies, waits for them, and re-layouts: 31.5 us -> 2.33 us
    slice x30 -> x0, local copies, waits for them, and re-layouts: 21 us -> none  [the longest x2 3.66 us: mlp(): dact[r0:r0 + r]]
    convert_element_type x8 -> x0, other arithmetic: 8.77 us -> none  [the longest x6 5.38 us: tensor_sum(): s = (mine.astype(F32) + to_core(other).astype(F32)).astype(BF)]
    all_gather x1 -> x0, blocking collectives: 8.59 us -> none  [gather_quarters(): return lax.all_gather(v, 'tensor', axis=0, tiled=False)]
    ppermute x18 -> x0, starting transfers between devices: 8.31 us -> none  [the longest x6 5.43 us: to_chip(): return lax.ppermute(v, 'tensor', chip_pairs)]
  transfers between devices with their start and end apart: 21 -> 0, of which waited for: 9 -> 0; matrix products, arithmetic and copies ran while one was open for 11% -> 0% of each run, Pallas kernels for 19% -> 0%
where the time goes in v2:
time: 406 us; the launch traced here: 400 us
  Pallas kernels  393 us (97%)
  local copies, waits for them, and re-layouts  4.91 us (1%)
    pallas_call x1, Pallas kernels, emit(): pl.pallas_call(functools.partial(emit_kernel, qw, kvw, quarter, hidden),...  164 us
    pallas_call x1, Pallas kernels, backward(): pl.pallas_call(functools.partial(back_kernel, n_dp), out_shape=[jax.Shape...  93.8 us
    pallas_call x1, Pallas kernels, front(): pl.pallas_call(functools.partial(front_kernel, n_dp), out_shape=[jax.Shap...  69.9 us
    pallas_call x1, Pallas kernels, middle(): pl.pallas_call(functools.partial(middle_kernel, n_dp), out_shape=[jax.Sha...  65.1 us

profile of v2, /device:TPU:0, one launch (start us, length us, event | category | flops | bytes accessed | tf_op | source)
XLA Modules:
  0.0 399.8 jit_solution(2444039547049586779)
XLA Ops:
  1.3 1.3 reshape.85.gain1
  2.6 1.3 reshape.87.gain2
  3.9 2.3 copy.36
  6.2 69.9 %front.1 = (bf16[640,512]{1,0:T(8,128)(2,1)}, bf16[640,512]{1,0:T(8,128)(2,1)}, bf16[640,256]{1,0:T(8,128)(2,1)}, bf16[640,192]{1,0:T(8,128)(2,1)}, bf16[2,512,7...) custom-call(s32[1]{0:T(128)S(6)} %copy.37.ids_p, ...), custom_call_target="tpu_custom_call" | custom-call | flops 10737418240 | bytes 83886080 | tf_op jit(solution)/shard_map/front/pallas_call | solution.py:618
  76.1 65.1 %middle.1 = (f32[192,2048]{1,0:T(8,128)}, f32[128,2048]{1,0:T(8,128)}, bf16[2,192,2176]{2,1,0:T(8,128)(2,1)}, bf16[2,128,2176]{2,1,0:T(8,128)(2,1)}, bf16[192,21...) custom-call(s32[1]{0:T(128)S(6)} %copy.37.ids_p, s32[2]{0:T(128)} %ids_c.5, ...), custom_call_target="tpu_custom_call" | custom-call | flops 26843545600 | bytes 62914560 | tf_op jit(solution)/shard_map/middle/pallas_call | solution.py:890
  141.2 93.8 %back.1 = (bf16[640,2048]{1,0:T(8,128)(2,1)}, bf16[640,2048]{1,0:T(8,128)(2,1)}, bf16[192,16,128]{2,1,0:T(8,128)(2,1)}, bf16[64,16,128]{2,1,0:T(8,128)(2,1)}, bf...) custom-call(s32[1]{0:T(128)S(6)} %copy.37.ids_p, s32[2]{0:T(128)} %ids_c.5, ...), custom_call_target="tpu_custom_call" | custom-call | flops 10066329600 | bytes 41943040 | tf_op jit(solution)/shard_map/back/pallas_call | solution.py:1372
  235.0 164.3 %emit.1 = (f32[64,2,2048]{2,1,0:T(2,128)}, f32[64,2048]{1,0:T(8,128)}, f32[64,512]{1,0:T(8,128)}, f32[64,512]{1,0:T(8,128)}, f32[64,2,128]{2,1,0:T(2,128)}, /*in...) custom-call(bf16[192,16,128]{2,1,0:T(8,128)(2,1)} %get-tuple-element, ...), custom_call_target="tpu_custom_call" | custom-call | bytes 20971520 | tf_op jit(solution)/shard_map/emit/pallas_call | solution.py:1440

commit v3 on v2

v3 whole, which is shorter than its diff:
```python
import functools
import math

import jax
import jax.numpy as jnp
import numpy as np
from jax import lax
from jax.experimental import pallas as pl
from jax.experimental.pallas import tpu as pltpu
from jax.sharding import PartitionSpec as P

HD = 64
R = 16
NA = 4
RK = NA * R
PLEN = 384
CLEN = 128
CONT_DEV = 2
ROWS = PLEN + CONT_DEV * CLEN
EPSILON = 1e-05
ROPE_BASE = 500000.0
MASKED_SCORE = -1e30

BF = jnp.bfloat16
F32 = jnp.float32
VM = pltpu.VMEM
LANE = 128


def dn(a, b):
    return jnp.dot(a, b, preferred_element_type=F32)


def dt(a, b):
    return lax.dot_general(a, b, (((1,), (1,)), ((), ())), preferred_element_type=F32)


def dr(a, b):
    return lax.dot_general(a, b, (((0,), (0,)), ((), ())), preferred_element_type=F32)


def sel_row(adapter):
    lane = lax.broadcasted_iota(jnp.int32, (1, RK), 1)
    return (lax.shift_right_logical(lane, 4) == adapter).astype(F32)


def swap_halves(v):
    lane = lax.broadcasted_iota(jnp.int32, v.shape, 1)
    return jnp.where((lane & 63) < 32, pltpu.roll(v, LANE - 32, 1), pltpu.roll(v, 32, 1))


def rot(v, cos, sin):
    return v * cos + swap_halves(v) * sin


def stack_heads(ref, r0, g):
    return jnp.concatenate(
        [ref[pl.ds(r0, CLEN), (4 * g + h) * HD : (4 * g + h + 1) * HD] for h in range(4)], axis=0
    )


def softmax_low(s):
    top = jnp.max(s, axis=-1, keepdims=True)
    e = jnp.exp(s - top)
    return (e * (1.0 / jnp.sum(e, axis=-1, keepdims=True))).astype(BF)


def causal_tile():
    r = lax.broadcasted_iota(jnp.int32, (4 * CLEN, CLEN), 0) & (CLEN - 1)
    c = lax.broadcasted_iota(jnp.int32, (4 * CLEN, CLEN), 1)
    return c <= r


P_OFF = (0, 128, 384)


def norm_back(v, gain, upstream):
    inv = lax.rsqrt(jnp.mean(v * v, axis=-1, keepdims=True) + EPSILON)
    scaled = v * inv
    weighted = upstream * gain
    return inv * (weighted - scaled * jnp.mean(weighted * scaled, axis=-1, keepdims=True))


def put_dq(dq, dq_ref, r0, g):
    for h in range(4):
        dq_ref[pl.ds(r0, CLEN), (4 * g + h) * HD : (4 * g + h + 1) * HD] = dq[h * CLEN : (h + 1) * CLEN]


def back_scores(p, dp):
    pf = p.astype(F32)
    return (pf * (dp - jnp.sum(pf * dp, axis=-1, keepdims=True))).astype(BF)


MESH = pl.DeviceIdType.MESH


def rows_loop(total, step, body):
    def one(i, carry):
        body(pl.multiple_of(i * step, step))
        return carry

    lax.fori_loop(0, total // step, one, 0)


def loop(first, last, body):
    def one(i, carry):
        body(i)
        return carry

    lax.fori_loop(first, last, one, 0)


def place():
    d = lax.axis_index("dp")
    t = lax.axis_index("tensor")
    return d, t


def remote(src, dst, send, recv, device):
    return pltpu.make_async_remote_copy(
        src_ref=src, dst_ref=dst, send_sem=send, recv_sem=recv, device_id=device, device_id_type=MESH
    )


def greet(d, t, n_dp):
    barrier = pltpu.get_barrier_semaphore()
    for device in [(d, t ^ 1), (d, t ^ 2)] + [((d + k) % n_dp, t) for k in range(1, n_dp)]:
        pl.semaphore_signal(barrier, inc=1, device_id=device, device_id_type=MESH)


def greeted(n_dp):
    pl.semaphore_wait(pltpu.get_barrier_semaphore(), n_dp + 1)


class Spread:
    def __init__(self, every, sems, d, t, hi):
        self.every, self.sems, self.d, self.t, self.hi = every, sems, d, t, hi
        self.z, self.x = d // 2, d % 2

    def across(self, z):
        block = z * 2 + self.x
        up_s, up_r, down_s, down_r, x_s, x_r = self.sems
        return remote(self.every.at[block], self.every.at[block], x_s.at[z], x_r.at[z], (self.d ^ 1, self.t))

    def along(self, z, s, up):
        block = z * 2 + self.x
        up_s, up_r, down_s, down_r, x_s, x_r = self.sems
        send, recv, step = (up_s, up_r, 2) if up else (down_s, down_r, -2)
        return remote(self.every.at[block], self.every.at[block], send.at[s], recv.at[s], (self.d + step, self.t))

    def start(self):
        self.across(self.z).start()

        @pl.when(self.z < self.hi - 1)
        def _():
            self.along(self.z, 1, True).start()

        @pl.when(self.z > 0)
        def _():
            self.along(self.z, 1, False).start()

    def hop(self, s):
        if s > self.hi - 1:
            return
        for up in (True, False):
            origin = self.z - s if up else self.z + s
            held = origin >= 0 if up else origin < self.hi
            further = self.z < self.hi - 1 if up else self.z > 0

            @pl.when(held)
            def _(origin=origin, up=up, further=further):
                self.along(origin, s, up).wait_recv()
                self.across(origin).start()
                if s + 1 <= self.hi - 1:

                    @pl.when(further)
                    def _():
                        self.along(origin, s + 1, up).start()

    def finish(self):
        for z in range(self.hi):
            across = self.across(z)
            across.wait_send()
            block = z * 2 + 1 - self.x
            up_s, up_r, down_s, down_r, x_s, x_r = self.sems
            remote(self.every.at[block], self.every.at[block], x_s.at[z], x_r.at[z], (self.d ^ 1, self.t)).wait_recv()
        for s in range(1, self.hi):
            for up in (True, False):
                origin = self.z - s + 1 if up else self.z + s - 1
                held = origin >= 0 if up else origin < self.hi
                further = self.z < self.hi - 1 if up else self.z > 0

                @pl.when(held & further)
                def _(origin=origin, up=up, s=s):
                    self.along(origin, s, up).wait_send()


class TensorSum:
    def __init__(self, snd, got, mine, theirs, sems, d, t):
        self.snd, self.got, self.mine, self.theirs, self.sems, self.t = snd, got, mine, theirs, sems, t
        self.lo = t % 2
        self.core = remote(snd.at[1 - self.lo], got, sems.at[0], sems.at[1], (d, t ^ 1))
        self.chip = remote(mine, theirs, sems.at[2], sems.at[3], (d, t ^ 2))

    def begin(self):
        self.core.start()

    def middle(self):
        self.core.wait_recv()

        def add(r):
            rows = pl.ds(r, 64)
            self.mine[rows] = (self.snd[self.lo, rows].astype(F32) + self.got[rows].astype(F32)).astype(BF)

        rows_loop(self.mine.shape[0], 64, add)
        self.chip.start()

    def end(self):
        self.chip.wait_recv()

    def drain(self):
        self.core.wait_send()
        self.chip.wait_send()


UNIT = (16, LANE)


def put_units(blocks, first, value):
    for b in range(value.shape[1] // LANE):
        for r in range(RK // 16):
            blocks[first + b * (RK // 16) + r] = value[r * 16 : (r + 1) * 16, b * LANE : (b + 1) * LANE]


class DirectReduce:
    def __init__(self, src, got, out, sems, d, t, n_dp):
        self.src, self.got, self.out, self.sems, self.d, self.t, self.n = src, got, out, sems, d, t, n_dp
        self.share = src.shape[0] // n_dp if src is not None else out.shape[0] // n_dp

    def part(self, d):
        return pl.ds(((d % 2) * (self.n // 2) + d // 2) * self.share, self.share)

    def to(self, k):
        peer = (self.d + k) % self.n
        return remote(self.src.at[self.part(peer)], self.got.at[k], self.sems[0].at[k], self.sems[1].at[k], (peer, self.t))

    def back(self, k):
        peer = (self.d + k) % self.n
        here = self.part(self.d)
        return remote(self.out.at[here], self.out.at[here], self.sems[2].at[k], self.sems[3].at[k], (peer, self.t))

    def from_back(self, k):
        peer = (self.d + self.n - k) % self.n
        there = self.part(peer)
        return remote(self.out.at[there], self.out.at[there], self.sems[2].at[k], self.sems[3].at[k], (peer, self.t))

    def start(self):
        for k in range(1, self.n):
            self.to(k).start()

    def add(self):
        for k in range(1, self.n):
            self.to(k).wait_recv()
        here = self.part(self.d)
        total = self.src[here].astype(F32)
        for k in range(1, self.n):
            total = total + self.got[k].astype(F32)
        self.out[here] = total.astype(BF)

    def sent(self):
        for k in range(1, self.n):
            self.to(k).wait_send()

    def spread(self):
        for k in range(1, self.n):
            self.back(k).start()

    def finish(self):
        for k in range(1, self.n):
            self.from_back(k).wait_recv()

    def spread_sent(self):
        for k in range(1, self.n):
            self.back(k).wait_send()


class PairReduce:
    def __init__(self, src, gx, gz, out, sems, d, t, n_dp):
        self.src, self.gx, self.gz, self.out, self.sems, self.t = src, gx, gz, out, sems, t
        self.hi, self.z, self.x = n_dp // 2, d // 2, d % 2
        self.share = out.shape[0] // n_dp
        self.mate = (d ^ 1, t)

    def part(self, z):
        return pl.ds((self.x * self.hi + z) * self.share, self.share)

    def half(self, x):
        return pl.ds(x * self.hi * self.share, self.hi * self.share)

    def on_line(self, k):
        z = (self.z + k) % self.hi
        return z, (z * 2 + self.x, self.t)

    def over(self):
        return remote(self.src.at[self.half(1 - self.x)], self.gx, self.sems[0].at[0], self.sems[1].at[0], self.mate)

    def to(self, k):
        z, device = self.on_line(k)
        return remote(self.src.at[self.part(z)], self.gz.at[k], self.sems[2].at[k], self.sems[3].at[k], device)

    def back(self, k, come=False):
        z, device = self.on_line(self.hi - k if come else k)
        here = self.part(z if come else self.z)
        return remote(self.out.at[here], self.out.at[here], self.sems[4].at[k], self.sems[5].at[k], device)

    def over_back(self, x):
        here = self.half(x)
        return remote(self.out.at[here], self.out.at[here], self.sems[6].at[0], self.sems[7].at[0], self.mate)

    def start(self):
        self.over().start()

    def middle(self):
        self.over().wait_recv()
        here = self.half(self.x)
        self.src[here] = (self.src[here].astype(F32) + self.gx[...].astype(F32)).astype(BF)
        for k in range(1, self.hi):
            self.to(k).start()

    def add(self):
        here = self.part(self.z)
        total = self.src[here].astype(F32)
        for k in range(1, self.hi):
            self.to(k).wait_recv()
            total = total + self.gz[k].astype(F32)
        self.out[here] = total.astype(BF)
        self.spread()

    def spread(self):
        for k in range(1, self.hi):
            self.back(k).start()

    def cross(self):
        for k in range(1, self.hi):
            self.back(k, True).wait_recv()
        self.over_back(self.x).start()

    def finish(self):
        self.over_back(1 - self.x).wait_recv()

    def spread_sent(self):
        for k in range(1, self.hi):
            self.back(k).wait_send()
        self.over_back(self.x).wait_send()

    def sent(self):
        self.over().wait_send()
        for k in range(1, self.hi):
            self.to(k).wait_send()


class Trade:
    def __init__(self, halves, sems, d, t):
        self.halves, self.sems, self.d, self.t = halves, sems, d, t

    def slot(self, n):
        return remote(self.halves.at[n], self.halves.at[n], self.sems.at[0], self.sems.at[1], (self.d, self.t ^ 1))

    def start(self):
        self.slot(self.t % 2).start()

    def finish(self):
        self.slot(1 - self.t % 2).wait_recv()

    def sent(self):
        self.slot(self.t % 2).wait_send()


def evens_first(n):
    r = lax.broadcasted_iota(jnp.int32, (n, n), 0)
    c = lax.broadcasted_iota(jnp.int32, (n, n), 1)
    return (c == jnp.where(r < n // 2, 2 * r, 2 * (r - n // 2) + 1)).astype(BF)


def all_sel(sc):
    return jnp.concatenate(
        [
            jnp.broadcast_to(sel_row(sc[0]), (PLEN, RK)),
            jnp.broadcast_to(sel_row(sc[1]), (CLEN, RK)),
            jnp.broadcast_to(sel_row(sc[2]), (CLEN, RK)),
        ],
        axis=0,
    )


def first_kernel(
    n_dp, ids_p, ids_c, group_map, gain1, gain2, bkv_ref, bm_h, amT_h, adT_h, bo_h,
    tok_h, aT_h, wkv_h, cos_h, sin_h, wq_h, bq_h, aoT_h, wo_h, dy_h, bd_h, wd_h, raw_h,
    n1q_h, q_h, kv_h, u_h, pp_h, pc_h, o_h, far_h, hp_h, hc_h, n2p_h, n2c_h, uop_h, uoc_h, wgu_h,
    dhp_h, dhc_h, dap_h, dac_h, smp_h, smc_h, ge_h,
    every, snd_p, s_p, snd_c, s_c, got0_p, t0_p, got0_c, t0_c, got1_p, t1_p, got1_c, t1_c,
    n2p, n2c, uop, uoc, hp, hc, xp, xc, dyp, dyc, dact, dud, tmp, ge, gots, gsum, bm, amT, adT, bo,
    lsem, osem, wsem, rsem, fsem, vsem, psem, csem, psem2, csem2, msem, nsem, up_s, up_r, down_s, down_r, x_s, x_r, g0, g1,
):
    d, t = place()
    sc = [ids_p[0], ids_c[0], ids_c[1], group_map[d * CONT_DEV], group_map[d * CONT_DEV + 1]]
    lo = t % 2
    hi = n_dp // 2
    rows, width = tok_h.shape
    wide = n2p.shape[2]
    qw = wq_h.shape[1]
    kvw = wkv_h.shape[1] // 2
    hidden = wd_h.shape[0]
    ht = 512
    steps = hidden // ht
    hpn, hcn = PLEN // 2, CLEN
    part = n1q_h.shape[1]
    qlanes = pl.ds(pl.multiple_of(lo * part, part), part)
    adapter_c = jnp.where(lo == 0, sc[1], sc[2])
    greet(d, t, n_dp)
    counts = [0, 0]

    def load(src, dst):
        c = pltpu.make_async_copy(src, dst, lsem.at[counts[0]])
        counts[0] += 1
        c.start()
        return c

    def store(src, dst):
        c = pltpu.make_async_copy(src, dst, osem.at[counts[1]])
        counts[1] += 1
        c.start()
        return c

    spread = Spread(every, (up_s, up_r, down_s, down_r, x_s, x_r), d, t, hi)
    sum_p = TensorSum(snd_p, got0_p, s_p, t0_p, psem, d, t)
    sum_c = TensorSum(snd_c, got0_c, s_c, t0_c, csem, d, t)
    sel = all_sel(sc)
    b2 = 2 * RK

    def attention(tok, n1, aT, wkv, cos, sin, wq, bq, aoT, wo, bd, wdc, raw, flat, bflat, kv, q, u, far, pp, pc, o):
        kt = raw.shape[1]
        raw_steps = width // kt

        def raw_copy(i, slot):
            return pltpu.make_async_copy(raw_h.at[pl.ds(i * kt, kt)], raw.at[slot], rsem.at[slot])

        def flat_copies(i, slot):
            here = pl.ds(i * kt, kt)
            return (
                pltpu.make_async_copy(flat.at[slot, 0], wgu_h.at[here, :hidden], fsem.at[slot, 0]),
                pltpu.make_async_copy(flat.at[slot, 1], wgu_h.at[here, hidden:], fsem.at[slot, 1]),
            )

        def wd_copy(i, slot):
            return pltpu.make_async_copy(wd_h.at[pl.ds(i * ht, ht)], wdc.at[slot, :, :width], wsem.at[slot, 0])

        load_tok = load(tok_h, tok.at[:, :width])
        load_kv = [load(a, b) for a, b in ((aT_h, aT), (wkv_h, wkv), (cos_h, cos), (sin_h, sin))]
        load_q = [load(a, b) for a, b in ((wq_h, wq), (bq_h, bq))]
        stores = []

        bkv = dn(evens_first(b2), bkv_ref[...].reshape(b2, kvw)).astype(BF)
        gain_row = gain1[...].astype(F32).reshape(1, width)
        load_tok.wait()

        def norm1(r):
            x = tok[pl.ds(r, 128), :width].astype(F32)
            inv = lax.rsqrt(jnp.mean(x * x, axis=-1, keepdims=True) + EPSILON)
            n1[pl.ds(r, 128)] = (x * inv * gain_row).astype(BF)

        rows_loop(rows, 128, norm1)
        load_o = [load(a, b) for a, b in ((aoT_h, aoT), (wo_h, wo))]
        load_dy = [load(a, b) for a, b in ((dy_h, tok.at[:, :width]), (bd_h, bd), (adT_h, adT))]
        for i in range(2):
            wd_copy(i, i).start()
        for i in range(raw.shape[0]):
            raw_copy(i, i).start()
        load_bm = load(bm_h, bm)
        load_x = [
            load(tok_h.at[pl.ds(pl.multiple_of(lo * hpn, hpn), hpn)], xp),
            load(tok_h.at[pl.ds(pl.multiple_of(PLEN + lo * hcn, hcn), hcn)], xc),
            load(amT_h, amT),
            load(bo_h, bo),
        ]
        for c in load_kv:
            c.wait()
        uf = dt(n1[...], aT[...])
        for part in range(3):
            u[:, part * RK : (part + 1) * RK] = (uf[:, part * RK : (part + 1) * RK] * sel).astype(BF)
        kvf = dn(n1[...], wkv[...])
        kv[:, :kvw] = rot(kvf[:, :kvw] + dn(u[:, RK : 2 * RK], bkv[:RK]), cos[...], sin[...]).astype(BF)
        kv[:, kvw:] = (kvf[:, kvw:] + dn(u[:, 2 * RK :], bkv[RK:])).astype(BF)
        every[d] = kv[:PLEN]
        greeted(n_dp)
        spread.start()

        for c in load_q:
            c.wait()
        qf = dn(n1[...], wq[...]) + dn(u[:, :RK], bq[...])
        for c in range(qw // LANE):
            lanes = slice(c * LANE, (c + 1) * LANE)
            q[:, lanes] = rot(qf[:, lanes], cos[...], sin[...]).astype(BF) * BF(0.125)
        stores.append(store(n1.at[:, qlanes], n1q_h))
        stores.append(store(q, q_h))
        stores.append(store(kv, kv_h))
        stores.append(store(u, u_h))

        def keep_o(of, r0, g):
            for h in range(4):
                o[pl.ds(r0, CLEN), (4 * g + h) * HD : (4 * g + h + 1) * HD] = of[h * CLEN : (h + 1) * CLEN]

        mask = causal_tile()
        for g in range(2):
            kg = kv[:PLEN, g * HD : (g + 1) * HD]
            vg = kv[:PLEN, kvw + g * HD : kvw + (g + 1) * HD]
            for i in range(PLEN // CLEN):
                size = (i + 1) * CLEN
                s = dt(stack_heads(q, i * CLEN, g), kg[:size])
                tail = jnp.where(mask, s[:, size - CLEN :], MASKED_SCORE)
                s = tail if i == 0 else jnp.concatenate([s[:, : size - CLEN], tail], axis=1)
                p = softmax_low(s)
                pp[g, :, P_OFF[i] : P_OFF[i] + size] = p
                keep_o(dn(p, vg[:size]).astype(BF), i * CLEN, g)
        stores.append(store(pp, pp_h))
        spread.hop(1)

        def project(r0, half, snd):
            ov = o[r0 : r0 + 2 * half]

            def columns(n):
                lanes = pl.ds(pl.multiple_of(n * 512, 512), 512)
                part = dn(ov, wo[:, lanes]).astype(BF)
                snd[0, :, lanes] = part[:half]
                snd[1, :, lanes] = part[half:]

            loop(0, width // 512, columns)
            uo = dt(ov, aoT[...]).astype(BF)
            pad = jnp.zeros((half, LANE - RK), BF)
            snd[0, :, width:] = jnp.concatenate([uo[:half], pad], axis=1)
            snd[1, :, width:] = jnp.concatenate([uo[half:], pad], axis=1)

        for c in load_o:
            c.wait()
        project(0, hpn, snd_p)
        sum_p.begin()

        for c in load_dy:
            c.wait()
        dudv = (dt(tok[:, :width], bd[...]) * sel).astype(BF)
        dud[...] = jnp.concatenate([dudv, jnp.zeros((rows, LANE - RK), BF)], axis=1)
        tok[:, width:] = dud[...]
        eye = (lax.broadcasted_iota(jnp.int32, (RK, RK), 0) == lax.broadcasted_iota(jnp.int32, (RK, RK), 1)).astype(BF)
        split = evens_first(256)

        slots, flats = raw.shape[0], flat.shape[0]

        def part_weights(i):
            slot = i % slots
            raw_copy(i, slot).wait()

            put = i % flats

            @pl.when(i >= flats)
            def _():
                for c in flat_copies(i - flats, put):
                    c.wait()

            apart = dn(split, raw[slot].reshape(2 * kt, hidden)).astype(BF)
            flat[put, 0] = apart[:kt]
            flat[put, 1] = apart[kt:]
            for c in flat_copies(i, put):
                c.start()

            @pl.when(i + slots < raw_steps)
            def _():
                raw_copy(i + slots, slot).start()

        def act_grad(i):
            slot = i % 2
            wd_copy(i, slot).wait()
            lanes = pl.ds(pl.multiple_of(i * ht, ht), ht)
            ad = dr(adT[:, lanes], eye).astype(BF)
            wdc[slot, :, width:] = jnp.concatenate([ad, jnp.zeros((ht, LANE - RK), BF)], axis=1)
            dact[:, lanes] = dt(tok[...], wdc[slot]).astype(BF)

            @pl.when(i + 2 < steps)
            def _():
                wd_copy(i + 2, slot).start()

        def both(i):
            act_grad(i)

            @pl.when(i == 0)
            def _():
                spread.hop(2)

            @pl.when(i == 1)
            def _():
                spread.hop(3)

            per = raw_steps // steps
            loop(i * per, (i + 1) * per, part_weights)

        sum_p.middle()
        loop(0, steps, both)
        load_bm.wait()
        bsplit = dn(evens_first(b2), bm[...].reshape(b2, hidden)).astype(BF)
        zero = jnp.zeros((RK, hidden), BF)
        bflat[:RK, :hidden] = bsplit[:RK]
        bflat[:RK, hidden:] = zero
        bflat[RK:, :hidden] = zero
        bflat[RK:, hidden:] = bsplit[RK:]
        stores.append(store(bflat, wgu_h.at[pl.ds(width, b2)]))
        for s in range(4, hi):
            spread.hop(s)
        spread.finish()

        far[0] = every[sc[3]]
        far[1] = every[sc[4]]
        stores.append(store(far, far_h))

        def attend(j):
            r0 = pl.multiple_of(PLEN + j * CLEN, CLEN)
            own = pl.ds(r0, CLEN)
            for g in range(2):
                lanes = slice(g * HD, (g + 1) * HD)
                vlanes = slice(kvw + g * HD, kvw + (g + 1) * HD)
                qs = stack_heads(q, r0, g)
                sf = dt(qs, far[j, :, lanes])
                so = jnp.where(mask, dt(qs, kv[own, lanes]), MASKED_SCORE)
                p = softmax_low(jnp.concatenate([sf, so], axis=1))
                pc[2 * j + g] = p
                keep_o((dn(p[:, :PLEN], far[j, :, vlanes]) + dn(p[:, PLEN:], kv[own, vlanes])).astype(BF), r0, g)

        loop(0, CONT_DEV, attend)
        stores.append(store(pc, pc_h))
        stores.append(store(o, o_h))
        project(PLEN, hcn, snd_c)
        sum_c.begin()
        for c in load_x:
            c.wait()
        for i in range(raw_steps - flats, raw_steps):
            for c in flat_copies(i, i % flats):
                c.wait()
        for c in stores:
            c.wait()

    pl.run_scoped(
        attention,
        VM((rows, wide), BF), VM((rows, width), BF), VM(aT_h.shape, BF), VM(wkv_h.shape, BF), VM(cos_h.shape, F32),
        VM(sin_h.shape, F32), VM(wq_h.shape, BF), VM(bq_h.shape, BF), VM(aoT_h.shape, BF), VM(wo_h.shape, BF), VM(bd_h.shape, BF),
        VM((2, ht, wide), BF), VM((3, 128, 2, hidden), BF), VM((3, 2, 128, hidden), BF), VM((b2, 2 * hidden), BF),
        VM((rows, 2 * kvw), BF), VM((rows, qw), BF), VM((rows, 3 * RK), BF), VM((CONT_DEV, PLEN, 2 * kvw), BF),
        VM((2, 4 * CLEN, 768), BF), VM((4, 4 * CLEN, 4 * CLEN), BF), VM((rows, qw), BF),
    )

    def feed_forward(wcat, wdn, acc, gu, dga, act, gg):
        nt = wdn.shape[2]

        def weights(k, slot):
            i = k % steps
            here = pl.ds(pl.multiple_of(i * ht, ht), ht)
            there = pl.ds(pl.multiple_of(hidden + i * ht, ht), ht)
            return [
                pltpu.make_async_copy(src, dst, wsem.at[slot, n])
                for n, (src, dst) in enumerate(
                    [(wgu_h.at[:, here], wcat.at[slot, :, :ht]), (wgu_h.at[:, there], wcat.at[slot, :, ht:])]
                )
            ]

        def down(n, slot):
            return pltpu.make_async_copy(wd_h.at[:, pl.ds(n * nt, nt)], wdn.at[slot], vsem.at[slot])

        for c in weights(0, 0):
            c.start()
        load_dy = [
            load(dy_h.at[pl.ds(pl.multiple_of(lo * hpn, hpn), hpn)], dyp),
            load(dy_h.at[pl.ds(pl.multiple_of(PLEN + lo * hcn, hcn), hcn)], dyc),
        ]
        for n in range(2):
            down(n, n).start()
        sum_c.middle()

        def norm2(which, total, x, h, n2, adapter):
            half = h.shape[0]
            total.end()
            sr = sel_row(adapter)
            uo = (total.mine[:, width : width + RK].astype(F32) + total.theirs[:, width : width + RK].astype(F32)) * sr
            uo = uo.astype(BF)
            tmp[:half] = dn(uo, bo[...])
            gain_two = gain2[...].astype(F32).reshape(1, width)

            def one(r):
                here = pl.ds(r, 64)
                hv = (
                    x[here].astype(F32)
                    + (total.mine[here, :width].astype(F32) + total.theirs[here, :width].astype(F32))
                    + tmp[here]
                )
                h[here] = hv
                inv = lax.rsqrt(jnp.mean(hv * hv, axis=-1, keepdims=True) + EPSILON)
                n2[lo, here, :width] = (hv * inv * gain_two).astype(BF)

            rows_loop(half, 64, one)
            n2[lo, :, width:] = jnp.concatenate([uo, jnp.zeros((half, LANE - RK), BF)], axis=1)
            c = remote(n2.at[lo], n2.at[lo], nsem.at[which, 0], nsem.at[which, 1], (d, t ^ 1))
            c.start()
            return c

        def arrived(which, n2):
            remote(n2.at[1 - lo], n2.at[1 - lo], nsem.at[which, 0], nsem.at[which, 1], (d, t ^ 1)).wait_recv()

        def begin(n2, uo, chosen):
            half = n2.shape[1]
            r = 2 * half
            um = dt(n2[:, :, :width].reshape(r, width), amT[...])
            um = jnp.concatenate([(um[:, :RK] * chosen).astype(BF), (um[:, RK:] * chosen).astype(BF)], axis=1)
            uo[...] = n2[:, :, width:]
            n2[:, :, width:] = um.reshape(2, half, 2 * RK)
            acc[:r] = jnp.zeros((r, wide), F32)

        def tile(k, n2, base, add):
            r = 2 * n2.shape[1]
            slot = k % 2
            i = k % steps
            for c in weights(k, slot):
                c.wait()

            @pl.when(k + 1 < 2 * steps)
            def _():
                for c in weights(k + 1, 1 - slot):
                    c.start()

            gu[:r] = dn(n2[...].reshape(r, wide), wcat[slot])
            lanes = pl.ds(pl.multiple_of(i * ht, ht), ht)

            def swiglu(r0):
                here = pl.ds(r0, 64)
                gate = gu[here, :ht]
                upper = gu[here, ht:]
                sigma = 1.0 / (1.0 + jnp.exp(-gate))
                silu = gate * sigma
                there = pl.ds(base + r0, 64)
                da = dact[there, lanes].astype(F32)
                dga[here, :ht] = (da * upper * (sigma * (1.0 + gate * (1.0 - sigma)))).astype(BF)
                dga[here, ht : 2 * ht] = (da * silu).astype(BF)
                av = (silu * upper).astype(BF)
                dga[here, 2 * ht :] = av
                act[there, lanes] = av

            for r0 in range(0, r, 64):
                swiglu(r0)
            acc[:r] += dt(dga[:r, : 2 * ht], wcat[slot])
            small = jnp.concatenate([n2[:, :, width:].reshape(r, 2 * RK), dud[base : base + r, :RK]], axis=1)
            g = dr(small, dga[:r])
            for n in range(3):
                part = g[n * RK : (n + 1) * RK, n * ht : (n + 1) * ht]
                if add:
                    total = (gg[n, :, lanes] + part).astype(BF)
                    units = ht // LANE * (RK // 16)
                    put_units(ge, n * (hidden // LANE * (RK // 16)) + i * units, total)
                else:
                    gg[n, :, lanes] = part

        def halves(a, snd):
            half = snd.shape[1]

            def one(r0):
                for n in range(2):
                    snd[n, pl.ds(r0, 64)] = a[pl.ds(pl.multiple_of(n * half + r0, 64), 64)].astype(BF)

            rows_loop(half, 64, one)

        n2_copy_p = norm2(0, sum_p, xp, hp, n2p, sc[0])
        store_hp = store(hp, hp_h)
        arrived(0, n2p)
        n2_copy_p.wait_send()
        store_n2p = store(n2p.at[:, :, qlanes], n2p_h)
        begin(n2p, uop, sel_row(sc[0]))
        tail_stores = [store(uop, uop_h)]

        def tile_p(k):
            tile(k, n2p, 0, False)

            @pl.when(k == steps // 2 - 1)
            def _():
                norm2(1, sum_c, xc, hc, n2c, adapter_c)

        loop(0, steps, tile_p)
        store_hc = store(hc, hc_h)
        n2_copy_c = remote(n2c.at[lo], n2c.at[lo], nsem.at[1, 0], nsem.at[1, 1], (d, t ^ 1))
        sum_p.drain()
        halves(acc, snd_p)
        store_n2p.wait()
        sum2_p = TensorSum(snd_p, got1_p, s_p, t1_p, psem2, d, t)
        sum2_p.begin()

        arrived(1, n2c)
        n2_copy_c.wait_send()
        store_n2c = store(n2c.at[:, :, qlanes], n2c_h)
        begin(
            n2c, uoc,
            jnp.concatenate([jnp.broadcast_to(sel_row(sc[1]), (hcn, RK)), jnp.broadcast_to(sel_row(sc[2]), (hcn, RK))], axis=0),
        )
        tail_stores.append(store(uoc, uoc_h))
        sum2_p.middle()

        loop(steps, 2 * steps, lambda k: tile(k, n2c, PLEN, True))
        sum_c.drain()
        halves(acc, snd_c)
        store_n2c.wait()
        sum2_c = TensorSum(snd_c, got1_c, s_c, t1_c, csem2, d, t)
        sum2_c.begin()
        reduce = DirectReduce(ge, gots, gsum, (g0, g1, None, None), d, t, n_dp)
        reduce.start()

        ud = dt(act[...], adT[...]).astype(BF)
        sum2_c.middle()
        sum2_p.core.wait_send()
        sum2_c.core.wait_send()
        pad = jnp.zeros((hpn, LANE - RK), BF)
        for n in range(2):
            snd_p[n, :, width:] = jnp.concatenate([ud[n * hpn : (n + 1) * hpn], pad], axis=1)
            snd_c[n, :, width:] = jnp.concatenate([ud[PLEN + n * hcn : PLEN + (n + 1) * hcn], pad[:hcn]], axis=1)

        def project_down(n):
            slot = n % 2
            down(n, slot).wait()
            part = dn(act[...], wdn[slot]).astype(BF)
            lanes = pl.ds(pl.multiple_of(n * nt, nt), nt)
            for i in range(2):
                snd_p[i, :, lanes] = part[i * hpn : (i + 1) * hpn]
                snd_c[i, :, lanes] = part[PLEN + i * hcn : PLEN + (i + 1) * hcn]

            @pl.when(n + 2 < width // nt)
            def _():
                down(n + 2, slot).start()

        loop(0, width // nt, project_down)
        mcore_p = remote(snd_p.at[1 - lo], got0_p, msem.at[0], msem.at[1], (d, t ^ 1))
        mcore_p.start()
        mcore_c = remote(snd_c.at[1 - lo], got0_c, msem.at[2], msem.at[3], (d, t ^ 1))
        mcore_c.start()

        def mlp_sum(core, snd, got, out):
            core.wait_recv()

            def add(r0):
                here = pl.ds(r0, 64)
                got[here] = (snd[lo, here].astype(F32) + got[here].astype(F32)).astype(BF)

            rows_loop(got.shape[0], 64, add)
            tail_stores.append(store(got, out))

        def back(which, total, h, dy, da, adapter):
            half = h.shape[0]
            total.end()
            sr = sel_row(adapter)
            du = total.mine[:, width:].astype(F32) + total.theirs[:, width:].astype(F32)
            dum = (du * jnp.concatenate([sr, sr], axis=1)).astype(BF)
            tmp[:half] = dn(dum, amT[...])
            gain = gain2[...].astype(F32).reshape(1, width)

            def one(r0):
                here = pl.ds(r0, 64)
                dn2 = total.mine[here, :width].astype(F32) + total.theirs[here, :width].astype(F32) + tmp[here]
                dh = dy[here].astype(F32) + norm_back(h[here], gain, dn2)
                h[here] = dh
                da[lo, here, :width] = dh.astype(BF)

            rows_loop(half, 64, one)
            da[lo, :, width:] = dum
            c = remote(da.at[lo], da.at[lo], nsem.at[which, 0], nsem.at[which, 1], (d, t ^ 1))
            c.start()
            return c

        for c in load_dy:
            c.wait()
        store_hp.wait()
        store_hc.wait()
        copy_p = back(2, sum2_p, hp, dyp, n2p, sc[0])
        tail_stores.append(store(hp, dhp_h))
        mlp_sum(mcore_p, snd_p, got0_p, smp_h)
        mlp_sum(mcore_c, snd_c, got0_c, smc_h)
        arrived(2, n2p)
        tail_stores.append(store(n2p, dap_h))
        reduce.add()
        tail_stores.append(store(gsum.at[reduce.part(d)], ge_h))
        copy_c = back(3, sum2_c, hc, dyc, n2c, adapter_c)
        tail_stores.append(store(hc, dhc_h))
        arrived(3, n2c)
        tail_stores.append(store(n2c, dac_h))
        copy_p.wait_send()
        copy_c.wait_send()
        sum2_p.chip.wait_send()
        sum2_c.chip.wait_send()
        mcore_p.wait_send()
        mcore_c.wait_send()
        reduce.sent()
        for c in tail_stores:
            c.wait()

    pl.run_scoped(
        feed_forward,
        VM((2, wide, 2 * ht), BF), VM((2, hidden, 512), BF), VM((PLEN, wide), F32), VM((PLEN, 2 * ht), F32), VM((PLEN, 3 * ht), BF),
        VM((rows, hidden), BF), VM((3, RK, hidden), F32),
    )


def first(n_dp, scalars, small, large):
    tok, aT, wkv, cos, sin, wq, bq, aoT, wo, dy, bd, wd, raw = large
    rows, width = tok.shape
    qw = wq.shape[1]
    kvw2 = wkv.shape[1]
    hidden = wd.shape[0]
    quarter = width // 2
    wide = width + LANE
    hpn, hcn = PLEN // 2, CLEN
    units = 3 * hidden // LANE * (RK // 16)
    share = units // n_dp
    outs = [
        ((rows, quarter), BF), ((rows, qw), BF), ((rows, kvw2), BF), ((rows, 3 * RK), BF), ((2, 4 * CLEN, 768), BF),
        ((4, 4 * CLEN, 4 * CLEN), BF), ((rows, qw), BF), ((CONT_DEV, PLEN, kvw2), BF), ((hpn, width), F32),
        ((hcn, width), F32), ((2, hpn, quarter), BF), ((2, hcn, quarter), BF), ((2, hpn, LANE), BF), ((2, hcn, LANE), BF),
        ((width + 2 * RK, 2 * hidden), BF),
        ((hpn, width), F32), ((hcn, width), F32), ((2, hpn, wide), BF), ((2, hcn, wide), BF), ((hpn, wide), BF),
        ((hcn, wide), BF), ((share, *UNIT), BF),
    ]
    dma = pltpu.SemaphoreType.DMA
    scratch = [
        VM((n_dp, PLEN, kvw2), BF), VM((2, hpn, wide), BF), VM((hpn, wide), BF), VM((2, hcn, wide), BF), VM((hcn, wide), BF),
    ] + [VM((hpn, wide), BF), VM((hpn, wide), BF), VM((hcn, wide), BF), VM((hcn, wide), BF)] * 2 + [
        VM((2, hpn, wide), BF), VM((2, hcn, wide), BF), VM((2, hpn, LANE), BF), VM((2, hcn, LANE), BF),
        VM((hpn, width), F32), VM((hcn, width), F32), VM((hpn, width), BF), VM((hcn, width), BF), VM((hpn, width), BF),
        VM((hcn, width), BF), VM((rows, hidden), BF), VM((rows, LANE), BF), VM((hpn, width), F32),
        VM((units, *UNIT), BF), VM((n_dp, share, *UNIT), BF), VM((units, *UNIT), BF),
        VM((RK, 2, hidden), BF), VM((2 * RK, width), BF), VM((RK, hidden), BF), VM((RK, width), BF),
        dma((20,)), dma((22,)), dma((2, 2)), dma((4,)), dma((4, 2)), dma((2,)), dma((4,)), dma((4,)), dma((4,)), dma((4,)),
        dma((4,)), dma((4, 2)),
    ] + [dma((n_dp // 2 + 1,))] * 6 + [dma((n_dp,))] * 2
    vm = pl.BlockSpec(memory_space=VM)
    anyspace = pl.BlockSpec(memory_space=pl.ANY)
    return pl.pallas_call(
        functools.partial(first_kernel, n_dp),
        out_shape=[jax.ShapeDtypeStruct(s, dtype) for s, dtype in outs],
        in_specs=[pl.BlockSpec(memory_space=pltpu.SMEM)] * 3 + [vm] * 3 + [anyspace] * (len(small) - 3 + len(large)),
        out_specs=[anyspace] * len(outs),
        scratch_shapes=scratch,
        compiler_params=pltpu.CompilerParams(vmem_limit_bytes=63 << 20, collective_id=1, has_side_effects=True),
        cost_estimate=pl.CostEstimate(flops=12 * rows * width * hidden, bytes_accessed=120 << 20, transcendentals=0),
        name="first",
    )(*scalars, *small, *large)


class Fold:
    def __init__(self, dfar, xr, zs, zr, sems, owners, others, d, t, hi):
        self.dfar, self.xr, self.zs, self.zr, self.sems = dfar, xr, zs, zr, sems
        self.owners, self.others, self.d, self.t, self.hi = owners, others, d, t, hi
        self.z, self.x = d // 2, d % 2

    def across(self, j):
        return remote(self.dfar.at[j], self.xr.at[j], self.sems[0].at[j], self.sems[1].at[j], (self.d ^ 1, self.t))

    def along(self, z, come=False):
        slot = z if come else self.z
        return remote(
            self.zr.at[slot] if come else self.zs.at[z], self.zr.at[slot], self.sems[2].at[z], self.sems[3].at[slot],
            (z * 2 + self.x, self.t),
        )

    def held(self, z, rows):
        dest = z * 2 + self.x
        total = None
        for parts, owners in ((self.dfar, self.owners), (self.xr, self.others)):
            for j in range(CONT_DEV):
                term = parts[j, rows].astype(F32) * (owners[j] == dest).astype(F32)
                total = term if total is None else total + term
        return total

    def fold(self):
        for j in range(CONT_DEV):
            self.across(j).wait_recv()
        order = sorted(range(self.hi), key=lambda z: min(z, self.hi - 1 - z))
        for z in order:

            @pl.when(self.z != z)
            def _(z=z):
                def put(r):
                    rows = pl.ds(r, 64)
                    self.zs[z, rows] = self.held(z, rows).astype(BF)

                rows_loop(PLEN, 64, put)
                self.along(z).start()

    def finish(self, total):
        def own(r):
            rows = pl.ds(r, 64)
            total[rows] += self.held(self.z, rows)

        rows_loop(PLEN, 64, own)
        for z in range(self.hi):

            @pl.when(self.z != z)
            def _(z=z):
                self.along(z, True).wait_recv()
                total[...] += self.zr[z].astype(F32)

    def drain(self):
        for j in range(CONT_DEV):
            self.across(j).wait_send()
        for z in range(self.hi):

            @pl.when(self.z != z)
            def _(z=z):
                self.along(z).wait_send()


def back_kernel(
    n_dp, ids_p, ids_c, group_map, gain1, bkv_ref,
    dac_h, wo_h, o_h, aoT_h, bo_h, n2c_h, uoc_h, q_h, kv_h, far_h, pc_h, cos_h, sin_h, dap_h, pp_h, n2p_h, uop_h, u_h, wq_h, wkv_h, bq_h,
    smp_h, hp_h, bd_h, smc_h, hc_h, dy_h, n1q_h, dhc_h, aT_h, dhp_h, tok_h, ge_h,
    out_h, tg_h, gef_h, l0_h, t1_h, t2_h,
    dac, wo, o, aoT, bo, n2c, uoc, q, kv, far, pc, cos, sin, dap, pp, n2p, uop, u, wq, wkv, bq,
    smp, hp, bd, smc, hc, aT, xc, xp, gef, tmp_p, tmp_c,
    do, dqp, dkv, dkvp, dfar, gacc, snd_p, got_p, s_p, t_p, snd_c, got_c, s_c, t_c,
    dsnd_p, dgot_p, ds_p, dt_p, dsnd_c, dgot_c, ds_c, dt_c, dup, duc, outp, outc, tgp, tgc, tmp,
    l0s, l0x, l0z, l0, l1s, l1x, l1z, l2s, l2x, l2z, t1, t2, xr, zs, zr,
    lsem, osem, dsem, ysem, psem, csem, dpsem, dcsem, nsem, q1, q2, f0, f1, f2, f3, *rsems,
):
    d, t = place()
    sc = [ids_p[0], ids_c[0], ids_c[1], group_map[d * CONT_DEV], group_map[d * CONT_DEV + 1]]
    lo = t % 2
    hi = n_dp // 2
    width = wq.shape[0]
    qw = wq.shape[1]
    kvw = wkv.shape[1] // 2
    quarter = n1q_h.shape[1]
    hpn, hcn = PLEN // 2, CLEN
    greet(d, t, n_dp)
    qlanes = pl.ds(pl.multiple_of(lo * quarter, quarter), quarter)
    every = PairReduce(None, None, None, gef, rsems[0:8], d, t, n_dp)
    pairs = [
        (ge_h, gef.at[every.part(d // 2)]), (dac_h, dac), (wo_h, wo), (o_h, o), (aoT_h, aoT), (bo_h, bo), (n2c_h, n2c),
        (uoc_h, uoc), (q_h, q), (kv_h, kv), (far_h, far), (pc_h, pc), (cos_h, cos), (sin_h, sin), (dap_h, dap),
        (pp_h, pp), (n2p_h, n2p), (uop_h, uop), (u_h, u), (wq_h, wq), (wkv_h, wkv), (bq_h, bq),
        (smp_h, smp), (hp_h, hp), (bd_h, bd), (smc_h, smc), (hc_h, hc),
        (aT_h, aT), (tok_h.at[pl.ds(pl.multiple_of(PLEN + lo * hcn, hcn), hcn)], xc),
        (tok_h.at[pl.ds(pl.multiple_of(lo * hpn, hpn), hpn)], xp),
    ]
    loads = {}

    def fetch(first, last):
        for n in range(first, last):
            src, dst = pairs[n]
            c = pltpu.make_async_copy(src, dst, lsem.at[n])
            c.start()
            loads[id(dst) if n else 0] = c

    fetch(0, 14)

    def need(*refs):
        for ref in refs:
            loads.pop(id(ref)).wait()

    stores = []

    def store(src, dst):
        c = pltpu.make_async_copy(src, dst, osem.at[len(stores)])
        c.start()
        stores.append(c)

    greeted(n_dp)
    loads.pop(0).wait()
    every.spread()
    mlp_p = remote(smp_h, tmp_p, ysem.at[0], ysem.at[1], (d, t ^ 2))
    mlp_p.start()
    mlp_c = remote(smc_h, tmp_c, ysem.at[2], ysem.at[3], (d, t ^ 2))
    mlp_c.start()

    at = np.cumsum([0, quarter, quarter, quarter, qw, qw, 2 * kvw]).tolist()
    bkv = dn(evens_first(2 * RK), bkv_ref[...].reshape(2 * RK, kvw)).astype(BF)

    def out_grads(da, n2, uo, sel, r0, first):
        half = da.shape[1]
        r = 2 * half
        dav = da[:, :, :width].reshape(r, width)
        duo = (dt(dav, bo[...]) * sel).astype(BF)
        do[r0 : r0 + r] = (dt(dav, wo[...]) + dn(duo, aoT[...])).astype(BF)
        gao = dr(duo, o[r0 : r0 + r])
        dum = da[:, :, width:].reshape(r, 2 * RK)
        gam = dr(dum, n2[...].reshape(r, quarter))
        gbo = dr(uo[:, :, :RK].reshape(r, RK), da[:, :, qlanes].reshape(r, quarter))
        parts = (gbo, gam[:RK], gam[RK:], gao)
        for n, part in enumerate(parts):
            lanes = slice(at[n], at[n + 1])
            gacc[:, lanes] = part if first else gacc[:, lanes] + part

    def unrotate(r0, r):
        here = slice(r0, r0 + r)
        for c in range(qw // LANE):
            lanes = slice(c * LANE, (c + 1) * LANE)
            dqp[here, lanes] = rot(dqp[here, lanes].astype(F32), cos[here], -sin[here]).astype(BF)
        dkvp[here, :kvw] = rot(dkv[here, :kvw].astype(BF).astype(F32), cos[here], -sin[here]).astype(BF)
        dkvp[here, kvw:] = dkv[here, kvw:].astype(BF)

    need(dac, wo, o, aoT, bo, n2c, uoc)
    sel_c = jnp.concatenate([jnp.broadcast_to(sel_row(sc[1]), (hcn, RK)), jnp.broadcast_to(sel_row(sc[2]), (hcn, RK))], axis=0)
    out_grads(dac, n2c, uoc, sel_c, PLEN, True)
    fetch(14, 22)
    need(q, kv, far, pc)

    def attend(j):
        r0 = pl.multiple_of(PLEN + j * CLEN, CLEN)
        own = pl.ds(r0, CLEN)
        for g in range(2):
            lanes = slice(g * HD, (g + 1) * HD)
            vlanes = slice(kvw + g * HD, kvw + (g + 1) * HD)
            qi = stack_heads(q, r0, g)
            doi = stack_heads(do, r0, g)
            p = pc[2 * j + g]
            dp = jnp.concatenate([dt(doi, far[j, :, vlanes]), dt(doi, kv[own, vlanes])], axis=1)
            ds = back_scores(p, dp)
            dqv = dn(ds[:, :PLEN], far[j, :, lanes]) + dn(ds[:, PLEN:], kv[own, lanes])
            put_dq((dqv * 0.125).astype(BF), dqp, r0, g)
            dk = dr(ds, qi)
            dv = dr(p, doi)
            dfar[j, :, lanes] = dk[:PLEN].astype(BF)
            dfar[j, :, vlanes] = dv[:PLEN].astype(BF)
            dkv[own, lanes] = dk[PLEN:]
            dkv[own, vlanes] = dv[PLEN:]
        fold.across(j).start()

    mate = (d ^ 1) * CONT_DEV
    others = [group_map[mate + j] for j in range(CONT_DEV)]
    fold = Fold(dfar, xr, zs, zr, (f0, f1, f2, f3), sc[3:], others, d, t, hi)
    loop(0, CONT_DEV, attend)
    fetch(22, len(pairs))
    need(cos, sin)
    unrotate(PLEN, 2 * hcn)

    def dn1(r0, snd, dsnd, dsum, first):
        half = snd.shape[1]
        r = 2 * half
        here = slice(r0, r0 + r)
        a, b = dqp[here], dkvp[here]
        du = jnp.concatenate(
            [dt(a, bq[...]), dt(b[:, :kvw], bkv[:RK]), dt(b[:, kvw:], bkv[RK:]), jnp.zeros((r, RK), F32)], axis=1
        ).astype(BF)
        dsnd[0] = du[:half]
        dsnd[1] = du[half:]
        dsum.begin()

        def columns(n):
            lanes = pl.ds(pl.multiple_of(n * 512, 512), 512)
            part = (dt(a, wq[lanes]) + dt(b, wkv[lanes])).astype(BF)
            snd[0, :, lanes] = part[:half]
            snd[1, :, lanes] = part[half:]

        loop(0, width // 512, columns)
        gbq = dr(u[here, :RK], a)
        gkv = dr(u[here, RK:], b)
        parts = (gbq, gkv[:RK, :kvw], gkv[RK:, kvw:])
        for part, start in zip(parts, (at[4], at[5], at[5] + kvw)):
            lanes = slice(start, start + part.shape[1])
            gacc[:, lanes] = part if first else gacc[:, lanes] + part

    need(wq, wkv, u, bq)
    dsum_c = TensorSum(dsnd_c, dgot_c, ds_c, dt_c, dcsem, d, t)
    dn1(PLEN, snd_c, dsnd_c, dsum_c, True)
    sum_c = TensorSum(snd_c, got_c, s_c, t_c, csem, d, t)
    sum_c.begin()
    fold.fold()

    need(dap, n2p, uop)
    out_grads(dap, n2p, uop, jnp.broadcast_to(sel_row(sc[0]), (PLEN, RK)), 0, False)
    load_dy = []
    for n in range(2):
        for ref, start, half in ((dap, n * hpn, hpn), (dac, PLEN + n * hcn, hcn)):
            here = pl.ds(start, half)
            for src, lanes in ((dy_h.at[here, qlanes], slice(0, quarter)), (n1q_h.at[here], slice(quarter, 2 * quarter))):
                c = pltpu.make_async_copy(src, ref.at[n, :, lanes], dsem.at[len(load_dy)])
                c.start()
                load_dy.append(c)
    dsum_c.middle()
    sum_c.middle()
    need(pp)
    for g in range(2):
        lanes = slice(g * HD, (g + 1) * HD)
        vlanes = slice(kvw + g * HD, kvw + (g + 1) * HD)
        kg = kv[:PLEN, lanes]
        vg = kv[:PLEN, vlanes]
        for i in reversed(range(PLEN // CLEN)):
            size = (i + 1) * CLEN
            qi = stack_heads(q, i * CLEN, g)
            doi = stack_heads(do, i * CLEN, g)
            p = pp[g, :, P_OFF[i] : P_OFF[i] + size]
            ds = back_scores(p, dt(doi, vg[:size]))
            put_dq((dn(ds, kg[:size]) * 0.125).astype(BF), dqp, i * CLEN, g)
            dk = dr(ds, qi)
            dv = dr(p, doi)
            if size == PLEN:
                dkv[:size, lanes] = dk
                dkv[:size, vlanes] = dv
            else:
                dkv[:size, lanes] += dk
                dkv[:size, vlanes] += dv
    every.cross()

    def finish_out(which, sm, theirs, copy, h, out, r0, adapter):
        half = h.shape[0]
        copy.wait_recv()
        sr = sel_row(adapter)
        ud = ((sm[:, width : width + RK].astype(F32) + theirs[:, width : width + RK].astype(F32)) * sr).astype(BF)
        tmp[:half] = dn(ud, bd[...])

        def one(r):
            here = pl.ds(r, 64)
            out[lo, here, :width] = (
                h[here] + (sm[here, :width].astype(F32) + theirs[here, :width].astype(F32)) + tmp[here]
            ).astype(BF)

        rows_loop(half, 64, one)
        out[lo, :, width:] = jnp.concatenate([ud, jnp.zeros((half, LANE - RK), BF)], axis=1)
        c = remote(out.at[lo], out.at[lo], nsem.at[which, 0], nsem.at[which, 1], (d, t ^ 1))
        c.start()
        return c

    def arrived(which, out):
        remote(out.at[1 - lo], out.at[1 - lo], nsem.at[which, 0], nsem.at[which, 1], (d, t ^ 1)).wait_recv()

    need(smp, hp, bd)
    out_copy_p = finish_out(0, smp, tmp_p, mlp_p, hp, outp, 0, sc[0])
    load_dhp = pltpu.make_async_copy(dhp_h, hp, lsem.at[32])
    load_dhp.start()

    adapter_c = jnp.where(lo == 0, sc[1], sc[2])
    per = quarter // LANE * (RK // 16)

    def fill(blocks, used):
        if blocks.shape[0] > used:
            blocks[used:] = jnp.zeros((blocks.shape[0] - used, *UNIT), BF)

    def share_du(which, total, du, adapter):
        total.end()
        sr = sel_row(adapter)
        raw = total.mine[:, : 3 * RK].astype(F32) + total.theirs[:, : 3 * RK].astype(F32)
        duq = (raw * jnp.concatenate([sr, sr, sr], axis=1)).astype(BF)
        du[lo] = jnp.concatenate([duq, jnp.zeros((duq.shape[0], RK), BF)], axis=1)
        c = remote(du.at[lo], du.at[lo], nsem.at[which, 0], nsem.at[which, 1], (d, t ^ 1))
        c.start()
        return c

    need(smc, hc, aT)
    out_copy_c = finish_out(1, smc, tmp_c, mlp_c, hc, outc, PLEN, adapter_c)
    load_dhc = pltpu.make_async_copy(dhc_h, hc, lsem.at[33])
    load_dhc.start()
    du_copy_c = share_du(4, dsum_c, duc, adapter_c)
    for c in load_dy:
        c.wait()
    arrived(0, outp)
    gbd = dr(outp[:, :, width : width + RK].reshape(PLEN, RK), dap[:, :, :quarter].reshape(PLEN, quarter))
    arrived(1, outc)
    gbd = gbd + dr(outc[:, :, width : width + RK].reshape(2 * hcn, RK), dac[:, :, :quarter].reshape(2 * hcn, quarter))

    put_units(l1s, 0, gacc[:, : at[3]].astype(BF))
    put_units(l1s, 3 * per, gbd.astype(BF))
    fill(l1s, 4 * per)
    red1 = PairReduce(l1s, l1x, l1z, t1.at[lo], rsems[8:16], d, t, n_dp)
    red1.start()
    trade1 = Trade(t1, q1, d, t)
    for n in range(2):
        store(outp.at[n, :, :width], out_h.at[pl.ds(n * hpn, hpn)])
        store(outc.at[n, :, :width], out_h.at[pl.ds(PLEN + n * hcn, hcn)])
    arrived(4, duc)
    ga_c = dr(duc[:, :, : 3 * RK].reshape(2 * hcn, 3 * RK), dac[:, :, quarter : 2 * quarter].reshape(2 * hcn, quarter))

    fold.finish(dkv.at[:PLEN])
    unrotate(0, PLEN)
    dsum_p = TensorSum(dsnd_p, dgot_p, ds_p, dt_p, dpsem, d, t)
    dn1(0, snd_p, dsnd_p, dsum_p, False)
    sum_p = TensorSum(snd_p, got_p, s_p, t_p, psem, d, t)
    dsum_p.middle()
    sum_p.begin()
    put_units(l0s, 0, gacc[:, at[3] :].astype(BF))
    fill(l0s, (at[6] - at[3]) // LANE * (RK // 16))
    red0 = PairReduce(l0s, l0x, l0z, l0, rsems[16:24], d, t, n_dp)
    red0.start()
    sum_p.middle()
    red1.middle()
    du_copy_p = share_du(5, dsum_p, dup, sc[0])
    arrived(5, dup)
    ga_p = dr(dup[:, :, : 3 * RK].reshape(PLEN, 3 * RK), dap[:, :, quarter : 2 * quarter].reshape(PLEN, quarter))
    ga = (ga_c + ga_p).astype(BF)
    for n in range(3):
        put_units(l2s, n * per, ga[n * RK : (n + 1) * RK])
    fill(l2s, 3 * per)
    red2 = PairReduce(l2s, l2x, l2z, t2.at[lo], rsems[24:32], d, t, n_dp)
    red2.start()
    trade2 = Trade(t2, q2, d, t)

    def last(which, total, du, x, dh, tg):
        half = x.shape[0]
        tmp[:half] = dn(du[lo, :, : 3 * RK], aT[...])
        gain = gain1[...].astype(F32).reshape(1, width)
        total.end()

        def one(r):
            here = pl.ds(r, 64)
            dn1v = total.mine[here].astype(F32) + total.theirs[here].astype(F32) + tmp[here]
            grad = dh[here] + norm_back(x[here].astype(F32), gain, dn1v)
            tg[lo, here] = grad.astype(BF)

        rows_loop(half, 64, one)
        c = remote(tg.at[lo], tg.at[lo], nsem.at[which, 0], nsem.at[which, 1], (d, t ^ 1))
        c.start()
        return c

    red1.add()
    red0.middle()
    need(xc)
    load_dhc.wait()
    tg_copy_c = last(2, sum_c, duc, xc, hc, tgc)
    red2.middle()
    red1.cross()
    red0.add()
    every.finish()
    store(gef, gef_h)
    red2.add()
    arrived(2, tgc)
    for n in range(2):
        store(tgc.at[n], tg_h.at[pl.ds(PLEN + n * hcn, hcn)])
    red0.cross()
    red1.finish()
    trade1.start()
    red2.cross()
    trade1.finish()
    store(t1, t1_h)
    need(xp)
    load_dhp.wait()
    tg_copy_p = last(3, sum_p, dup, xp, hp, tgp)
    red0.finish()
    store(l0, l0_h)
    red2.finish()
    trade2.start()
    arrived(3, tgp)
    for n in range(2):
        store(tgp.at[n], tg_h.at[pl.ds(n * hpn, hpn)])
    trade2.finish()
    store(t2, t2_h)
    for c in (out_copy_p, out_copy_c, tg_copy_c, tg_copy_p, du_copy_c, du_copy_p, mlp_p, mlp_c):
        c.wait_send()
    for total in (sum_p, sum_c, dsum_p, dsum_c):
        total.drain()
    fold.drain()
    every.spread_sent()
    for red in (red0, red1, red2):
        red.sent()
        red.spread_sent()
    trade1.sent()
    trade2.sent()
    for c in stores:
        c.wait()


def backward(n_dp, scalars, small, large):
    (dac, wo, o, aoT, bo, n2c, uoc, q, kv, far, pc, cos, sin, dap, pp, n2p, uop, u, wq, wkv, bq, smp, hp, bd, smc, hc, dy, n1q,
     dhc, aT, dhp, tok, ge) = large
    rows, width = tok.shape
    qw = wq.shape[1]
    kvw2 = wkv.shape[1]
    quarter = n1q.shape[1]
    wide = dap.shape[2]
    hpn, hcn = PLEN // 2, CLEN
    per = quarter // LANE * (RK // 16)
    up = lambda a: -(-a // n_dp) * n_dp
    ue = ge.shape[0] * n_dp
    u0 = up((2 * qw + kvw2) // LANE * (RK // 16))
    u1 = up(4 * per)
    u2 = up(3 * per)
    outs = [
        ((rows, width), BF), ((rows, width), BF), ((ue, *UNIT), BF), ((u0, *UNIT), BF), ((2, u1, *UNIT), BF),
        ((2, u2, *UNIT), BF),
    ]
    dma = pltpu.SemaphoreType.DMA
    hi = n_dp // 2
    same = lambda a: VM(a.shape, a.dtype)

    def sums(half, n):
        return [VM((2, half, n), BF), VM((half, n), BF), VM((half, n), BF), VM((half, n), BF)]

    scratch = [
        same(dac), same(wo), same(o), same(aoT), same(bo), VM((2, hcn, quarter), BF), VM((2, hcn, LANE), BF), same(q), same(kv),
        same(far), same(pc), same(cos), same(sin), same(dap), same(pp), VM((2, hpn, quarter), BF), VM((2, hpn, LANE), BF),
        same(u), same(wq), same(wkv), same(bq), same(smp), same(hp), same(bd), same(smc), same(hc),
        same(aT), VM((hcn, width), BF), VM((hpn, width), BF), VM((ue, *UNIT), BF),
        same(smp), same(smc),
        VM((rows, qw), BF), VM((rows, qw), BF), VM((rows, kvw2), F32), VM((rows, kvw2), BF),
        VM((CONT_DEV, PLEN, kvw2), BF), VM((RK, 2 * qw + 3 * quarter + kvw2), F32),
        *sums(hpn, width), *sums(hcn, width), *sums(hpn, 2 * LANE), *sums(hcn, 2 * LANE),
        VM((2, hpn, 2 * LANE), BF), VM((2, hcn, 2 * LANE), BF),
        VM((2, hpn, wide), BF), VM((2, hcn, wide), BF), VM((2, hpn, width), BF), VM((2, hcn, width), BF), VM((hpn, width), F32),
        VM((u0, *UNIT), BF), VM((u0 // 2, *UNIT), BF), VM((hi, u0 // n_dp, *UNIT), BF), VM((u0, *UNIT), BF),
        VM((u1, *UNIT), BF), VM((u1 // 2, *UNIT), BF), VM((hi, u1 // n_dp, *UNIT), BF),
        VM((u2, *UNIT), BF), VM((u2 // 2, *UNIT), BF), VM((hi, u2 // n_dp, *UNIT), BF),
        VM((2, u1, *UNIT), BF), VM((2, u2, *UNIT), BF),
        VM((CONT_DEV, PLEN, kvw2), BF), VM((hi, PLEN, kvw2), BF), VM((hi, PLEN, kvw2), BF),
        dma((34,)), dma((13,)), dma((8,)), dma((4,)), dma((4,)), dma((4,)), dma((4,)), dma((4,)), dma((6, 2)), dma((2,)), dma((2,)),
    ] + [dma((CONT_DEV,))] * 2 + [dma((hi,))] * 2 + [dma((n_dp,))] * 32
    vm = pl.BlockSpec(memory_space=VM)
    anyspace = pl.BlockSpec(memory_space=pl.ANY)
    return pl.pallas_call(
        functools.partial(back_kernel, n_dp),
        out_shape=[jax.ShapeDtypeStruct(s, dtype) for s, dtype in outs],
        in_specs=[pl.BlockSpec(memory_space=pltpu.SMEM)] * 3 + [vm] * len(small) + [anyspace] * len(large),
        out_specs=[anyspace] * len(outs),
        scratch_shapes=scratch,
        compiler_params=pltpu.CompilerParams(vmem_limit_bytes=63 << 20, collective_id=3, has_side_effects=True),
        cost_estimate=pl.CostEstimate(flops=6 * rows * width * (2 * qw + kvw2), bytes_accessed=40 << 20, transcendentals=0),
        name="back",
    )(*scalars, *small, *large)


def emit_kernel(
    qw, kvw, quarter, hidden, ge, l0, t1, t2, out_h, tg_h,
    gbm, gad, gao, gbq, gbkv, gbo, gam, gbd, ga, out_o, tg_o, buf, sem,
):
    pairs = ((out_h, out_o), (tg_h, tg_o))
    copies = [pltpu.make_async_copy(src, buf.at[n], sem.at[n]) for n, (src, _) in enumerate(pairs)]
    for c in copies:
        c.start()
    high = RK // 16

    def take(blocks, first, count, put):
        for b in range(count // LANE):
            for r in range(high):
                put(slice(r * 16, (r + 1) * 16), slice(b * LANE, (b + 1) * LANE), blocks[first + b * high + r].astype(F32))

    def plain(dst, row=0, lane=0):
        def put(rows, lanes, value):
            dst[rows.start + row : rows.stop + row, lanes.start + lane : lanes.stop + lane] = value

        return put

    def paired(dst, n):
        def put(rows, lanes, value):
            dst[rows, n, lanes] = value

        return put

    seg = hidden // LANE * high
    take(ge, 0, hidden, paired(gbm, 0))
    take(ge, seg, hidden, paired(gbm, 1))
    take(ge, 2 * seg, hidden, plain(gad))
    take(l0, 0, qw, plain(gao))
    begin = qw // LANE * high
    half = kvw // LANE * high
    take(l0, begin, qw, plain(gbq))
    take(l0, 2 * begin, kvw, paired(gbkv, 0))
    take(l0, 2 * begin + half, kvw, paired(gbkv, 1))
    per = quarter // LANE * high
    for c in copies:
        c.wait()
    copies = [pltpu.make_async_copy(buf.at[n], dst, sem.at[2 + n]) for n, (_, dst) in enumerate(pairs)]
    for c in copies:
        c.start()
    for t in range(t1.shape[0]):
        take(t1.at[t], 0, quarter, plain(gbo, 0, t * quarter))
        take(t1.at[t], per, quarter, plain(gam, 0, t * quarter))
        take(t1.at[t], 2 * per, quarter, plain(gam, RK, t * quarter))
        take(t1.at[t], 3 * per, quarter, plain(gbd, 0, t * quarter))
        for n in range(3):
            take(t2.at[t], n * per, quarter, plain(ga, n * RK, t * quarter))
    for c in copies:
        c.wait()


def emit(qw, kvw, quarter, hidden, grads, results):
    width = 2 * quarter
    outs = [
        ((RK, 2, hidden), F32), ((RK, hidden), F32), ((RK, qw), F32), ((RK, qw), F32), ((RK, 2, kvw), F32), ((RK, width), F32),
        ((2 * RK, width), F32), ((RK, width), F32), ((3 * RK, width), F32),
    ] + [(a.shape, a.dtype) for a in results]
    vm = pl.BlockSpec(memory_space=VM)
    anyspace = pl.BlockSpec(memory_space=pl.ANY)
    return pl.pallas_call(
        functools.partial(emit_kernel, qw, kvw, quarter, hidden),
        out_shape=[jax.ShapeDtypeStruct(s, dtype) for s, dtype in outs],
        in_specs=[vm] * len(grads) + [anyspace] * len(results),
        out_specs=[vm] * 9 + [anyspace] * 2,
        scratch_shapes=[VM((2, *results[0].shape), BF), pltpu.SemaphoreType.DMA((4,))],
        compiler_params=pltpu.CompilerParams(vmem_limit_bytes=61 << 20),
        cost_estimate=pl.CostEstimate(flops=0, bytes_accessed=20 << 20, transcendentals=0),
        name="emit",
    )(*grads, *results)


def rope_tables():
    position = np.concatenate([np.arange(PLEN)] + [PLEN + np.arange(CLEN)] * CONT_DEV).astype(np.float32)
    exponent = np.arange(HD // 2, dtype=np.float32) * np.float32(2.0 / HD)
    frequency = np.exp(np.float32(-math.log(ROPE_BASE)) * exponent).astype(np.float32)
    angle = position[:, None] * frequency[None, :]
    cos, sin = np.cos(angle).astype(np.float32), np.sin(angle).astype(np.float32)
    return np.tile(cos, (1, 4)), np.concatenate([-sin, sin, -sin, sin], axis=1)


def shards(
    tokens, cotangent, gain_attn, gain_mlp, w_query, w_kv, w_out, w_gate_up, w_down, a_attn, b_query, b_kv,
    a_out, b_out, a_mlp, b_mlp, a_down, b_down, prompt_adapter, cont_adapter, group_map,
):
    rows, width = tokens.shape
    qw = w_query.shape[1]
    kvw = w_kv.shape[2]
    hidden = w_down.shape[0]
    n_dp = lax.axis_size("dp")
    quarter = width // 2
    cos_np, sin_np = rope_tables()
    cos, sin = jnp.asarray(cos_np), jnp.asarray(sin_np)
    gain1, gain2 = gain_attn, gain_mlp
    aT = a_attn.transpose(1, 2, 3, 0).reshape(3 * RK, width)
    aoT = a_out.transpose(1, 2, 0).reshape(RK, qw)
    amT = a_mlp.transpose(1, 2, 3, 0).reshape(2 * RK, width)
    adT = a_down.transpose(1, 2, 0).reshape(RK, hidden)
    bq = b_query.reshape(RK, qw)
    bkv = b_kv.reshape(RK, 2, kvw)
    bo = b_out.reshape(RK, width)
    bm = b_mlp.reshape(RK, 2, hidden)
    bd = b_down.reshape(RK, width)
    wkv = w_kv.reshape(width, 2 * kvw)
    (n1q, q, kv, u, pp, pc, o, far, h_p, h_c, n2p, n2c, uop, uoc, _, dh_p, dh_c, dap, dac, sm_p, sm_c, ge) = first(
        n_dp, [prompt_adapter, cont_adapter, group_map], [gain1, gain2, bkv, bm, amT, adT, bo],
        [tokens, aT, wkv, cos, sin, w_query, bq, aoT, w_out, cotangent, bd, w_down, w_gate_up],
    )
    results = backward(
        n_dp, [prompt_adapter, cont_adapter, group_map], [gain1, bkv],
        [dac, w_out, o, aoT, bo, n2c, uoc, q, kv, far, pc, cos, sin, dap, pp, n2p, uop, u, w_query, wkv, bq, sm_p, h_p, bd, sm_c,
         h_c, cotangent, n1q, dh_c, aT, dh_p, tokens, ge],
    )
    gbm, gad, gao, gbq, gbkv, gbo, gam, gbd, ga, output, tokens_grad = emit(qw, kvw, quarter, hidden, results[2:], results[:2])
    return (
        output,
        tokens_grad,
        ga.reshape(3, NA, R, width).transpose(3, 0, 1, 2),
        gbq.reshape(b_query.shape),
        gbkv.reshape(b_kv.shape),
        gao.reshape(NA, R, qw).transpose(2, 0, 1),
        gbo.reshape(b_out.shape),
        gam.reshape(2, NA, R, width).transpose(3, 0, 1, 2),
        gbm.reshape(b_mlp.shape),
        gad.reshape(NA, R, hidden).transpose(2, 0, 1),
        gbd.reshape(b_down.shape),
    )


def solution(mesh):
    in_specs = (
        P("dp", None), P("dp", None), P(), P(), P(None, "tensor"), P(None, None, "tensor"), P("tensor", None),
        P(None, None, "tensor"), P("tensor", None), P(), P(None, None, "tensor"), P(None, None, None, "tensor"),
        P("tensor", None, None), P(), P(), P(None, None, None, "tensor"), P("tensor", None, None), P(),
        P("dp"), P("dp"), P(),
    )
    out_specs = (
        P("dp", None), P("dp", None), P(), P(None, None, "tensor"), P(None, None, None, "tensor"),
        P("tensor", None, None), P(), P(), P(None, None, None, "tensor"), P("tensor", None, None), P(),
    )
    return jax.shard_map(shards, mesh=mesh, in_specs=in_specs, out_specs=out_specs, check_vma=False)
```

time: 406 us -> 206 us (0.51); the launches traced: 400 us -> 205 us
  Pallas kernels: 393 us -> 201 us
    pallas_call x1, Pallas kernels: 164 us -> 9.17 us  [emit(): pl.pallas_call(functools.partial(emit_kernel, qw, kvw, quarter, hidden),...]
    pallas_call x2 -> x1, Pallas kernels: 135 us -> 108 us  [first(): pl.pallas_call(functools.partial(first_kernel, n_dp), out_shape=[jax.Shap...]
    pallas_call x1, Pallas kernels: 93.8 us -> 83.4 us  [backward(): pl.pallas_call(functools.partial(back_kernel, n_dp), out_shape=[jax.Shape...]
where the time goes in v3:
time: 206 us; the launch traced here: 205 us
  Pallas kernels  201 us (98%)
  local copies, waits for them, and re-layouts  2.33 us (1%)
    pallas_call x1, Pallas kernels, first(): pl.pallas_call(functools.partial(first_kernel, n_dp), out_shape=[jax.Shap...  108 us
    pallas_call x1, Pallas kernels, backward(): pl.pallas_call(functools.partial(back_kernel, n_dp), out_shape=[jax.Shape...  83.4 us
    pallas_call x1, Pallas kernels, emit(): pl.pallas_call(functools.partial(emit_kernel, qw, kvw, quarter, hidden),...  9.17 us

profile of v3, /device:TPU:0, one launch (start us, length us, event | category | flops | bytes accessed | tf_op | source)
XLA Modules:
  0.0 204.6 jit_solution(8025496097354348010)
XLA Ops:
  1.3 2.3 %copy.36 = bf16[256,8,2,128]{3,1,2,0:T(8,128)(2,1)} copy(bf16[256,8,2,128]{3,2,1,0:T(2,128)(2,1)} %bitcast.38) | data formatting | bytes 2097152
  3.6 108.1 %first.1 = (bf16[640,1024]{1,0:T(8,128)(2,1)}, bf16[640,512]{1,0:T(8,128)(2,1)}, bf16[640,256]{1,0:T(8,128)(2,1)}, bf16[640,192]{1,0:T(8,128)(2,1)}, bf16[2,512,...) custom-call(s32[1]{0:T(128)S(6)} %copy.37.ids_p, ...), custom_call_target="tpu_custom_call" | custom-call | flops 32212254720 | bytes 125829120 | tf_op jit(solution)/shard_map/first/pallas_call | solution.py:944
  111.7 83.4 %back.1 = (bf16[640,2048]{1,0:T(8,128)(2,1)}, bf16[640,2048]{1,0:T(8,128)(2,1)}, bf16[192,16,128]{2,1,0:T(8,128)(2,1)}, bf16[40,16,128]{2,1,0:T(8,128)(2,1)}, bf...) custom-call(s32[1]{0:T(128)S(6)} %copy.37.ids_p, s32[2]{0:T(128)} %ids_c.3, s32[16]{0:T(128)} %group_map.3, ...), custom_call_target="tpu_custom_call" | custom-call | flops 10066329600 | bytes 41943040 | tf_op jit(solution)/shard_map/back/pallas_call | solution.py:1412
  195.2 9.2 %emit.1 = (f32[64,2,2048]{2,1,0:T(2,128)}, f32[64,2048]{1,0:T(8,128)}, f32[64,512]{1,0:T(8,128)}, f32[64,512]{1,0:T(8,128)}, f32[64,2,128]{2,1,0:T(2,128)}, /*in...) custom-call(bf16[192,16,128]{2,1,0:T(8,128)(2,1)} %get-tuple-element, ...), custom_call_target="tpu_custom_call" | custom-call | bytes 20971520 | tf_op jit(solution)/shard_map/emit/pallas_call | solution.py:1486
